TPU v7x, 256 devices: a whole 4x4x8 slice. The times are simulated.
256 devices in a mesh: lon: 16 (over y_lo, z), lat: 16 (over y_hi, x, core).
Axes of the slice: x: 4, y: 4 (y_hi: 2, y_lo: 2; y = y_hi * 2 + y_lo), z: 8, core: 2. Of those that a mesh axis runs over, the one named last changes fastest.
Arguments:
- tokens: bfloat16 [768, 288, 512], P('lon', 'lat'), may hold values from -45 to 45
- cotangent: bfloat16 [768, 288, 512], P('lon', 'lat'), may hold values from -6 to 6
- region: int32 [768, 288], P('lon', 'lat'), may hold values from 0 to 2
- gain: float32 [512], replicated, may hold values from 0.25 to 1.75
- w_qkv: bfloat16 [512, 1536], replicated, may hold values from -16 to 16
- w_proj: bfloat16 [512, 512], replicated, may hold values from -0.25 to 0.25
Outputs:
- mixed: bfloat16 [768, 288, 512], P('lon', 'lat')
- tokens_grad: bfloat16 [768, 288, 512], P('lon', 'lat')
- qkv_grad: float32 [512, 1536], replicated
- proj_grad: float32 [512, 512], replicated
- gain_grad: float32 [512], replicated
All inputs are finite; a program needn't handle non-finite values.
Results may differ from a plain program's by a relative error of at most 0.011.
Values may be sent and summed in bfloat16 or wider, within the bound.
No kernel may reach another device: no remote copies, remote signals or barrier semaphores. Data moves between devices by JAX's collectives and lax.ppermute only.
A program may use at most 128 MiB of HBM per device.

v0:
```python
import jax
import jax.numpy as jnp
from jax import lax
from jax.sharding import PartitionSpec as P

HEADS = 8
WIN_LON = 12
WIN_LAT = 6
SHIFT_LON = 6
SHIFT_LAT = 3


def shifted(block, axis, distance):
    devices = range(lax.axis_size(axis))
    route = [((i - distance) % len(devices), i) for i in devices]
    return lax.ppermute(block, axis, route)


def to_windows(array_in):
    rows_lon, cols_lat, channels = array_in.shape
    shaped = array_in.reshape(rows_lon // WIN_LON, WIN_LON, cols_lat // WIN_LAT, WIN_LAT, channels)
    return shaped.transpose(0, 2, 1, 3, 4).reshape(-1, WIN_LON * WIN_LAT, channels)


def from_windows(array_in, rows_lon, cols_lat):
    channels = array_in.shape[-1]
    shaped = array_in.reshape(rows_lon // WIN_LON, cols_lat // WIN_LAT, WIN_LON, WIN_LAT, channels)
    return shaped.transpose(0, 2, 1, 3, 4).reshape(rows_lon * cols_lat, channels)


def contract_rows(left, right):
    return lax.dot_general(
        left, right, (((0,), (0,)), ((), ())), preferred_element_type=jnp.float32
    )


def contract_cols(left, right):
    return lax.dot_general(
        left, right, (((1,), (1,)), ((), ())), preferred_element_type=jnp.float32
    )


def layer_pass(rolled_x, rolled_g, labels, gain, w_qkv, w_proj):
    rows_lon, cols_lat, channels = rolled_x.shape
    count = rows_lon * cols_lat
    head_dim = channels // HEADS
    score_scale = head_dim ** (-0.5)
    window_len = WIN_LON * WIN_LAT
    flat_input = rolled_x.reshape(count, channels).astype(jnp.float32)
    average = jnp.mean(flat_input, axis=-1, keepdims=True)
    centred = flat_input - average
    variance = jnp.mean(centred * centred, axis=-1, keepdims=True)
    inverse = lax.rsqrt(variance + 1e-05)
    normed = centred * inverse
    hidden = (normed * gain).astype(jnp.bfloat16)
    projected = jnp.dot(hidden, w_qkv, preferred_element_type=jnp.float32).astype(jnp.bfloat16)
    windowed = to_windows(projected.reshape(rows_lon, cols_lat, 3 * channels))
    windowed = windowed.reshape(-1, window_len, 3, HEADS, head_dim)
    queries = windowed[:, :, 0]
    keys_win = windowed[:, :, 1]
    values_win = windowed[:, :, 2]
    labels_win = to_windows(labels.reshape(rows_lon, cols_lat, 1))[:, :, 0]
    allowed = labels_win[:, :, None] == labels_win[:, None, :]
    scores = (
        jnp.einsum("wihd,wjhd->whij", queries, keys_win, preferred_element_type=jnp.float32)
        * score_scale
    )
    scores = jnp.where(allowed[:, None], scores, -1e30)
    row_max = jnp.max(scores, axis=-1, keepdims=True)
    lifted = jnp.exp(scores - row_max)
    attention = lifted / jnp.sum(lifted, axis=-1, keepdims=True)
    attention_b = attention.astype(jnp.bfloat16)
    attended = jnp.einsum(
        "whij,wjhd->wihd", attention_b, values_win, preferred_element_type=jnp.float32
    ).astype(jnp.bfloat16)
    attended_flat = from_windows(attended.reshape(-1, window_len, channels), rows_lon, cols_lat)
    branch = jnp.dot(attended_flat, w_proj, preferred_element_type=jnp.float32)
    mixed = (flat_input + branch).astype(jnp.bfloat16)
    upstream = rolled_g.reshape(count, channels)
    grad_proj = contract_rows(attended_flat, upstream)
    grad_attended = contract_cols(upstream, w_proj).astype(jnp.bfloat16)
    grad_att_win = to_windows(grad_attended.reshape(rows_lon, cols_lat, channels))
    grad_att_win = grad_att_win.reshape(-1, window_len, HEADS, head_dim)
    grad_attention = jnp.einsum(
        "wihd,wjhd->whij", grad_att_win, values_win, preferred_element_type=jnp.float32
    )
    grad_values = jnp.einsum(
        "whij,wihd->wjhd", attention_b, grad_att_win, preferred_element_type=jnp.float32
    )
    inner = jnp.sum(grad_attention * attention, axis=-1, keepdims=True)
    grad_scores = (attention * (grad_attention - inner)).astype(jnp.bfloat16)
    grad_queries = (
        jnp.einsum("whij,wjhd->wihd", grad_scores, keys_win, preferred_element_type=jnp.float32)
        * score_scale
    )
    grad_keys = (
        jnp.einsum("whij,wihd->wjhd", grad_scores, queries, preferred_element_type=jnp.float32)
        * score_scale
    )
    grad_stack = jnp.stack([grad_queries, grad_keys, grad_values], 2).astype(jnp.bfloat16)
    grad_projected = from_windows(
        grad_stack.reshape(-1, window_len, 3 * channels), rows_lon, cols_lat
    )
    grad_qkv = contract_rows(hidden, grad_projected)
    grad_hidden = contract_cols(grad_projected, w_qkv)
    grad_gain = jnp.sum(grad_hidden * normed, axis=0)
    grad_normed = grad_hidden * gain
    grad_input = inverse * (
        grad_normed
        - jnp.mean(grad_normed, axis=-1, keepdims=True)
        - normed * jnp.mean(grad_normed * normed, axis=-1, keepdims=True)
    )
    grad_tokens = (upstream.astype(jnp.float32) + grad_input).astype(jnp.bfloat16)
    return (
        mixed.reshape(rows_lon, cols_lat, channels),
        grad_tokens.reshape(rows_lon, cols_lat, channels),
        grad_qkv,
        grad_proj,
        grad_gain,
    )


def body(tokens, cotangent, region, gain, w_qkv, w_proj):
    rows_lon, cols_lat, channels = tokens.shape
    lon_pieces = shifted((tokens[:SHIFT_LON], cotangent[:SHIFT_LON], region[:SHIFT_LON]), "lon", -1)
    half_x = jnp.concatenate([tokens[SHIFT_LON:], lon_pieces[0]], 0)
    half_g = jnp.concatenate([cotangent[SHIFT_LON:], lon_pieces[1]], 0)
    half_r = jnp.concatenate([region[SHIFT_LON:], lon_pieces[2]], 0)
    lat_pieces = shifted(
        (half_x[:, :SHIFT_LAT], half_g[:, :SHIFT_LAT], half_r[:, :SHIFT_LAT]), "lat", -1
    )
    rolled_x = jnp.concatenate([half_x[:, SHIFT_LAT:], lat_pieces[0]], 1)
    rolled_g = jnp.concatenate([half_g[:, SHIFT_LAT:], lat_pieces[1]], 1)
    rolled_r = jnp.concatenate([half_r[:, SHIFT_LAT:], lat_pieces[2]], 1)
    lat_index = lax.axis_index("lat") * cols_lat + jnp.arange(cols_lat, dtype=jnp.int32)
    wrapped = (lat_index >= cols_lat * lax.axis_size("lat") - SHIFT_LAT).astype(jnp.int32)
    labels = rolled_r * 2 + wrapped[None, :]
    mixed_r, grad_r, grad_qkv, grad_proj, grad_gain = layer_pass(
        rolled_x, rolled_g, labels, gain, w_qkv, w_proj
    )
    packed = jnp.stack([mixed_r, grad_r], 0)
    from_lat = shifted(packed[:, :, cols_lat - SHIFT_LAT :], "lat", 1)
    half_back = jnp.concatenate([from_lat, packed[:, :, : cols_lat - SHIFT_LAT]], 2)
    from_lon = shifted(half_back[:, rows_lon - SHIFT_LON :], "lon", 1)
    restored = jnp.concatenate([from_lon, half_back[:, : rows_lon - SHIFT_LON]], 1)
    grad_qkv, grad_proj, grad_gain = lax.psum((grad_qkv, grad_proj, grad_gain), ("lon", "lat"))
    return (restored[0], restored[1], grad_qkv, grad_proj, grad_gain)


def solution(mesh):
    return jax.shard_map(
        body,
        mesh=mesh,
        in_specs=(P("lon", "lat", None), P("lon", "lat", None), P("lon", "lat"), P(), P(), P()),
        out_specs=(P("lon", "lat", None), P("lon", "lat", None), P(), P(), P()),
        check_vma=False,
    )
```

profile of v0, /device:TPU:1, one launch (start us, length us, event | category | flops | bytes accessed | tf_op | source)
XLA Modules:
  0.0 445.1 jit_solution(2761194167784220969)
XLA Ops:
  8.3 7.5 %collective-permute-start = (bf16[6,18,512]{2,0,1:T(8,128)(2,1)S(1)}, bf16[6,18,512]{2,0,1:T(8,128)(2,1)S(1)}, u32[]{:S(2)}, u32[]{:S(2)}) collective-permute-start(bf16[6,18,512]{2,0,1:T(8,128)(2,1)S(1)} %slice.64), channel_id=1, source_target_pairs={{16,0},{32,16},{48,32},{64,48},{80,64},{96,80},{112,96},{128,112},... | collective-permute-start | bytes 331784 | tf_op jit(solution)/shard_map/ppermute | solution.py:16
  30.7 5.3 %collective-permute-start.5 = (bf16[48,3,512]{2,0,1:T(8,128)(2,1)}, bf16[48,3,512]{2,0,1:T(8,128)(2,1)}, u32[]{:S(2)}, u32[]{:S(2)}) collective-permute-start(bf16[48,3,512]{2,0,1:T(8,128)(2,1)} %pad_maximum_fusion.5), channel_id=1, source_target_pairs={{1,0},{2,1},{3,2},{4,3},{5,4},{6,5},{7,6},{8,7},{9,8},{10,9},{11,1... | collective-permute-start | bytes 442376 | tf_op jit(solution)/shard_map/ppermute | solution.py:16
  44.6 4.6 %convolution_convert_fusion = bf16[864,1536]{1,0:T(8,128)(2,1)} fusion(bf16[512,1536]{1,0:T(8,128)(2,1)S(1)} %copy-done, f32[864,512]{1,0:T(8,128)} %reshape.171, f32[512]{0:T(512)S(1)} %copy-done.18, f32[864]{0:T(1024)S(1)} %rsqrt.13, f32[864]{0:T(1024)S(1)} %div.23), kind=kOutput, calls=%fused_computation.6 | convolution fusion | flops 1362051072 | bytes 6005504 | tf_op jit(solution)/shard_map/dot_general | solution.py:56
  49.1 5.3 %reshape_reshape.17 = bf16[4,12,3,6,1536]{4,3,2,1,0:T(8,128)(2,1)} reshape(bf16[864,1536]{1,0:T(8,128)(2,1)} %convolution_convert_fusion) | data formatting | bytes 5308416 | tf_op jit(solution)/shard_map/reshape;reshape | solution.py:21
  54.4 4.2 copy.46
  58.6 8.2 %reshape_reshape.18 = bf16[12,72,3,8,64]{4,3,2,1,0:T(8,128)(2,1)} reshape(bf16[4,3,12,6,1536]{4,3,2,1,0:T(8,128)(2,1)} %copy.46) | data formatting | bytes 5308416 | tf_op jit(solution)/shard_map/reshape;reshape | solution.py:58
  66.8 5.1 %fusion.36 = (bf16[12,72,1,8,64]{4,3,2,1,0:T(8,128)(2,1)}, bf16[12,72,1,8,64]{4,3,2,1,0:T(8,128)(2,1)}, bf16[12,72,1,8,64]{4,3,2,1,0:T(8,128)(2,1)}) fusion(bf16[12,72,3,8,64]{4,3,2,1,0:T(8,128)(2,1)} %reshape_reshape.18), kind=kLoop, calls=%fused_computation.77 | loop fusion | bytes 5308416 | tf_op jit(solution)/shard_map/slice | solution.py:59
  71.9 3.8 copy.71
  75.7 3.8 copy.72
  79.6 3.9 copy.70
  91.6 3.8 reshape_reshape.21
  95.4 3.8 copy.56
  115.0 8.7 %copy.61 = bf16[12,72,3,8,64]{4,3,2,1,0:T(8,128)(2,1)} copy(bf16[12,72,3,8,64]{1,4,3,0,2:T(8,128)(2,1)} %pad_maximum_fusion) | data formatting | bytes 5308416 | tf_op jit(solution)/shard_map/stack | solution.py:100
  123.7 8.2 %convert_element_type.83 = bf16[4,3,12,6,1536]{4,3,2,1,0:T(8,128)(2,1)} reshape(bf16[12,72,3,8,64]{4,3,2,1,0:T(8,128)(2,1)} %copy.61) | data formatting | bytes 5308416 | tf_op jit(solution)/shard_map/convert_element_type | solution.py:100
  131.9 4.0 copy.62
  136.0 5.4 %reshape.170 = bf16[864,1536]{1,0:T(8,128)(2,1)} reshape(bf16[4,12,3,6,1536]{4,3,2,1,0:T(8,128)(2,1)} %copy.62) | data formatting | bytes 5308416 | tf_op jit(solution)/shard_map/reshape | solution.py:28
  145.4 4.8 %multiply_reduce_fusion.1 = (f32[512]{0:T(512)S(1)}, f32[864]{0:T(1024)S(1)}, f32[864]{0:T(1024)S(1)}, f32[864,512]{1,0:T(8,128)}) fusion(f32[864,512]{1,0:T(8,128)S(1)} %copy-done.1, f32[864]{0:T(1024)S(1)} %rsqrt.13, f32[864]{0:T(1024)S(1)} %div.23, f32[512]{0:T(512)S(1)} %copy-done.18, bf16[864,1536]{1,0:T(8,128)(2,1)} %reshape.170, ...), kind=kOutput, calls=%fused_computation.12 | convolution fusion | flops 1362491136 | bytes 7783936 | tf_op jit(solution)/shard_map/dot_general | solution.py:38
  150.3 3.5 fusion.38
  153.8 3.9 copy.52
  157.6 3.9 reshape_reshape.19
  181.5 4.7 %collective-permute-done.6 = bf16[2,48,3,512]{3,2,1,0:T(4,128)(2,1)S(1)} collective-permute-done((bf16[2,48,3,512]{3,2,1,0:T(4,128)(2,1)S(1)}, bf16[2,48,3,512]{3,2,1,0:T(4,128)(2,1)S(1)}, u32[]{:S(2)}, u32[]{:S(2)}) %collective-permute-start.6) | collective-permute-done | bytes 294944 | tf_op jit(solution)/shard_map/ppermute | solution.py:16
  187.8 80.2 %psum.23 = f32[512]{0:T(512)} all-reduce(f32[512]{0:T(512)S(1)} %get-tuple-element.15), channel_id=1, replica_groups=mesh['lon'=16,'lat'=16] {'lon','lat'}, use_global_device_ids=true, to_apply=%region_10.11 | all-reduce | flops 512 | bytes 4096 | tf_op jit(solution)/shard_map/psum | solution.py:146
  272.3 161.1 %all-reduce.3.cloned.1.call-done = (f32[512,1536]{1,0:T(8,128)}, f32[512,512]{1,0:T(8,128)}) async-done(((f32[512,1536]{1,0:T(8,128)}, f32[512,512]{1,0:T(8,128)}), (f32[512,1536]{1,0:T(8,128)}, f32[512,512]{1,0:T(8,128)})) %all-reduce.3.cloned.1.call-update) | async-done | bytes 4194320 | tf_op jit(solution)/shard_map/psum | solution.py:146
  433.5 3.8 copy.76
  (118 shorter events, 79.3 us)
Async XLA Ops:
  7.2 37.4 %copy-start = (bf16[512,1536]{1,0:T(8,128)(2,1)S(1)}, bf16[512,1536]{1,0:T(8,128)(2,1)}, u32[]{:S(2)}) copy-start(bf16[512,1536]{1,0:T(8,128)(2,1)} %param.10) | copy-start | bytes 4718596
  7.2 13.5 %copy-start.17 = (s32[48,18]{0,1:T(8,128)S(1)}, s32[48,18]{0,1:T(8,128)}, u32[]{:S(2)}) copy-start(s32[48,18]{0,1:T(8,128)} %param.8) | copy-start | bytes 10372
  7.2 426.3 %all-reduce.3.cloned.1.call-start = ((), (), s32[]{:S(2)}) async-start(), calls=%async_computation | async-start | bytes 8388608 | tf_op jit(solution)/shard_map/psum | solution.py:146
  8.3 18.0 %collective-permute-start = (bf16[6,18,512]{2,0,1:T(8,128)(2,1)S(1)}, bf16[6,18,512]{2,0,1:T(8,128)(2,1)S(1)}, u32[]{:S(2)}, u32[]{:S(2)}) collective-permute-start(bf16[6,18,512]{2,0,1:T(8,128)(2,1)S(1)} %slice.64), channel_id=1, source_target_pairs={{16,0},{32,16},{48,32},{64,48},{80,64},{96,80},{112,96},{128,112},... | collective-permute-start | bytes 331784 | tf_op jit(solution)/shard_map/ppermute | solution.py:16
  15.8 5.3 %collective-permute-start.2 = (s32[6,18]{0,1:T(8,128)}, s32[6,18]{0,1:T(8,128)S(1)}, u32[]{:S(2)}, u32[]{:S(2)}) collective-permute-start(s32[6,18]{0,1:T(8,128)} %bitcast.75), channel_id=1, source_target_pairs={{16,0},{32,16},{48,32},{64,48},{80,64},{96,80},{112,96},{128,112},... | collective-permute-start | bytes 1304 | tf_op jit(solution)/shard_map/ppermute | solution.py:16
  17.4 12.5 %collective-permute-start.4 = (bf16[6,18,512]{2,0,1:T(8,128)(2,1)S(1)}, bf16[6,18,512]{2,0,1:T(8,128)(2,1)S(1)}, u32[]{:S(2)}, u32[]{:S(2)}) collective-permute-start(bf16[6,18,512]{2,0,1:T(8,128)(2,1)S(1)} %slice.75), channel_id=1, source_target_pairs={{16,0},{32,16},{48,32},{64,48},{80,64},{96,80},{112,96},{128,112},... | collective-permute-start | bytes 331784 | tf_op jit(solution)/shard_map/ppermute | solution.py:16
  18.2 2.6 copy-start.12
  21.2 3.9 collective-permute-start.3
  27.2 11.0 %collective-permute-start.1 = (bf16[48,3,512]{2,0,1:T(8,128)(2,1)S(1)}, bf16[48,3,512]{2,0,1:T(8,128)(2,1)S(1)}, u32[]{:S(2)}, u32[]{:S(2)}) collective-permute-start(bf16[48,3,512]{2,0,1:T(8,128)(2,1)S(1)} %pad_maximum_fusion.6), channel_id=1, source_target_pairs={{1,0},{2,1},{3,2},{4,3},{5,4},{6,5},{7,6},{8,7},{9,8},{10,9},{11,1... | collective-permute-start | bytes 442376 | tf_op jit(solution)/shard_map/ppermute | solution.py:16
  30.7 52.8 %collective-permute-start.5 = (bf16[48,3,512]{2,0,1:T(8,128)(2,1)}, bf16[48,3,512]{2,0,1:T(8,128)(2,1)}, u32[]{:S(2)}, u32[]{:S(2)}) collective-permute-start(bf16[48,3,512]{2,0,1:T(8,128)(2,1)} %pad_maximum_fusion.5), channel_id=1, source_target_pairs={{1,0},{2,1},{3,2},{4,3},{5,4},{6,5},{7,6},{8,7},{9,8},{10,9},{11,1... | collective-permute-start | bytes 442376 | tf_op jit(solution)/shard_map/ppermute | solution.py:16
  41.9 2.7 copy-start.18
  79.6 3.9 copy-start.7
  99.2 3.1 copy-start.16
  102.3 1.6 copy-start.10
  102.3 1.9 copy-start.11
  105.4 1.4 copy-start.3
  136.0 5.4 %copy-start.9 = (bf16[48,3,512]{2,0,1:T(8,128)(2,1)S(1)}, bf16[48,3,512]{2,0,1:T(8,128)(2,1)}, u32[]{:S(2)}) copy-start(bf16[48,3,512]{2,0,1:T(8,128)(2,1)} %copy-done.8) | copy-start | bytes 442372
  141.7 3.7 copy-start.1
  145.4 4.8 %copy-start.4 = (bf16[864,1536]{1,0:T(8,128)(2,1)S(1)}, bf16[864,1536]{1,0:T(8,128)(2,1)}, u32[]{:S(2)}) copy-start(bf16[864,1536]{1,0:T(8,128)(2,1)} %reshape.170) | copy-start | bytes 7962628
  145.4 4.8 %copy-start.6 = (bf16[864,512]{1,0:T(8,128)(2,1)S(1)}, bf16[864,512]{1,0:T(8,128)(2,1)}, u32[]{:S(2)}) copy-start(bf16[864,512]{1,0:T(8,128)(2,1)} %convert_element_type.86) | copy-start | bytes 2654212
  177.2 3.7 copy-start.5
  181.3 4.9 %collective-permute-start.6 = (bf16[2,48,3,512]{3,2,1,0:T(4,128)(2,1)S(1)}, bf16[2,48,3,512]{3,2,1,0:T(4,128)(2,1)S(1)}, u32[]{:S(2)}, u32[]{:S(2)}) collective-permute-start(bf16[2,48,3,512]{3,2,1,0:T(4,128)(2,1)S(1)} %slice.93), channel_id=1, source_target_pairs={{15,0},{0,1},{1,2},{2,3},{3,4},{4,5},{5,6},{6,7},{7,8},{8,9},{9,10... | collective-permute-start | bytes 884744 | tf_op jit(solution)/shard_map/ppermute | solution.py:16
  187.0 80.9 %collective-permute-start.7 = (bf16[2,6,18,512]{3,2,1,0:T(8,128)(2,1)}, bf16[2,6,18,512]{3,2,1,0:T(8,128)(2,1)}, u32[]{:S(2)}, u32[]{:S(2)}) collective-permute-start(bf16[2,6,18,512]{3,2,1,0:T(8,128)(2,1)} %pad_maximum_fusion.4), channel_id=1, source_target_pairs={{240,0},{0,16},{16,32},{32,48},{48,64},{64,80},{80,96},{96,112},{1... | collective-permute-start | bytes 663560 | tf_op jit(solution)/shard_map/ppermute | solution.py:16
  433.5 3.8 copy-start.13
  (4 other events, 4.6 us)
Sparse Core Ops, SparseCore 0:
  169.3 264.0 all-reduce.2
where the time goes:
time: 448 us; the launch traced here: 445 us
  waiting for transfers between devices  168 us (38%)
  local copies, waits for them, and re-layouts  114 us (25%)
  blocking collectives  80.2 us (18%)
  matrix products  30.8 us (7%)
  starting transfers between devices  19.5 us (4%)
  other arithmetic  17.9 us (4%)
  between operations  14.4 us (3%)
    psum x1, waiting for transfers between devices, body(): lax.psum((grad_qkv, grad_proj, grad_gain), ('lon', 'lat'))  161 us
    psum x1, blocking collectives, body(): lax.psum((grad_qkv, grad_proj, grad_gain), ('lon', 'lat'))  80.2 us
    unnamed x46, local copies, waits for them, and re-layouts  21.5 us
    ppermute x8, starting transfers between devices, shifted(): return lax.ppermute(block, axis, route)  19.4 us
  transfers between devices with their start and end apart: 9, of which 3 were waited for; matrix products, arithmetic and copies ran while one was open for 16% of the time, Pallas kernels for 0%

commit v1 on v0

v1 whole, which is shorter than its diff:
```python
import functools

import jax
import jax.numpy as jnp
import numpy as np
from jax import lax
from jax.experimental import pallas as pl
from jax.experimental.pallas import tpu as pltpu
from jax.sharding import Mesh, PartitionSpec as P

HEADS = 8
HEAD_DIM = 64
WIN_LON = 12
WIN_LAT = 6
WIN = WIN_LON * WIN_LAT
SHIFT_LON = 6
SHIFT_LAT = 3
D = 512
ROWS_LON = 48
COLS_LAT = 18
SLAB = WIN_LAT * ROWS_LON
EDGE = 8
HALF = 6 * WIN
F32 = jnp.float32
BF16 = jnp.bfloat16
VMEM_LIMIT = 56 * 1024 * 1024

PLANE = ("y_lo", "y_hi", "x")
LON_AXES = ("y_lo", "z")
LAT_AXES = ("y_hi", "x", "core")


def window_source(window, row):
    jj, ii = divmod(row, WIN_LON)
    return jj, (window * WIN_LON + ii + SHIFT_LON) % ROWS_LON


def inner_pick():
    out = np.zeros((3 * WIN, SLAB), np.float32)
    for window in range(3):
        for row in range(WIN):
            jj, i = window_source(window, row)
            out[window * WIN + row, jj * ROWS_LON + i] = 1
    return out


def edge_pick(column):
    out = np.zeros((WIN, SLAB + COLS_LAT * EDGE), np.float32)
    for row in range(WIN):
        jj, i = window_source(3, row)
        if i >= SHIFT_LON:
            out[row, jj * ROWS_LON + i] = 1
        else:
            out[row, SLAB + (SHIFT_LAT + column * WIN_LAT + jj) * EDGE + i] = 1
    return out


def last_pick():
    third = SHIFT_LAT * ROWS_LON
    out = np.zeros((4 * WIN, 2 * third + COLS_LAT * EDGE + SHIFT_LAT * 2 * EDGE), np.float32)
    for window in range(4):
        for row in range(WIN):
            jj, i = window_source(window, row)
            if i >= SHIFT_LON:
                at = jj * ROWS_LON + i
            elif jj < SHIFT_LAT:
                at = 2 * third + (COLS_LAT - SHIFT_LAT + jj) * EDGE + i
            else:
                at = 2 * third + COLS_LAT * EDGE + (jj - SHIFT_LAT) * 2 * EDGE + i
            out[window * WIN + row, at] = 1
    return out


def slab_place():
    out = np.zeros((SLAB, 4 * WIN), np.float32)
    for window in range(4):
        for row in range(WIN):
            jj, i = window_source(window, row)
            out[jj * ROWS_LON + i, window * WIN + row] = 1
    return out


def dot(a, b):
    return jnp.dot(a, b, preferred_element_type=F32)


def dot_nt(a, b):
    return lax.dot_general(a, b, (((1,), (1,)), ((), ())), preferred_element_type=F32)


def dot_tn(a, b):
    return lax.dot_general(a, b, (((0,), (0,)), ((), ())), preferred_element_type=F32)


def normalise(x):
    centred = x - jnp.mean(x, axis=-1, keepdims=True)
    variance = jnp.mean(centred * centred, axis=-1, keepdims=True)
    inverse = lax.rsqrt(variance + 1e-05)
    return centred * inverse, inverse


def windows_pass(x_w, g_w, lab_w, gain, wqkv, wproj, att_o, dp_o, proj, gatt, onehot, att, dp):
    normed, _ = normalise(x_w[...].astype(F32))
    hidden = (normed * gain[...]).astype(BF16)
    proj[...] = dot(hidden, wqkv[...])
    gatt[...] = dot_nt(g_w[...], wproj[...])
    lane = lax.broadcasted_iota(jnp.int32, (HALF, 128), 1).astype(F32)
    onehot[...] = jnp.where(lab_w == lane, 1.0, 0.0)
    low = lax.broadcasted_iota(jnp.int32, (WIN, 128), 1) < HEAD_DIM

    def stacked(pair):
        return jnp.concatenate([jnp.where(low, pair, 0.0), jnp.where(low, 0.0, pair)], 0)

    def unstacked(both):
        return jnp.where(low, both[:WIN], both[WIN:])

    def one_window(window, _):
        rows = pl.ds(pl.multiple_of(window * WIN, 8), WIN)
        marks = onehot[rows, :]
        marks_q = jnp.concatenate([marks, marks], 0).astype(BF16)
        bar_k = ((marks - 1.0) * 1e30).astype(BF16)
        pairs = range(HEADS // 2)
        q, k, v, do = [], [], [], []
        for pair in pairs:
            cols = pl.ds(pair * 128, 128)
            q.append(stacked(proj[rows, pl.ds(pair * 128, 128)].astype(BF16).astype(F32) * HEAD_DIM**-0.5).astype(BF16))
            k.append(proj[rows, pl.ds(D + pair * 128, 128)].astype(BF16))
            v.append(proj[rows, pl.ds(2 * D + pair * 128, 128)].astype(BF16))
            do.append(stacked(gatt[rows, cols]).astype(BF16))
        s = [dot_nt(jnp.concatenate([k[p], bar_k], 1), jnp.concatenate([q[p], marks_q], 1)) for p in pairs]
        da = [dot_nt(v[p], do[p]) for p in pairs]
        a, ab, ds = [], [], []
        for p in pairs:
            lifted = jnp.exp(s[p] - jnp.max(s[p], axis=0, keepdims=True))
            a.append(lifted * (1.0 / jnp.sum(lifted, axis=0, keepdims=True)))
            ab.append(a[p].astype(BF16))
        for p in pairs:
            inner = jnp.sum(da[p] * a[p], axis=0, keepdims=True)
            ds.append((a[p] * (da[p] - inner)).astype(BF16))
        for p in pairs:
            cols = pl.ds(p * 128, 128)
            att[rows, cols] = unstacked(dot_tn(ab[p], v[p]))
            dp[rows, pl.ds(2 * D + p * 128, 128)] = dot(ab[p], do[p])
            dp[rows, cols] = unstacked(dot_tn(ds[p], k[p])) * HEAD_DIM**-0.5
            dp[rows, pl.ds(D + p * 128, 128)] = dot(ds[p], q[p])
        return 0

    lax.fori_loop(0, 6, one_window, 0)
    att_o[...] = att[...].astype(BF16)
    dp_o[...] = dp[...].astype(BF16)
    return hidden


def first_kernel(x, g, r, pick, gain, wqkv, wproj, x_w, g_w, att_o, dp_o, gqkv, gproj, proj, gatt, onehot, att, dp):
    parts = {}
    for name, ref in (("x", x), ("g", g), ("r", r)):
        got = []
        for column in range(2):
            start = SHIFT_LAT + column * WIN_LAT
            got.append(dot(pick[...], ref[start : start + WIN_LAT].reshape(SLAB, ref.shape[-1])))
        parts[name] = jnp.concatenate(got, 0)
    x_w[...] = parts["x"].astype(BF16)
    g_w[...] = parts["g"].astype(BF16)
    hidden = windows_pass(x_w, g_w, parts["r"], gain, wqkv, wproj, att_o, dp_o, proj, gatt, onehot, att, dp)
    gqkv[...] = dot_tn(hidden, dp_o[...])
    gproj[...] = dot_tn(att_o[...], g_w[...])


def second_kernel(
    where, x, g, r, h_lon, h_lat, h_cor, pick0, pick1, pick2, gain, wqkv, wproj, gqkv1, gproj1,
    x_w, g_w, att_o, dp_o, keep, send, proj, gatt, onehot, att, dp, total,
):
    parts = []
    for first, width, ref in ((0, D, x), (D, D, g), (2 * D, 128, r)):
        lanes = pl.ds(first, width)
        got = []
        for column, pick in ((0, pick0), (1, pick1)):
            start = SHIFT_LAT + column * WIN_LAT
            own = ref[start : start + WIN_LAT].reshape(SLAB, width)
            got.append(dot(pick[...], jnp.concatenate([own, h_lon[:, lanes]], 0)))
        own = ref[COLS_LAT - SHIFT_LAT :].reshape(SHIFT_LAT * ROWS_LON, width)
        got.append(dot(pick2[...], jnp.concatenate([own, h_lat[:, lanes], h_lon[:, lanes], h_cor[:, lanes]], 0)))
        parts.append(jnp.concatenate(got, 0))
    x_w[...] = parts[0].astype(BF16)
    g_w[...] = parts[1].astype(BF16)
    row = lax.broadcasted_iota(jnp.int32, (HALF, 128), 0)
    past = jnp.zeros((HALF, 128), jnp.bool_)
    for window in range(2, 6):
        past = past | ((row >= window * WIN + WIN // 2) & (row < (window + 1) * WIN))
    labels = parts[2] + jnp.where(past, 3.0, 0.0) * where[1].astype(F32)
    hidden = windows_pass(x_w, g_w, labels, gain, wqkv, wproj, att_o, dp_o, proj, gatt, onehot, att, dp)
    total[:, pl.ds(0, 3 * D)] = gqkv1[...] + dot_tn(hidden, dp_o[...])
    total[:, pl.ds(3 * D, D)] = gproj1[...] + dot_tn(att_o[...], g_w[...])
    scaled = jnp.sum(total[:, pl.ds(0, 3 * D)] * wqkv[...].astype(F32), axis=1, keepdims=True)
    diagonal = lax.broadcasted_iota(jnp.int32, (128, 128), 0) == lax.broadcasted_iota(jnp.int32, (128, 128), 1)
    line = [
        jnp.sum(jnp.where(diagonal, scaled[at * 128 : (at + 1) * 128], 0.0), axis=0, keepdims=True) for at in range(4)
    ]
    tile = jnp.concatenate(line + [jnp.zeros((12, 128), F32)], 0).astype(BF16)
    core = where[0]
    for ref, half in ((keep, core), (send, 1 - core)):
        ref[:, pl.ds(0, 4 * D)] = total[pl.ds(pl.multiple_of(half * 256, 256), 256), :].astype(BF16)
        for piece in range(16):
            ref[pl.ds(piece * 16, 16), pl.ds(4 * D, 128)] = tile


def third_kernel(x1, g1, att1, dp1, x2, g2, att2, dp2, place, gain, wqkv, wproj, mixed, tgrad, mixed_f, tgrad_f):
    for at, (x, g, att, dp) in enumerate(((x1, g1, att1, dp1), (x2, g2, att2, dp2))):
        rows = pl.ds(at * HALF, HALF)
        flat = x[...].astype(F32)
        mixed_f[rows, :] = flat + dot(att[...], wproj[...])
        normed, inverse = normalise(flat)
        grad_normed = dot_nt(dp[...], wqkv[...]) * gain[...]
        grad_input = inverse * (
            grad_normed
            - jnp.mean(grad_normed, axis=-1, keepdims=True)
            - normed * jnp.mean(grad_normed * normed, axis=-1, keepdims=True)
        )
        tgrad_f[rows, :] = g[...].astype(F32) + grad_input
    for ref, out in ((mixed_f, mixed), (tgrad_f, tgrad)):
        for column in range(3):
            if column < 2:
                ordered = jnp.concatenate(
                    [ref[pl.ds(column * 3 * WIN, 3 * WIN), :], ref[pl.ds(HALF + column * WIN, WIN), :]], 0
                )
            else:
                ordered = ref[pl.ds(HALF + 2 * WIN, 4 * WIN), :]
            slab = dot(place[...], ordered.astype(BF16)).astype(BF16)
            out[column * WIN_LAT : (column + 1) * WIN_LAT] = slab.reshape(WIN_LAT, ROWS_LON, D)


def pass_scratch():
    return [
        pltpu.VMEM((HALF, 3 * D), F32),
        pltpu.VMEM((HALF, D), F32),
        pltpu.VMEM((HALF, 128), F32),
        pltpu.VMEM((HALF, D), F32),
        pltpu.VMEM((HALF, 3 * D), F32),
    ]


def call(kernel, outs, scratch, flops, name, scalars=0):
    def run(*args):
        specs = [pl.BlockSpec(memory_space=pltpu.SMEM)] * scalars
        specs += [pl.BlockSpec(memory_space=pltpu.VMEM)] * (len(args) - scalars)
        return pl.pallas_call(
            kernel,
            out_shape=[jax.ShapeDtypeStruct(*out) for out in outs],
            in_specs=specs,
            out_specs=[pl.BlockSpec(memory_space=pltpu.VMEM)] * len(outs),
            scratch_shapes=scratch,
            compiler_params=pltpu.CompilerParams(vmem_limit_bytes=VMEM_LIMIT),
            cost_estimate=pl.CostEstimate(flops=flops, bytes_accessed=8 * 2**20, transcendentals=2**19),
            name=name,
        )(*args)

    return run


def swapped(block, axis, size, bit):
    return lax.ppermute(block, axis, [(i, i ^ bit) for i in range(size)])


def reduced(keep, send):
    mine = (keep.astype(F32) + swapped(send, "core", 2, 1).astype(F32)).astype(BF16)
    pieces = lax.all_to_all(mine.reshape(16, 16, -1), PLANE, 0, 0, tiled=True)
    return jnp.sum(pieces.astype(F32), 0).astype(BF16)


def body(tokens, cotangent, region, gain, w_qkv, w_proj):
    x = tokens.transpose(1, 0, 2)
    g = cotangent.transpose(1, 0, 2)
    r = jnp.broadcast_to(region.T.astype(BF16)[:, :, None], (COLS_LAT, ROWS_LON, 128))
    lon_back = [((i + 1) % 16, i) for i in range(16)]
    lat_back = lon_back
    both_back = [(((i + 1) % 16) * 16 + (j + 1) % 16, i * 16 + j) for i in range(16) for j in range(16)]

    def edge(lats, lons):
        return jnp.concatenate([x[lats, lons], g[lats, lons], r[lats, lons]], -1).reshape(-1, 2 * D + 128)

    h_lon = lax.ppermute(edge(slice(None), slice(0, EDGE)), LON_AXES, lon_back)
    h_lat = lax.ppermute(edge(slice(0, SHIFT_LAT), slice(None)), LAT_AXES, lat_back)
    h_cor = lax.ppermute(edge(slice(0, SHIFT_LAT), slice(0, 2 * EDGE)), LON_AXES + LAT_AXES, both_back)

    gain_row = gain.reshape(1, D)
    acts = [((HALF, D), BF16), ((HALF, D), BF16), ((HALF, D), BF16), ((HALF, 3 * D), BF16)]
    constant = functools.partial(jnp.asarray, dtype=BF16)
    x1, g1, att1, dp1, gqkv1, gproj1 = call(
        first_kernel, acts + [((D, 3 * D), F32), ((D, D), F32)], pass_scratch(), 4 * 10**9, "inner"
    )(x, g, r, constant(inner_pick()), gain_row, w_qkv, w_proj)

    where = jnp.stack([lax.axis_index("core"), (lax.axis_index(LAT_AXES) == 15).astype(jnp.int32)]).astype(jnp.int32)
    width = 4 * D + 128
    x2, g2, att2, dp2, keep, send = call(
        second_kernel,
        acts + [((256, width), BF16), ((256, width), BF16)],
        pass_scratch() + [pltpu.VMEM((D, 4 * D), F32)],
        4 * 10**9,
        "outer",
        1,
    )(
        where, x, g, r, h_lon, h_lat, h_cor, constant(edge_pick(0)), constant(edge_pick(1)), constant(last_pick()),
        gain_row, w_qkv, w_proj, gqkv1, gproj1,
    )

    piece = reduced(keep, send)
    piece, x1, x2 = lax.optimization_barrier((piece, x1, x2))
    mixed_c, tgrad_c = call(
        third_kernel,
        [((COLS_LAT, ROWS_LON, D), BF16)] * 2,
        [pltpu.VMEM((2 * HALF, D), F32)] * 2,
        4 * 10**9,
        "tokens",
    )(x1, g1, att1, dp1, x2, g2, att2, dp2, constant(slab_place()), gain_row, w_qkv, w_proj)
    for bit in (1, 2, 4):
        piece = (piece.astype(F32) + swapped(piece, "z", 8, bit).astype(F32)).astype(BF16)

    lon_on = [(j, i) for i, j in lon_back]
    both_on = [(j, i) for i, j in both_back]
    outs = jnp.stack([mixed_c, tgrad_c], 0)
    own = COLS_LAT - SHIFT_LAT
    back_lon = lax.ppermute(outs[:, :own, :EDGE], LON_AXES, lon_on)
    back_lat = lax.ppermute(outs[:, own:], LAT_AXES, lon_on)
    back_cor = lax.ppermute(outs[:, own:, :EDGE], LON_AXES + LAT_AXES, both_on)
    strip = jnp.concatenate([back_cor, back_lon], 1)
    whole = jnp.concatenate([back_lat, outs[:, :own]], 1)
    strip = jnp.pad(strip, ((0, 0), (0, 0), (0, ROWS_LON - EDGE), (0, 0)))
    column = lax.broadcasted_iota(jnp.int32, whole.shape, 2)
    restored = jnp.where(column < SHIFT_LON, strip, whole)
    mixed = restored[0].transpose(1, 0, 2)
    tokens_grad = restored[1].transpose(1, 0, 2)

    gain_grad = piece[:4, 4 * D :].astype(F32).reshape(D) / gain
    grads = lax.all_to_all(jnp.broadcast_to(piece[None, :, : 4 * D], (16, 16, 4 * D)), PLANE, 0, 0, tiled=True)
    grads = grads.reshape(256, 4 * D)
    other = swapped(grads, "core", 2, 1)
    first = lax.axis_index("core") == 0
    full = jnp.concatenate([jnp.where(first, grads, other), jnp.where(first, other, grads)], 0).astype(F32)
    return mixed, tokens_grad, full[:, : 3 * D], full[:, 3 * D :], gain_grad


def solution(mesh):
    fine = Mesh(mesh.devices.reshape(2, 8, 2, 4, 2), ("y_lo", "z", "y_hi", "x", "core"))
    grid = P(LON_AXES, LAT_AXES, None)
    return jax.shard_map(
        body,
        mesh=fine,
        in_specs=(grid, grid, P(LON_AXES, LAT_AXES), P(), P(), P()),
        out_specs=(grid, grid, P(), P(), P()),
        check_vma=False,
    )
```

time: 448 us -> 125 us (0.28)
  waiting for transfers between devices: 168 us -> 18.4 us
  local copies, waits for them, and re-layouts: 114 us -> 11.6 us
  blocking collectives: 80.2 us -> 19.7 us
  Pallas kernels: 0 us -> 31.7 us
  matrix products: 30.8 us -> 0 us
  between operations: 14.4 us -> 0.81 us
  starting transfers between devices: 19.5 us -> 31.7 us
  other arithmetic: 17.9 us -> 8.87 us
    psum x1 -> x0, waiting for transfers between devices: 161 us -> none  [body(): lax.psum((grad_qkv, grad_proj, grad_gain), ('lon', 'lat'))]
    psum x1 -> x0, blocking collectives: 80.2 us -> none  [body(): lax.psum((grad_qkv, grad_proj, grad_gain), ('lon', 'lat'))]
    another operation x10 -> x0, local copies, waits for them, and re-layouts: 39.6 us -> none  [the longest x1 8.7 us: layer_pass(): jnp.stack([grad_queries, grad_keys, grad_values], 2).astype(jnp.bfloat16)]
    pallas_call x0 -> x3, Pallas kernels: none -> 31.7 us  [run(): pl.pallas_call(kernel, out_shape=[jax.ShapeDtypeStruct(*out) for out in o...]
    dot_general x12 -> x0, matrix products: 30.8 us -> none  [the longest x2 7.71 us: contract_cols(): lax.dot_general(left, right, (((1,), (1,)), ((), ())), preferred_element_...]
    convert_element_type x6 -> x0, local copies, waits for them, and re-layouts: 20.9 us -> none  [the longest x1 8.23 us: layer_pass(): jnp.stack([grad_queries, grad_keys, grad_values], 2).astype(jnp.bfloat16)]
    unnamed x46 -> x12, local copies, waits for them, and re-layouts: 21.5 us -> 0.85 us
    all_to_all x0 -> x1, blocking collectives: none -> 19.7 us  [reduced(): pieces = lax.all_to_all(mine.reshape(16, 16, -1), PLANE, 0, 0, tiled=True)]
  transfers between devices with their start and end apart: 9 -> 12, of which waited for: 3 -> 5; matrix products, arithmetic and copies ran while one was open for 16% -> 8% of each run, Pallas kernels for 0% -> 15%
where the time goes in v1:
time: 125 us; the launch traced here: 123 us
  starting transfers between devices  31.7 us (25%)
  Pallas kernels  31.7 us (25%)
  blocking collectives  19.7 us (16%)
  waiting for transfers between devices  18.4 us (15%)
  local copies, waits for them, and re-layouts  11.6 us (9%)
  other arithmetic  8.87 us (7%)
    pallas_call x3, Pallas kernels, run(): pl.pallas_call(kernel, out_shape=[jax.ShapeDtypeStruct(*out) for out in o...  31.7 us
    all_to_all x1, blocking collectives, reduced(): pieces = lax.all_to_all(mine.reshape(16, 16, -1), PLANE, 0, 0, tiled=True)  19.7 us
    ppermute x5, waiting for transfers between devices, swapped(): return lax.ppermute(block, axis, [(i, i ^ bit) for i in range(size)])  14.5 us
    ppermute x1, starting transfers between devices, body(): back_lat = lax.ppermute(outs[:, own:], LAT_AXES, lon_on)  7.8 us
    ppermute x1, starting transfers between devices, body(): h_lon = lax.ppermute(edge(slice(None), slice(0, EDGE)), LON_AXES, lon_back)  7.49 us
    ppermute x1, starting transfers between devices, body(): lax.ppermute(edge(slice(0, SHIFT_LAT), slice(0, 2 * EDGE)), LON_AXES + LA...  4.34 us
    ppermute x5, starting transfers between devices, swapped(): return lax.ppermute(block, axis, [(i, i ^ bit) for i in range(size)])  4.01 us
    ppermute x1, waiting for transfers between devices, body(): back_cor = lax.ppermute(outs[:, own:, :EDGE], LON_AXES + LAT_AXES, both_on)  3.87 us
  transfers between devices with their start and end apart: 12, of which 5 were waited for; matrix products, arithmetic and copies ran while one was open for 8% of the time, Pallas kernels for 15%

profile of v1, /device:TPU:1, one launch (start us, length us, event | category | flops | bytes accessed | tf_op | source)
XLA Modules:
  0.0 122.9 jit_solution(14884857517940038226)
XLA Ops:
  3.3 7.5 %collective-permute-start = (bf16[144,1152]{1,0:T(8,128)(2,1)S(1)}, bf16[144,1152]{1,0:T(8,128)(2,1)S(1)}, u32[]{:S(2)}, u32[]{:S(2)}) collective-permute-start(bf16[144,1152]{1,0:T(8,128)(2,1)S(1)} %maximum_bitcast_fusion), channel_id=1, source_target_pairs={{16,0},{32,16},{48,32},{64,48},{80,64},{96,80},{112,96},{128,112},... | collective-permute-start | bytes 995336 | tf_op jit(solution)/shard_map/ppermute | solution.py:281
  15.5 4.3 %collective-permute-start.2 = (bf16[48,1152]{1,0:T(8,128)(2,1)S(1)}, bf16[48,1152]{1,0:T(8,128)(2,1)S(1)}, u32[]{:S(2)}, u32[]{:S(2)}) collective-permute-start(bf16[48,1152]{1,0:T(8,128)(2,1)S(1)} %bitcast.52), channel_id=1, source_target_pairs={{17,0},{18,1},{19,2},{20,3},{21,4},{22,5},{23,6},{24,7},{25,8},{26... | collective-permute-start | bytes 331784 | tf_op jit(solution)/shard_map/ppermute | solution.py:283
  20.7 11.4 %inner.1 = (bf16[432,512]{1,0:T(8,128)(2,1)}, bf16[432,512]{1,0:T(8,128)(2,1)}, bf16[432,512]{1,0:T(8,128)(2,1)}, bf16[432,1536]{1,0:T(8,128)(2,1)}, f32[512,1536]{1,0:T(8,128)}, /*index=5*/f32[512,512]{1,0:T(8,128)}) custom-call(bf16[18,48,512]{2,1,0:T(8,128)(2,1)} %bitcast.45, bf16[18,48,512]{2,1,0:T(8,128)(2,1)} %bitcast.50, ...), custom_call_target="tpu_custom_call" | custom-call | flops 4000000000 | bytes 8388608 | tf_op jit(solution)/shard_map/inner/pallas_call | solution.py:246
  33.6 12.9 %outer.1 = (bf16[432,512]{1,0:T(8,128)(2,1)}, bf16[432,512]{1,0:T(8,128)(2,1)}, bf16[432,512]{1,0:T(8,128)(2,1)}, bf16[432,1536]{1,0:T(8,128)(2,1)}, bf16[256,21...) custom-call(s32[2]{0:T(128)} %pad_add_fusion.where, bf16[18,48,512]{2,1,0:T(8,128)(2,1)} %bitcast.46, ...), custom_call_target="tpu_custom_call" | custom-call | flops 4000000000 | bytes 8388608 | tf_op jit(solution)/shard_map/outer/pallas_call | solution.py:246
  47.0 2.6 %collective-permute-done.3 = bf16[256,2176]{1,0:T(8,128)(2,1)S(1)} collective-permute-done((bf16[256,2176]{1,0:T(8,128)(2,1)}, bf16[256,2176]{1,0:T(8,128)(2,1)S(1)}, u32[]{:S(2)}, u32[]{:S(2)}) %collective-permute-start.3) | collective-permute-done | bytes 1114144 | tf_op jit(solution)/shard_map/ppermute | solution.py:261
  49.6 1.5 %add_convert_fusion = bf16[256,2176]{1,0:T(8,128)(2,1)S(1)} fusion(bf16[256,2176]{1,0:T(8,128)(2,1)S(1)} %collective-permute-done.3, bf16[256,2176]{1,0:T(8,128)(2,1)} %get-tuple-element.24), kind=kLoop, calls=%fused_computation.3 | loop fusion | flops 2228224 | bytes 3342336 | tf_op jit(solution)/shard_map/convert_element_type | solution.py:265
  51.1 19.7 %all_to_all.10 = bf16[16,16,2176]{2,1,0:T(8,128)(2,1)S(1)} all-to-all(bf16[16,16,2176]{2,1,0:T(8,128)(2,1)S(1)} %bitcast.39), channel_id=1, replica_groups=mesh['y_lo'=2,'z'=8,'y_hi'=2,'x'=4,'core'=2] {'y_lo','y_hi','x'}, dimensions={0} | all-to-all | bytes 2228224 | tf_op jit(solution)/shard_map/all_to_all | solution.py:266
  71.0 1.9 %collective-permute-start.7 = (bf16[16,2176]{1,0:T(8,128)(2,1)S(1)}, bf16[16,2176]{1,0:T(8,128)(2,1)S(1)}, u32[]{:S(2)}, u32[]{:S(2)}) collective-permute-start(bf16[16,2176]{1,0:T(8,128)(2,1)S(1)} %reduce_sum.12), channel_id=1, source_target_pairs={{0,16},{16,0},{32,48},{48,32},{64,80},{80,64},{96,112},{112,96},{1... | collective-permute-start | bytes 208904 | tf_op jit(solution)/shard_map/ppermute | solution.py:261
  72.9 1.7 %collective-permute-done.7 = bf16[16,2176]{1,0:T(8,128)(2,1)S(1)} collective-permute-done((bf16[16,2176]{1,0:T(8,128)(2,1)S(1)}, bf16[16,2176]{1,0:T(8,128)(2,1)S(1)}, u32[]{:S(2)}, u32[]{:S(2)}) %collective-permute-start.7) | collective-permute-done | bytes 69664 | tf_op jit(solution)/shard_map/ppermute | solution.py:261
  74.7 4.0 %collective-permute-done.8 = bf16[16,2176]{1,0:T(8,128)(2,1)S(1)} collective-permute-done((bf16[16,2176]{1,0:T(8,128)(2,1)S(1)}, bf16[16,2176]{1,0:T(8,128)(2,1)S(1)}, u32[]{:S(2)}, u32[]{:S(2)}) %collective-permute-start.8) | collective-permute-done | bytes 69664 | tf_op jit(solution)/shard_map/ppermute | solution.py:261
  78.8 1.2 collective-permute-start.9
  80.0 6.2 %collective-permute-done.9 = bf16[16,2176]{1,0:T(8,128)(2,1)S(1)} collective-permute-done((bf16[16,2176]{1,0:T(8,128)(2,1)S(1)}, bf16[16,2176]{1,0:T(8,128)(2,1)S(1)}, u32[]{:S(2)}, u32[]{:S(2)}) %collective-permute-start.9) | collective-permute-done | bytes 69664 | tf_op jit(solution)/shard_map/ppermute | solution.py:261
  86.2 1.1 broadcast_in_dim.22
  87.3 3.7 %all-to-all-start.1 = ((bf16[16,16,2048]{2,1,0:T(8,128)(2,1)}), bf16[16,16,2048]{2,1,0:T(8,128)(2,1)S(1)}, u32[]{:S(2)}, u32[]{:S(2)}) async-start(bf16[16,16,2048]{2,1,0:T(8,128)(2,1)} %broadcast_in_dim.22), calls=%async_computation.1 | async-start | bytes 2097152 | tf_op jit(solution)/shard_map/all_to_all | solution.py:334
  90.9 7.4 %tokens.1 = (bf16[18,48,512]{2,1,0:T(8,128)(2,1)}, bf16[18,48,512]{2,1,0:T(8,128)(2,1)}) custom-call(bf16[432,512]{1,0:T(8,128)(2,1)} %get-tuple-element.28.x1, bf16[432,512]{1,0:T(8,128)(2,1)} %get-tuple-element.29.g1, bf16[432,512]{1,0:T(8,128)(2,1)} %get-tuple-element.30.att1, bf16[432,1536]{1,0:T(8,128)(2,1)} %get-tuple-element.31.dp1, ...), custom_call_target="tpu_custom_call" | custom-call | flops 4000000000 | bytes 8388608 | tf_op jit(solution)/shard_map/tokens/pallas_call | solution.py:246
  98.4 1.8 %pad_maximum_fusion.3 = bf16[2,15,8,512]{3,2,1,0:T(8,128)(2,1)} fusion(bf16[1,18,48,512]{3,2,1,0:T(8,128)(2,1)} %bitcast.35, bf16[1,18,48,512]{3,2,1,0:T(8,128)(2,1)} %bitcast.31), kind=kLoop, calls=%fused_computation.17 | loop fusion | flops 491520 | bytes 2015232 | tf_op jit(solution)/shard_map/slice | solution.py:322
  100.2 1.5 %collective-permute-start.5 = (bf16[2,15,8,512]{3,2,1,0:T(8,128)(2,1)}, bf16[2,15,8,512]{3,2,1,0:T(8,128)(2,1)}, u32[]{:S(2)}, u32[]{:S(2)}) collective-permute-start(bf16[2,15,8,512]{3,2,1,0:T(8,128)(2,1)} %pad_maximum_fusion.3), channel_id=1, source_target_pairs={{0,16},{16,32},{32,48},{48,64},{64,80},{80,96},{96,112},{112,128},... | collective-permute-start | bytes 737288 | tf_op jit(solution)/shard_map/ppermute | solution.py:322
  101.7 7.8 %collective-permute-start.6 = (bf16[2,3,48,512]{3,2,1,0:T(8,128)(2,1)S(1)}, bf16[2,3,48,512]{3,2,1,0:T(8,128)(2,1)S(1)}, u32[]{:S(2)}, u32[]{:S(2)}) collective-permute-start(bf16[2,3,48,512]{3,2,1,0:T(8,128)(2,1)S(1)} %pad_maximum_fusion.2), channel_id=1, source_target_pairs={{0,1},{1,2},{2,3},{3,4},{4,5},{5,6},{6,7},{7,8},{8,9},{9,10},{10,1... | collective-permute-start | bytes 884744 | tf_op jit(solution)/shard_map/ppermute | solution.py:323
  109.8 1.9 %collective-permute-start.4 = (bf16[2,3,8,512]{3,2,1,0:T(8,128)(2,1)S(1)}, bf16[2,3,8,512]{3,2,1,0:T(8,128)(2,1)S(1)}, u32[]{:S(2)}, u32[]{:S(2)}) collective-permute-start(bf16[2,3,8,512]{3,2,1,0:T(8,128)(2,1)S(1)} %pad_maximum_fusion.5), channel_id=1, source_target_pairs={{0,17},{1,18},{2,19},{3,20},{4,21},{5,22},{6,23},{7,24},{8,25},{9,... | collective-permute-start | bytes 147464 | tf_op jit(solution)/shard_map/ppermute | solution.py:324
  112.3 3.9 %collective-permute-done.4 = bf16[2,3,8,512]{3,2,1,0:T(8,128)(2,1)S(1)} collective-permute-done((bf16[2,3,8,512]{3,2,1,0:T(8,128)(2,1)S(1)}, bf16[2,3,8,512]{3,2,1,0:T(8,128)(2,1)S(1)}, u32[]{:S(2)}, u32[]{:S(2)}) %collective-permute-start.4) | collective-permute-done | bytes 49184 | tf_op jit(solution)/shard_map/ppermute | solution.py:324
  116.2 1.6 %fusion.3 = bf16[2,18,48,512]{3,2,1,0:T(8,128)(2,1)S(1)} fusion(bf16[1,18,48,512]{3,2,1,0:T(8,128)(2,1)S(1)} %bitcast.38, bf16[1,18,48,512]{3,2,1,0:T(8,128)(2,1)S(1)} %bitcast.34, bf16[2,15,8,512]{3,2,1,0:T(8,128)(2,1)} %collective-permute-done.5, bf16[2,3,8,512]{3,2,1,0:T(8,128)(2,1)S(1)} %collective-permute-done.4, ...), kind=kLoop, calls=%fused_computation.6 | loop fusion | flops 12386304 | bytes 4128816 | tf_op jit(solution)/shard_map/jit(_where)/select_n | solution.py:329
  117.8 1.3 %slice_bitcast_fusion = (bf16[48,18,512]{2,0,1:T(8,128)(2,1)}, bf16[48,18,512]{2,0,1:T(8,128)(2,1)}) fusion(bf16[2,18,48,512]{3,2,1,0:T(8,128)(2,1)S(1)} %fusion.3), kind=kLoop, calls=%fused_computation.11 | loop fusion | bytes 3538944 | tf_op jit(solution)/shard_map/transpose | solution.py:331
  119.8 1.1 maximum_convert_fusion.1
  120.9 2.0 %slice.91 = f32[512,1536]{1,0:T(8,128)} slice(f32[512,2048]{1,0:T(8,128)S(1)} %maximum_convert_fusion), slice={[0:512], [0:1536]} | slice | bytes 6291456 | tf_op jit(solution)/shard_map/slice | solution.py:339
  (51 shorter events, 12.1 us)
Async XLA Ops:
  3.3 29.4 %collective-permute-start = (bf16[144,1152]{1,0:T(8,128)(2,1)S(1)}, bf16[144,1152]{1,0:T(8,128)(2,1)S(1)}, u32[]{:S(2)}, u32[]{:S(2)}) collective-permute-start(bf16[144,1152]{1,0:T(8,128)(2,1)S(1)} %maximum_bitcast_fusion), channel_id=1, source_target_pairs={{16,0},{32,16},{48,32},{64,48},{80,64},{96,80},{112,96},{128,112},... | collective-permute-start | bytes 995336 | tf_op jit(solution)/shard_map/ppermute | solution.py:281
  12.8 19.9 %collective-permute-start.1 = (bf16[144,1152]{1,0:T(8,128)(2,1)S(1)}, bf16[144,1152]{1,0:T(8,128)(2,1)S(1)}, u32[]{:S(2)}, u32[]{:S(2)}) collective-permute-start(bf16[144,1152]{1,0:T(8,128)(2,1)S(1)} %bitcast.41), channel_id=1, source_target_pairs={{1,0},{2,1},{3,2},{4,3},{5,4},{6,5},{7,6},{8,7},{9,8},{10,9},{11,1... | collective-permute-start | bytes 995336 | tf_op jit(solution)/shard_map/ppermute | solution.py:282
  15.5 17.2 %collective-permute-start.2 = (bf16[48,1152]{1,0:T(8,128)(2,1)S(1)}, bf16[48,1152]{1,0:T(8,128)(2,1)S(1)}, u32[]{:S(2)}, u32[]{:S(2)}) collective-permute-start(bf16[48,1152]{1,0:T(8,128)(2,1)S(1)} %bitcast.52), channel_id=1, source_target_pairs={{17,0},{18,1},{19,2},{20,3},{21,4},{22,5},{23,6},{24,7},{25,8},{26... | collective-permute-start | bytes 331784 | tf_op jit(solution)/shard_map/ppermute | solution.py:283
  32.7 0.6 copy-start.5
  32.7 0.8 copy-start.3
  32.7 0.8 copy-start.4
  46.5 3.1 %collective-permute-start.3 = (bf16[256,2176]{1,0:T(8,128)(2,1)}, bf16[256,2176]{1,0:T(8,128)(2,1)S(1)}, u32[]{:S(2)}, u32[]{:S(2)}) collective-permute-start(bf16[256,2176]{1,0:T(8,128)(2,1)} %get-tuple-element.25), channel_id=1, source_target_pairs={{0,1},{1,0},{2,3},{3,2},{4,5},{5,4},{6,7},{7,6},{8,9},{9,8},{10,11... | collective-permute-start | bytes 3342344 | tf_op jit(solution)/shard_map/ppermute | solution.py:261
  71.0 3.6 %collective-permute-start.7 = (bf16[16,2176]{1,0:T(8,128)(2,1)S(1)}, bf16[16,2176]{1,0:T(8,128)(2,1)S(1)}, u32[]{:S(2)}, u32[]{:S(2)}) collective-permute-start(bf16[16,2176]{1,0:T(8,128)(2,1)S(1)} %reduce_sum.12), channel_id=1, source_target_pairs={{0,16},{16,0},{32,48},{48,32},{64,80},{80,64},{96,112},{112,96},{1... | collective-permute-start | bytes 208904 | tf_op jit(solution)/shard_map/ppermute | solution.py:261
  74.6 4.1 %collective-permute-start.8 = (bf16[16,2176]{1,0:T(8,128)(2,1)S(1)}, bf16[16,2176]{1,0:T(8,128)(2,1)S(1)}, u32[]{:S(2)}, u32[]{:S(2)}) collective-permute-start(bf16[16,2176]{1,0:T(8,128)(2,1)S(1)} %add_convert_fusion.3), channel_id=1, source_target_pairs={{0,32},{16,48},{32,0},{48,16},{64,96},{80,112},{96,64},{112,80},{1... | collective-permute-start | bytes 208904 | tf_op jit(solution)/shard_map/ppermute | solution.py:261
  78.8 7.3 %collective-permute-start.9 = (bf16[16,2176]{1,0:T(8,128)(2,1)S(1)}, bf16[16,2176]{1,0:T(8,128)(2,1)S(1)}, u32[]{:S(2)}, u32[]{:S(2)}) collective-permute-start(bf16[16,2176]{1,0:T(8,128)(2,1)S(1)} %add_convert_fusion.2), channel_id=1, source_target_pairs={{0,64},{16,80},{32,96},{48,112},{64,0},{80,16},{96,32},{112,48},{1... | collective-permute-start | bytes 208904 | tf_op jit(solution)/shard_map/ppermute | solution.py:261
  87.3 22.3 %all-to-all-start.1 = ((bf16[16,16,2048]{2,1,0:T(8,128)(2,1)}), bf16[16,16,2048]{2,1,0:T(8,128)(2,1)S(1)}, u32[]{:S(2)}, u32[]{:S(2)}) async-start(bf16[16,16,2048]{2,1,0:T(8,128)(2,1)} %broadcast_in_dim.22), calls=%async_computation.1 | async-start | bytes 2097152 | tf_op jit(solution)/shard_map/all_to_all | solution.py:334
  98.4 3.3 %copy-start = (bf16[18,48,512]{2,1,0:T(8,128)(2,1)S(1)}, bf16[18,48,512]{2,1,0:T(8,128)(2,1)}, u32[]{:S(2)}) copy-start(bf16[18,48,512]{2,1,0:T(8,128)(2,1)} %get-tuple-element.36) | copy-start | bytes 2654212
  98.4 3.3 %copy-start.1 = (bf16[18,48,512]{2,1,0:T(8,128)(2,1)S(1)}, bf16[18,48,512]{2,1,0:T(8,128)(2,1)}, u32[]{:S(2)}) copy-start(bf16[18,48,512]{2,1,0:T(8,128)(2,1)} %get-tuple-element.37) | copy-start | bytes 2654212
  100.2 11.5 %copy-start.2 = (f32[512]{0:T(512)S(1)}, f32[512]{0:T(512)}, u32[]{:S(2)}) copy-start(f32[512]{0:T(512)} %param.14) | copy-start | bytes 6148
  100.2 16.0 %collective-permute-start.5 = (bf16[2,15,8,512]{3,2,1,0:T(8,128)(2,1)}, bf16[2,15,8,512]{3,2,1,0:T(8,128)(2,1)}, u32[]{:S(2)}, u32[]{:S(2)}) collective-permute-start(bf16[2,15,8,512]{3,2,1,0:T(8,128)(2,1)} %pad_maximum_fusion.3), channel_id=1, source_target_pairs={{0,16},{16,32},{32,48},{48,64},{64,80},{80,96},{96,112},{112,128},... | collective-permute-start | bytes 737288 | tf_op jit(solution)/shard_map/ppermute | solution.py:322
  101.7 14.4 %collective-permute-start.6 = (bf16[2,3,48,512]{3,2,1,0:T(8,128)(2,1)S(1)}, bf16[2,3,48,512]{3,2,1,0:T(8,128)(2,1)S(1)}, u32[]{:S(2)}, u32[]{:S(2)}) collective-permute-start(bf16[2,3,48,512]{3,2,1,0:T(8,128)(2,1)S(1)} %pad_maximum_fusion.2), channel_id=1, source_target_pairs={{0,1},{1,2},{2,3},{3,4},{4,5},{5,6},{6,7},{7,8},{8,9},{9,10},{10,1... | collective-permute-start | bytes 884744 | tf_op jit(solution)/shard_map/ppermute | solution.py:323
  109.5 9.6 %collective-permute-start.10 = (bf16[256,2048]{1,0:T(8,128)(2,1)S(1)}, bf16[256,2048]{1,0:T(8,128)(2,1)S(1)}, u32[]{:S(2)}, u32[]{:S(2)}) collective-permute-start(bf16[256,2048]{1,0:T(8,128)(2,1)S(1)} %bitcast.40), channel_id=1, source_target_pairs={{0,1},{1,0},{2,3},{3,2},{4,5},{5,4},{6,7},{7,6},{8,9},{9,8},{10,11... | collective-permute-start | bytes 3145736 | tf_op jit(solution)/shard_map/ppermute | solution.py:261
  109.8 6.3 %collective-permute-start.4 = (bf16[2,3,8,512]{3,2,1,0:T(8,128)(2,1)S(1)}, bf16[2,3,8,512]{3,2,1,0:T(8,128)(2,1)S(1)}, u32[]{:S(2)}, u32[]{:S(2)}) collective-permute-start(bf16[2,3,8,512]{3,2,1,0:T(8,128)(2,1)S(1)} %pad_maximum_fusion.5), channel_id=1, source_target_pairs={{0,17},{1,18},{2,19},{3,20},{4,21},{5,22},{6,23},{7,24},{8,25},{9,... | collective-permute-start | bytes 147464 | tf_op jit(solution)/shard_map/ppermute | solution.py:324

commit v2 on v1

v2 whole, which is shorter than its diff:
```python
import functools

import jax
import jax.numpy as jnp
import numpy as np
from jax import lax
from jax.experimental import pallas as pl
from jax.experimental.pallas import tpu as pltpu
from jax.sharding import Mesh, PartitionSpec as P

HEADS = 8
HEAD_DIM = 64
WIN_LON = 12
WIN_LAT = 6
WIN = WIN_LON * WIN_LAT
SHIFT_LON = 6
SHIFT_LAT = 3
D = 512
ROWS_LON = 48
COLS_LAT = 18
SLAB = WIN_LAT * ROWS_LON
EDGE = 8
HALF = 6 * WIN
LON_ROWS, LAT_ROWS, COR_ROWS = 96, 128, 32
LON_IDS, LAT_IDS, COR_IDS = 90, 126, 18
F32 = jnp.float32
BF16 = jnp.bfloat16
MIB = 1024 * 1024

PLANE = ("y_lo", "y_hi", "x")
LON_AXES = ("y_lo", "z")
LAT_AXES = ("y_hi", "x", "core")


def window_source(window, row):
    jj, ii = divmod(row, WIN_LON)
    return jj, (window * WIN_LON + ii + SHIFT_LON) % ROWS_LON


def inner_pick():
    out = np.zeros((3 * WIN, SLAB), np.float32)
    for window in range(3):
        for row in range(WIN):
            jj, i = window_source(window, row)
            out[window * WIN + row, jj * ROWS_LON + i] = 1
    return out


def edge_pick(column):
    out = np.zeros((WIN, WIN_LAT * 16 + LON_ROWS), np.float32)
    for row in range(WIN):
        jj, i = window_source(3, row)
        if i >= SHIFT_LON:
            out[row, jj * 16 + i - 32] = 1
        else:
            out[row, WIN_LAT * 16 + (column * WIN_LAT + jj) * SHIFT_LON + i] = 1
    return out


def last_pick():
    own = SHIFT_LAT * ROWS_LON
    out = np.zeros((4 * WIN, own + LAT_ROWS + LON_ROWS + COR_ROWS), np.float32)
    for window in range(4):
        for row in range(WIN):
            jj, i = window_source(window, row)
            if i >= SHIFT_LON and jj < SHIFT_LAT:
                at = jj * ROWS_LON + i
            elif i >= SHIFT_LON:
                at = own + (jj - SHIFT_LAT) * (ROWS_LON - SHIFT_LON) + i - SHIFT_LON
            elif jj < SHIFT_LAT:
                at = own + LAT_ROWS + (2 * WIN_LAT + jj) * SHIFT_LON + i
            else:
                at = own + LAT_ROWS + LON_ROWS + (jj - SHIFT_LAT) * SHIFT_LON + i
            out[window * WIN + row, at] = 1
    return out


def slab_place():
    out = np.zeros((SLAB, 4 * WIN), np.float32)
    for window in range(4):
        for row in range(WIN):
            jj, i = window_source(window, row)
            out[jj * ROWS_LON + i, window * WIN + row] = 1
    return out


def dot(a, b):
    return jnp.dot(a, b, preferred_element_type=F32)


def dot_nt(a, b):
    return lax.dot_general(a, b, (((1,), (1,)), ((), ())), preferred_element_type=F32)


def dot_tn(a, b):
    return lax.dot_general(a, b, (((0,), (0,)), ((), ())), preferred_element_type=F32)


def normalise(x):
    centred = x - jnp.mean(x, axis=-1, keepdims=True)
    variance = jnp.mean(centred * centred, axis=-1, keepdims=True)
    inverse = lax.rsqrt(variance + 1e-05)
    return centred * inverse, inverse


def staged(pairs, sems):
    copies = [pltpu.make_async_copy(source, scratch, sems.at[at]) for at, (source, scratch) in enumerate(pairs)]
    for copy in copies:
        copy.start()
    return copies


def rows_of(shape, where):
    row = lax.broadcasted_iota(jnp.int32, shape, 0)
    return jnp.where(lax.broadcasted_iota(jnp.int32, shape, 1) == where(row), 1.0, 0.0).astype(BF16)


def strip_row(first, pitch):
    def where(row):
        lat = (row * 10923) >> 16
        return (lat + first) * pitch + row - lat * SHIFT_LON

    return where


def slab_row(row):
    lat = (row >= 42).astype(jnp.int32) + (row >= 84).astype(jnp.int32)
    return jnp.where(row < LAT_IDS, lat * ROWS_LON + SHIFT_LON + row - lat * 42, -1)


def spread_row(kept):
    def where(row):
        lat, lon = row >> 3, row & 7
        return jnp.where((lon < SHIFT_LON) & (lat < kept), lat * SHIFT_LON + lon, -1)

    return where


def wide_row(row):
    lat = (row >= 48).astype(jnp.int32) + (row >= 96).astype(jnp.int32)
    lon = row - lat * ROWS_LON
    return jnp.where(lon >= SHIFT_LON, lat * 42 + lon - SHIFT_LON, -1)


def diagonal(rows):
    shape = (rows, 128)
    return lax.broadcasted_iota(jnp.int32, shape, 0) == lax.broadcasted_iota(jnp.int32, shape, 1)


def region_marks(region, lats):
    columns = region.T
    return jnp.concatenate(
        [jnp.broadcast_to(columns[:, lat : lat + 1], (ROWS_LON, 128)) for lat in lats], 0
    ).astype(BF16)


def windows_pass(x_w, g_w, lab_w, gain, wqkv, wproj, att_b, dp_b, proj, gatt, onehot, att, dp, loads=()):
    normed, _ = normalise(x_w[...].astype(F32))
    hidden = (normed * gain[...]).astype(BF16)
    for load in loads:
        load.wait()
    proj[...] = dot(hidden, wqkv[...])
    gatt[...] = dot_nt(g_w[...], wproj[...])
    lane = lax.broadcasted_iota(jnp.int32, (HALF, 128), 1).astype(F32)
    onehot[...] = jnp.where(lab_w == lane, 1.0, 0.0)
    low = lax.broadcasted_iota(jnp.int32, (WIN, 128), 1) < HEAD_DIM

    def stacked(pair):
        return jnp.concatenate([jnp.where(low, pair, 0.0), jnp.where(low, 0.0, pair)], 0)

    def unstacked(both):
        return jnp.where(low, both[:WIN], both[WIN:])

    def one_window(window):
        rows = pl.ds(window * WIN, WIN)
        marks = onehot[rows, :]
        marks_q = jnp.concatenate([marks, marks], 0).astype(BF16)
        bar_k = ((marks - 1.0) * 1e30).astype(BF16)
        pairs = range(HEADS // 2)
        q, k, v, do = [], [], [], []
        for pair in pairs:
            cols = pl.ds(pair * 128, 128)
            q.append(stacked(proj[rows, pl.ds(pair * 128, 128)].astype(BF16).astype(F32) * HEAD_DIM**-0.5).astype(BF16))
            k.append(proj[rows, pl.ds(D + pair * 128, 128)].astype(BF16))
            v.append(proj[rows, pl.ds(2 * D + pair * 128, 128)].astype(BF16))
            do.append(stacked(gatt[rows, cols]).astype(BF16))
        s = [dot_nt(jnp.concatenate([k[p], bar_k], 1), jnp.concatenate([q[p], marks_q], 1)) for p in pairs]
        da = [dot_nt(v[p], do[p]) for p in pairs]
        a, ab, ds = [], [], []
        for p in pairs:
            lifted = jnp.exp(s[p] - jnp.max(s[p], axis=0, keepdims=True))
            a.append(lifted * (1.0 / jnp.sum(lifted, axis=0, keepdims=True)))
            ab.append(a[p].astype(BF16))
        for p in pairs:
            inner = jnp.sum(da[p] * a[p], axis=0, keepdims=True)
            ds.append((a[p] * (da[p] - inner)).astype(BF16))
        for p in pairs:
            cols = pl.ds(p * 128, 128)
            att[rows, cols] = unstacked(dot_tn(ab[p], v[p]))
            dp[rows, pl.ds(2 * D + p * 128, 128)] = dot(ab[p], do[p])
            dp[rows, cols] = unstacked(dot_tn(ds[p], k[p])) * HEAD_DIM**-0.5
            dp[rows, pl.ds(D + p * 128, 128)] = dot(ds[p], q[p])

    for window in range(6):
        one_window(window)
    att_b[...] = att[...].astype(BF16)
    dp_b[...] = dp[...].astype(BF16)
    return hidden


def first_kernel(
    x_h, g_h, region_h, pick_h, wqkv_h, wproj_h, pick0_h, pick1_h, pick2_h, gain,
    x_o, g_o, att_o, dp_o, gqkv, gproj, wqkv, wproj, pick0, pick1, pick2, strips, tails, region,
    proj, gatt, onehot, att, dp, x_w, g_w, att_b, dp_b, out_sems, x, g, pick, sems,
):
    lats = pl.ds(SHIFT_LAT, 2 * WIN_LAT)
    end = pl.ds(COLS_LAT - SHIFT_LAT, SHIFT_LAT)
    own = [(region_h, region), (pick_h, pick), (x_h.at[lats], x), (g_h.at[lats], g), (wqkv_h, wqkv), (wproj_h, wproj)]
    later = [(pick0_h, pick0), (pick1_h, pick1), (pick2_h, pick2)]
    for at, ref in enumerate((x_h, g_h)):
        later += [(ref.at[lats, pl.ds(32, 16), :], strips.at[at]), (ref.at[end], tails.at[at])]
    loads = staged(own + later, sems)
    for load in loads[:4]:
        load.wait()
    ids = region[...].astype(F32)
    parts = {"r": []}
    for column in range(2):
        start = SHIFT_LAT + column * WIN_LAT
        parts["r"].append(dot(pick[...], region_marks(ids, range(start, start + WIN_LAT))))
    parts["r"] = jnp.concatenate(parts["r"], 0)
    for name, ref in (("x", x), ("g", g)):
        got = []
        for column in range(2):
            start = column * WIN_LAT
            got.append(dot(pick[...], ref[start : start + WIN_LAT].reshape(SLAB, D)))
        parts[name] = jnp.concatenate(got, 0)
    x_w[...] = parts["x"].astype(BF16)
    g_w[...] = parts["g"].astype(BF16)
    stores = staged([(x_w, x_o), (g_w, g_o)], out_sems.at[0])
    hidden = windows_pass(x_w, g_w, parts["r"], gain, wqkv, wproj, att_b, dp_b, proj, gatt, onehot, att, dp, loads[4:6])
    stores += staged([(att_b, att_o), (dp_b, dp_o)], out_sems.at[1])
    gqkv[...] = dot_tn(hidden, dp_b[...])
    gproj[...] = dot_tn(att_b[...], g_w[...])
    for copy in loads[6:] + stores:
        copy.wait()


def second_kernel(
    where, h_lon, h_lat, h_cor, gain, gqkv1, gproj1, wqkv, wproj, pick0, pick1, pick2, strips, tails, region,
    x_o, g_o, att_o, dp_o, keep, send, proj, gatt, onehot, att, dp, x_w, g_w, att_b, dp_b, out_sems, total,
):
    parts = []
    ids = region[...].astype(F32)
    halos = ((h_lon, LON_ROWS, LON_IDS), (h_lat, LAT_ROWS, LAT_IDS), (h_cor, COR_ROWS, COR_IDS))
    for array in range(3):
        if array == 2:
            halo = []
            for packed, rows, at in halos:
                line = packed[pl.ds(at // 16 * 16, 16), pl.ds(0, 128)].astype(F32)[at % 16 : at % 16 + 1]
                column = jnp.sum(jnp.where(diagonal(rows), line, 0.0), axis=1, keepdims=True)
                halo.append(jnp.broadcast_to(column, (rows, 128)).astype(BF16))
        else:
            halo = [packed[:, pl.ds(array * D, D)] for packed, _, _ in halos]

        got = []
        for column, pick in ((0, pick0), (1, pick1)):
            first = column * WIN_LAT
            if array == 2:
                marks = region_marks(ids, range(SHIFT_LAT + first, SHIFT_LAT + first + WIN_LAT))
                own = jnp.concatenate([marks[lat * ROWS_LON + 32 : (lat + 1) * ROWS_LON] for lat in range(WIN_LAT)], 0)
            else:
                own = strips[array, first : first + WIN_LAT].reshape(WIN_LAT * 16, D)
            got.append(dot(pick[...], jnp.concatenate([own, halo[0]], 0)))
        if array == 2:
            own = region_marks(ids, range(COLS_LAT - SHIFT_LAT, COLS_LAT))
        else:
            own = tails[array].reshape(SHIFT_LAT * ROWS_LON, D)
        got.append(dot(pick2[...], jnp.concatenate([own, halo[1], halo[0], halo[2]], 0)))
        parts.append(jnp.concatenate(got, 0))
    x_w[...] = parts[0].astype(BF16)
    g_w[...] = parts[1].astype(BF16)
    stores = staged([(x_w, x_o), (g_w, g_o)], out_sems.at[0])
    row = lax.broadcasted_iota(jnp.int32, (HALF, 128), 0)
    past = jnp.zeros((HALF, 128), jnp.bool_)
    for window in range(2, 6):
        past = past | ((row >= window * WIN + WIN // 2) & (row < (window + 1) * WIN))
    labels = parts[2] + jnp.where(past, 3.0, 0.0) * where[1].astype(F32)
    hidden = windows_pass(x_w, g_w, labels, gain, wqkv, wproj, att_b, dp_b, proj, gatt, onehot, att, dp)
    stores += staged([(att_b, att_o), (dp_b, dp_o)], out_sems.at[1])
    total[:, pl.ds(0, 3 * D)] = gqkv1[...] + dot_tn(hidden, dp_b[...])
    total[:, pl.ds(3 * D, D)] = gproj1[...] + dot_tn(att_b[...], g_w[...])
    scaled = jnp.sum(total[:, pl.ds(0, 3 * D)] * wqkv[...].astype(F32), axis=1, keepdims=True)
    line = [
        jnp.sum(jnp.where(diagonal(128), scaled[at * 128 : (at + 1) * 128], 0.0), axis=0, keepdims=True) for at in range(4)
    ]
    tile = jnp.concatenate(line + [jnp.zeros((12, 128), F32)], 0).astype(BF16)
    core = where[0]
    for ref, half in ((keep, core), (send, 1 - core)):
        ref[:, pl.ds(0, 4 * D)] = total[pl.ds(pl.multiple_of(half * 256, 256), 256), :].astype(BF16)
        for piece in range(16):
            ref[pl.ds(piece * 16, 16), pl.ds(4 * D, 128)] = tile
    for store in stores:
        store.wait()


def third_kernel(
    x1_h, g1_h, att1_h, dp1_h, x2_h, g2_h, att2_h, dp2_h, place_h, wqkv_h, wproj_h, gain,
    mixed, tgrad, s_lon, s_lat, s_cor, mixed_f, tgrad_f, xs, gs, atts, dps, place, wqkv, wproj, sems,
):
    first = [(wproj_h, wproj), (wqkv_h, wqkv), (x1_h, xs.at[0]), (att1_h, atts.at[0]), (dp1_h, dps.at[0])]
    second = [(g1_h, gs.at[0]), (x2_h, xs.at[1]), (att2_h, atts.at[1]), (dp2_h, dps.at[1]), (g2_h, gs.at[1])]
    loads = staged(first + second + [(place_h, place)], sems)
    for at in range(2):
        for load in loads[:6] if at == 0 else loads[6:]:
            load.wait()
        x, g, att, dp = xs.at[at], gs.at[at], atts.at[at], dps.at[at]
        rows = pl.ds(at * HALF, HALF)
        flat = x[...].astype(F32)
        mixed_f[rows, :] = flat + dot(att[...], wproj[...])
        normed, inverse = normalise(flat)
        grad_normed = dot_nt(dp[...], wqkv[...]) * gain[...]
        grad_input = inverse * (
            grad_normed
            - jnp.mean(grad_normed, axis=-1, keepdims=True)
            - normed * jnp.mean(grad_normed * normed, axis=-1, keepdims=True)
        )
        tgrad_f[rows, :] = g[...].astype(F32) + grad_input
    for at, (ref, out) in enumerate(((mixed_f, mixed), (tgrad_f, tgrad))):
        lanes = pl.ds(at * D, D)
        strips = []
        for column in range(3):
            if column < 2:
                ordered = jnp.concatenate(
                    [ref[pl.ds(column * 3 * WIN, 3 * WIN), :], ref[pl.ds(HALF + column * WIN, WIN), :]], 0
                )
            else:
                ordered = ref[pl.ds(HALF + 2 * WIN, 4 * WIN), :]
            slab = dot(place[...], ordered.astype(BF16)).reshape(WIN_LAT, ROWS_LON, D)
            out[column * WIN_LAT : (column + 1) * WIN_LAT] = slab.astype(BF16)
            strips.append(slab[:, :EDGE].reshape(WIN_LAT * EDGE, D))
        strip = jnp.concatenate(strips, 0).astype(BF16)
        last = slab[SHIFT_LAT:].reshape(SHIFT_LAT * ROWS_LON, D).astype(BF16)
        s_lon[:, lanes] = dot(rows_of((LON_ROWS, COLS_LAT * EDGE), strip_row(0, EDGE)), strip).astype(BF16)
        s_lat[:, lanes] = dot(rows_of((LAT_ROWS, SHIFT_LAT * ROWS_LON), slab_row), last).astype(BF16)
        s_cor[:, lanes] = dot(rows_of((COR_ROWS, COLS_LAT * EDGE), strip_row(15, EDGE)), strip).astype(BF16)


def restore_kernel(mixed_c, tgrad_c, h_lon, h_lat, h_cor, mixed, tgrad):
    kept = COLS_LAT - SHIFT_LAT
    first = lax.broadcasted_iota(jnp.int32, (EDGE, D), 0) < SHIFT_LON
    for at, (own, out) in enumerate(((mixed_c, mixed), (tgrad_c, tgrad))):
        lanes = pl.ds(at * D, D)
        out[SHIFT_LAT:] = own[:kept]
        lon = dot(rows_of((kept * EDGE, LON_ROWS), spread_row(kept)), h_lon[:, lanes])
        cor = dot(rows_of((SHIFT_LAT * EDGE, COR_ROWS), spread_row(SHIFT_LAT)), h_cor[:, lanes])
        lat = dot(rows_of((SHIFT_LAT * ROWS_LON, LAT_ROWS), wide_row), h_lat[:, lanes])
        for row in range(COLS_LAT):
            if row < SHIFT_LAT:
                strip = cor[row * EDGE : (row + 1) * EDGE]
                inner = lat[row * ROWS_LON : (row + 1) * ROWS_LON]
                whole = jnp.concatenate([jnp.where(first, strip, inner[:EDGE]), inner[EDGE:]], 0)
                out[row] = whole.astype(BF16)
            else:
                strip = lon[(row - SHIFT_LAT) * EDGE : (row - SHIFT_LAT + 1) * EDGE]
                inner = own[row - SHIFT_LAT, pl.ds(0, 2 * EDGE), :].astype(F32)
                whole = jnp.concatenate([jnp.where(first, strip, inner[:EDGE]), inner[EDGE:]], 0)
                out[row, pl.ds(0, 2 * EDGE), :] = whole.astype(BF16)


def add_kernel(keep, received, out):
    out[...] = (keep[...].astype(F32) + received[...].astype(F32)).astype(BF16)


def sum_kernel(pieces, out):
    total = pieces[0].astype(F32)
    for piece in range(1, 16):
        total = total + pieces[piece].astype(F32)
    out[...] = total.astype(BF16)


def spread_kernel(piece, received, copies, gain):
    total = (piece[...].astype(F32) + received[...].astype(F32)).astype(BF16)
    gain[...] = total[:, 4 * D :].astype(F32)
    for at in range(16):
        copies[at] = total[:, : 4 * D]


def place_kernel(later, half, grads, *refs):
    gqkv, gproj, wide, square, sems = refs[2:] if later else refs
    copies = []
    for part in range(4):
        rows = pl.ds(part * 64, 64)
        wide[rows, :] = grads[rows, pl.ds(0, 3 * D)].astype(F32)
        square[rows, :] = grads[rows, pl.ds(3 * D, D)].astype(F32)
        there = pl.ds(pl.multiple_of(half[0] * 256 + part * 64, 64), 64)
        for at, (source, out) in enumerate(((wide, gqkv), (square, gproj))):
            copies.append(pltpu.make_async_copy(source.at[rows], out.at[there], sems.at[part, at]))
            copies[-1].start()
    for copy in copies:
        copy.wait()


def place(half, grads, *filled):
    hbm = pl.BlockSpec(memory_space=pl.ANY)
    return pl.pallas_call(
        functools.partial(place_kernel, bool(filled)),
        out_shape=[jax.ShapeDtypeStruct((D, 3 * D), F32), jax.ShapeDtypeStruct((D, D), F32)],
        in_specs=[pl.BlockSpec(memory_space=pltpu.SMEM), pl.BlockSpec(memory_space=pltpu.VMEM)] + [hbm] * len(filled),
        out_specs=[hbm, hbm],
        input_output_aliases={2: 0, 3: 1} if filled else {},
        scratch_shapes=[
            pltpu.VMEM((256, 3 * D), F32),
            pltpu.VMEM((256, D), F32),
            pltpu.SemaphoreType.DMA((4, 2)),
        ],
        compiler_params=pltpu.CompilerParams(vmem_limit_bytes=8 * MIB),
        cost_estimate=pl.CostEstimate(flops=10**6, bytes_accessed=3 * 2**20, transcendentals=0),
        name="place",
    )(half, grads, *filled)


def edges_kernel(x_h, g_h, region_h, h_lon, h_lat, h_cor, strips, slabs, region, sems):
    loads = [(region_h, region)]
    for at, ref in enumerate((x_h, g_h)):
        loads += [(ref.at[:, pl.ds(0, 2 * EDGE), :], strips.at[at]), (ref.at[pl.ds(0, SHIFT_LAT)], slabs.at[at])]
    for load in staged(loads, sems):
        load.wait()
    ids = region[...].astype(F32)
    marks = region_marks(ids, range(COLS_LAT))
    strip = jnp.concatenate([marks[lat * ROWS_LON : lat * ROWS_LON + 2 * EDGE] for lat in range(COLS_LAT)], 0)
    width = COLS_LAT * 2 * EDGE
    slab = SHIFT_LAT * ROWS_LON
    for out, rows, at, pick, source in (
        (h_lon, LON_ROWS, LON_IDS, rows_of((LON_ROWS, width), strip_row(SHIFT_LAT, 2 * EDGE)), strip),
        (h_lat, LAT_ROWS, LAT_IDS, rows_of((LAT_ROWS, slab), slab_row), marks[:slab]),
        (h_cor, COR_ROWS, COR_IDS, rows_of((COR_ROWS, width), strip_row(0, 2 * EDGE)), strip),
    ):
        line = jnp.sum(jnp.where(diagonal(rows), dot(pick, source), 0.0), axis=0, keepdims=True)
        line = jnp.concatenate([line] * (D // 128), 1)
        here = lax.broadcasted_iota(jnp.int32, (rows, D), 0) == at
        for array in range(2):
            tokens = slabs[array].reshape(slab, D) if out is h_lat else strips[array].reshape(width, D)
            out[:, pl.ds(array * D, D)] = jnp.where(here, line, dot(pick, tokens)).astype(BF16)


def pass_scratch():
    return [
        pltpu.VMEM((HALF, 3 * D), F32),
        pltpu.VMEM((HALF, D), F32),
        pltpu.VMEM((HALF, 128), F32),
        pltpu.VMEM((HALF, D), F32),
        pltpu.VMEM((HALF, 3 * D), F32),
        pltpu.VMEM((HALF, D), BF16),
        pltpu.VMEM((HALF, D), BF16),
        pltpu.VMEM((HALF, D), BF16),
        pltpu.VMEM((HALF, 3 * D), BF16),
        pltpu.SemaphoreType.DMA((2, 2)),
    ]


def call(kernel, outs, scratch, flops, name, scalars=0, far=0, kept=0, vmem=24):
    def run(*args):
        args = list(args)
        for at in range(scalars, scalars + far):
            args[at] = pltpu.with_memory_space_constraint(args[at], pltpu.HBM)
        specs = [pl.BlockSpec(memory_space=pltpu.SMEM)] * scalars
        specs += [pl.BlockSpec(memory_space=pltpu.HBM)] * far
        specs += [pl.BlockSpec(memory_space=pltpu.VMEM)] * (len(args) - scalars - far)
        return pl.pallas_call(
            kernel,
            out_shape=[pltpu.HBM(*out) if at < kept else jax.ShapeDtypeStruct(*out) for at, out in enumerate(outs)],
            in_specs=specs,
            out_specs=[pl.BlockSpec(memory_space=pltpu.HBM if at < kept else pltpu.VMEM) for at in range(len(outs))],
            scratch_shapes=scratch,
            compiler_params=pltpu.CompilerParams(vmem_limit_bytes=vmem * MIB),
            cost_estimate=pl.CostEstimate(flops=flops, bytes_accessed=8 * 2**20, transcendentals=2**19),
            name=name,
        )(*args)

    return run


def swapped(block, axis, size, bit):
    return lax.ppermute(block, axis, [(i, i ^ bit) for i in range(size)])


def body(tokens, cotangent, region, gain, w_qkv, w_proj):
    x = tokens.transpose(1, 0, 2)
    g = cotangent.transpose(1, 0, 2)
    edges = [((rows, 2 * D), BF16) for rows in (LON_ROWS, LAT_ROWS, COR_ROWS)]
    ids = region.T
    scratch = [pltpu.VMEM((2, COLS_LAT, 2 * EDGE, D), BF16), pltpu.VMEM((2, SHIFT_LAT, ROWS_LON, D), BF16)]
    scratch += [pltpu.VMEM((COLS_LAT, ROWS_LON), jnp.int32), pltpu.SemaphoreType.DMA((5,))]
    e_lon, e_lat, e_cor = call(edges_kernel, edges, scratch, 10**6, "edges", far=3, vmem=8)(x, g, ids)
    lon_back = [((i + 1) % 16, i) for i in range(16)]
    lat_back = lon_back
    both_back = [(((i + 1) % 16) * 16 + (j + 1) % 16, i * 16 + j) for i in range(16) for j in range(16)]

    h_lon = lax.ppermute(e_lon, LON_AXES, lon_back)
    h_lat = lax.ppermute(e_lat, LAT_AXES, lat_back)
    h_cor = lax.ppermute(e_cor, LON_AXES + LAT_AXES, both_back)

    gain_row = gain.reshape(1, D)
    acts = [((HALF, D), BF16), ((HALF, D), BF16), ((HALF, D), BF16), ((HALF, 3 * D), BF16)]
    constant = functools.partial(jnp.asarray, dtype=BF16)
    weights = [((D, 3 * D), BF16), ((D, D), BF16)]
    picks = [inner_pick(), edge_pick(0), edge_pick(1), last_pick()]
    passed = [((D, 3 * D), F32), ((D, D), F32)] + weights + [(pick.shape, BF16) for pick in picks[1:]]
    passed += [((2, 2 * WIN_LAT, 16, D), BF16), ((2, SHIFT_LAT, ROWS_LON, D), BF16), ((COLS_LAT, ROWS_LON), jnp.int32)]
    slabs = [pltpu.VMEM((2 * WIN_LAT, ROWS_LON, D), BF16)] * 2 + [pltpu.VMEM((3 * WIN, SLAB), BF16)]
    picks = [constant(pick) for pick in picks]
    x1, g1, att1, dp1, *passed = call(
        first_kernel,
        acts + passed,
        pass_scratch() + slabs + [pltpu.SemaphoreType.DMA((13,))],
        4 * 10**9,
        "inner",
        far=9,
        kept=4,
    )(x, g, ids, picks[0], w_qkv, w_proj, *picks[1:], gain_row)

    where = jnp.stack([lax.axis_index("core"), (lax.axis_index(LAT_AXES) == 15).astype(jnp.int32)]).astype(jnp.int32)
    width = 4 * D + 128
    x2, g2, att2, dp2, keep, send = call(
        second_kernel,
        acts + [((256, width), BF16), ((256, width), BF16)],
        pass_scratch() + [pltpu.VMEM((D, 4 * D), F32)],
        4 * 10**9,
        "outer",
        1,
        kept=4,
    )(where, h_lon, h_lat, h_cor, gain_row, *passed)

    (mine,) = call(add_kernel, [((256, width), BF16)], [], 10**5, "add", vmem=8)(keep, swapped(send, "core", 2, 1))
    mine, x1, x2 = lax.optimization_barrier((mine, x1, x2))
    pieces = lax.all_to_all(mine.reshape(16, 16, -1), PLANE, 0, 0, tiled=True)
    mixed_c, tgrad_c, s_lon, s_lat, s_cor = call(
        third_kernel,
        [((COLS_LAT, ROWS_LON, D), BF16)] * 2
        + edges,
        [pltpu.VMEM((2 * HALF, D), F32)] * 2
        + [pltpu.VMEM((2, HALF, D), BF16)] * 3
        + [pltpu.VMEM((2, HALF, 3 * D), BF16), pltpu.VMEM((SLAB, 4 * WIN), BF16)]
        + [pltpu.VMEM(*weight) for weight in weights]
        + [pltpu.SemaphoreType.DMA((11,))],
        4 * 10**9,
        "tokens",
        far=11,
        vmem=28,
    )(x1, g1, att1, dp1, x2, g2, att2, dp2, constant(slab_place()), w_qkv, w_proj, gain_row)
    lon_on = [(j, i) for i, j in lon_back]
    both_on = [(j, i) for i, j in both_back]
    t_lon = lax.ppermute(s_lon, LON_AXES, lon_on)
    t_lat = lax.ppermute(s_lat, LAT_AXES, lon_on)
    t_cor = lax.ppermute(s_cor, LON_AXES + LAT_AXES, both_on)

    pieces, t_lon, t_lat, t_cor = lax.optimization_barrier((pieces, t_lon, t_lat, t_cor))
    (piece,) = call(sum_kernel, [((16, width), BF16)], [], 10**5, "sum", vmem=8)(pieces)
    for bit in (1, 2):
        (piece,) = call(add_kernel, [((16, width), BF16)], [], 10**5, "add", vmem=4)(piece, swapped(piece, "z", 8, bit))
    copies, gain_tile = call(spread_kernel, [((16, 16, 4 * D), BF16), ((16, 128), F32)], [], 10**5, "spread", vmem=8)(
        piece, swapped(piece, "z", 8, 6)
    )
    gain_grad = gain_tile[:4].reshape(D) / gain
    grads = lax.all_to_all(copies, PLANE, 0, 0, tiled=True)
    mixed, tokens_grad = call(restore_kernel, [((COLS_LAT, ROWS_LON, D), BF16)] * 2, [], 10**6, "restore", vmem=10)(
        mixed_c, tgrad_c, t_lon, t_lat, t_cor
    )
    grads, mixed, tokens_grad = lax.optimization_barrier((grads, mixed, tokens_grad))
    grads = grads.reshape(256, 4 * D)
    other = swapped(grads, "core", 2, 1)
    core = where[:1]
    qkv_grad, proj_grad = place(1 - core, other, *place(core, grads))

    return mixed.transpose(1, 0, 2), tokens_grad.transpose(1, 0, 2), qkv_grad, proj_grad, gain_grad


def solution(mesh):
    fine = Mesh(mesh.devices.reshape(2, 8, 2, 4, 2), ("y_lo", "z", "y_hi", "x", "core"))
    grid = P(LON_AXES, LAT_AXES, None)
    return jax.shard_map(
        body,
        mesh=fine,
        in_specs=(grid, grid, P(LON_AXES, LAT_AXES), P(), P(), P()),
        out_specs=(grid, grid, P(), P(), P()),
        check_vma=False,
    )
```

time: 125 us -> 117 us (0.936); the launches traced: 123 us -> 117 us
  waiting for transfers between devices: 18.4 us -> 41.1 us
  blocking collectives: 19.7 us -> 0 us
  other arithmetic: 8.87 us -> 0.66 us
    all_to_all x1 -> x0, blocking collectives: 19.7 us -> none  [reduced(): pieces = lax.all_to_all(mine.reshape(16, 16, -1), PLANE, 0, 0, tiled=True)]
    all_to_all x1 -> x2, waiting for transfers between devices: 0.01 us -> 12.9 us  [the longest x1 12.9 us: body(): grads = lax.all_to_all(copies, PLANE, 0, 0, tiled=True)]
    unnamed x12 -> x22, local copies, waits for them, and re-layouts: 0.85 us -> 10.8 us
    ppermute x6, waiting for transfers between devices: 3.88 us -> 12.3 us  [the longest x1 12.3 us: body(): t_cor = lax.ppermute(s_cor, LON_AXES + LAT_AXES, both_on)]
    ppermute x6, starting transfers between devices: 24 us -> 16 us  [the longest x1 4.85 us: body(): h_lon = lax.ppermute(e_lon, LON_AXES, lon_back)]
    all_to_all x1 -> x2, starting transfers between devices: 3.66 us -> 11.4 us  [the longest x1 7.66 us: body(): grads = lax.all_to_all(copies, PLANE, 0, 0, tiled=True)]
    slice x10 -> x0, local copies, waits for them, and re-layouts: 7.25 us -> none  [the longest x3 2.65 us: edge(): x[lats, lons]]
    slice x4 -> x0, other arithmetic: 2.92 us -> none  [the longest x1 1.8 us: body(): back_lon = lax.ppermute(outs[:, :own, :EDGE], LON_AXES, lon_on)]
  transfers between devices with their start and end apart: 12 -> 13, of which waited for: 5 -> 7; matrix products, arithmetic and copies ran while one was open for 8% -> 1% of each run, Pallas kernels for 15% -> 15%
where the time goes in v2:
time: 117 us
  waiting for transfers between devices  41.1 us (35%)
  starting transfers between devices  32.1 us (27%)
  Pallas kernels  31.1 us (27%)
  local copies, waits for them, and re-layouts  10.8 us (9%)
    pallas_call x10, Pallas kernels, run(): pl.pallas_call(kernel, out_shape=[pltpu.HBM(*out) if at < kept else jax.S...  28.3 us
    ppermute x5, waiting for transfers between devices, swapped(): return lax.ppermute(block, axis, [(i, i ^ bit) for i in range(size)])  16 us
    all_to_all x1, waiting for transfers between devices, body(): grads = lax.all_to_all(copies, PLANE, 0, 0, tiled=True)  12.9 us
    ppermute x1, waiting for transfers between devices, body(): t_cor = lax.ppermute(s_cor, LON_AXES + LAT_AXES, both_on)  12.3 us
    unnamed x22, local copies, waits for them, and re-layouts  10.8 us
    all_to_all x1, starting transfers between devices, body(): grads = lax.all_to_all(copies, PLANE, 0, 0, tiled=True)  7.66 us
    ppermute x1, starting transfers between devices, body(): h_lon = lax.ppermute(e_lon, LON_AXES, lon_back)  4.85 us
    ppermute x1, starting transfers between devices, body(): h_cor = lax.ppermute(e_cor, LON_AXES + LAT_AXES, both_back)  4.82 us
  transfers between devices with their start and end apart: 13, of which 7 were waited for; matrix products, arithmetic and copies ran while one was open for 1% of the time, Pallas kernels for 15%

profile of v2, /device:TPU:1, one launch (start us, length us, event | category | flops | bytes accessed | tf_op | source)
XLA Modules:
  0.0 116.8 jit_solution(10248274810666050352)
XLA Ops:
  0.6 1.8 %edges.1 = (bf16[96,1024]{1,0:T(8,128)(2,1)S(1)}, bf16[128,1024]{1,0:T(8,128)(2,1)S(1)}, bf16[32,1024]{1,0:T(8,128)(2,1)S(1)}) custom-call(bf16[18,48,512]{2,1,0:T(8,128)(2,1)} %bitcast.17, bf16[18,48,512]{2,1,0:T(8,128)(2,1)} %bitcast.19, s32[18,48]{1,0:T(8,128)} %bitcast.21), custom_call_target="tpu_custom_call" | custom-call | flops 1000000 | bytes 8388608 | tf_op jit(solution)/shard_map/edges/pallas_call | solution.py:469
  2.5 3.3 %collective-permute-start.1 = (bf16[128,1024]{1,0:T(8,128)(2,1)S(1)}, bf16[128,1024]{1,0:T(8,128)(2,1)S(1)}, u32[]{:S(2)}, u32[]{:S(2)}) collective-permute-start(bf16[128,1024]{1,0:T(8,128)(2,1)S(1)} %get-tuple-element.52), channel_id=1, source_target_pairs={{1,0},{2,1},{3,2},{4,3},{5,4},{6,5},{7,6},{8,7},{9,8},{10,9},{11,1... | collective-permute-start | bytes 786440 | tf_op jit(solution)/shard_map/ppermute | solution.py:500
  5.8 4.9 %collective-permute-start = (bf16[96,1024]{1,0:T(8,128)(2,1)S(1)}, bf16[96,1024]{1,0:T(8,128)(2,1)S(1)}, u32[]{:S(2)}, u32[]{:S(2)}) collective-permute-start(bf16[96,1024]{1,0:T(8,128)(2,1)S(1)} %get-tuple-element.51), channel_id=1, source_target_pairs={{16,0},{32,16},{48,32},{64,48},{80,64},{96,80},{112,96},{128,112},... | collective-permute-start | bytes 589832 | tf_op jit(solution)/shard_map/ppermute | solution.py:499
  10.7 4.8 %collective-permute-start.2 = (bf16[32,1024]{1,0:T(8,128)(2,1)S(1)}, bf16[32,1024]{1,0:T(8,128)(2,1)S(1)}, u32[]{:S(2)}, u32[]{:S(2)}) collective-permute-start(bf16[32,1024]{1,0:T(8,128)(2,1)S(1)} %get-tuple-element.53), channel_id=1, source_target_pairs={{17,0},{18,1},{19,2},{20,3},{21,4},{22,5},{23,6},{24,7},{25,8},{26... | collective-permute-start | bytes 196616 | tf_op jit(solution)/shard_map/ppermute | solution.py:501
  15.5 8.0 %inner.1 = (bf16[432,512]{1,0:T(8,128)(2,1)}, bf16[432,512]{1,0:T(8,128)(2,1)}, bf16[432,512]{1,0:T(8,128)(2,1)}, bf16[432,1536]{1,0:T(8,128)(2,1)}, f32[512,153...) custom-call(bf16[18,48,512]{2,1,0:T(8,128)(2,1)} %bitcast.18, ...), custom_call_target="tpu_custom_call" | custom-call | flops 4000000000 | bytes 8388608 | tf_op jit(solution)/shard_map/inner/pallas_call | solution.py:469
  23.5 1.7 %copy-done.1 = f32[512,1536]{1,0:T(8,128)} copy-done((f32[512,1536]{1,0:T(8,128)}, f32[512,1536]{1,0:T(8,128)S(1)}, u32[]{:S(2)}) %copy-start.1) | copy-done | bytes 3145752
  28.4 1.9 %copy-done.2 = f32[512,1536]{1,0:T(8,128)S(1)} copy-done((f32[512,1536]{1,0:T(8,128)S(1)}, f32[512,1536]{1,0:T(8,128)}, u32[]{:S(2)}) %copy-start.2) | copy-done | bytes 3145752
  34.5 8.1 %outer.1 = (bf16[432,512]{1,0:T(8,128)(2,1)}, bf16[432,512]{1,0:T(8,128)(2,1)}, bf16[432,512]{1,0:T(8,128)(2,1)}, bf16[432,1536]{1,0:T(8,128)(2,1)}, bf16[256,21...) custom-call(s32[2]{0:T(128)S(1)} %pad_add_fusion.where, bf16[96,1024]{1,0:T(8,128)(2,1)S(1)} %collective-permute-done.h_lon, ...), custom_call_target="tpu_custom_call" | custom-call | flops 4000000000 | bytes 8388608 | tf_op jit(solution)/shard_map/outer/pallas_call | solution.py:469
  42.9 2.7 %collective-permute-done.3.received = bf16[256,2176]{1,0:T(8,128)(2,1)S(1)} collective-permute-done((bf16[256,2176]{1,0:T(8,128)(2,1)S(1)}, bf16[256,2176]{1,0:T(8,128)(2,1)S(1)}, u32[]{:S(2)}, u32[]{:S(2)}) %collective-permute-start.3) | collective-permute-done | bytes 1114144 | tf_op jit(solution)/shard_map/ppermute | solution.py:484
  45.6 1.3 %add.13 = bf16[256,2176]{1,0:T(8,128)(2,1)} custom-call(bf16[256,2176]{1,0:T(8,128)(2,1)S(1)} %get-tuple-element.64.keep, bf16[256,2176]{1,0:T(8,128)(2,1)S(1)} %collective-permute-done.3.received), custom_call_target="tpu_custom_call" | custom-call | flops 100000 | bytes 8388608 | tf_op jit(solution)/shard_map/add/pallas_call | solution.py:469
  46.9 3.7 %all-to-all-start = ((bf16[16,16,2176]{2,1,0:T(8,128)(2,1)}), bf16[16,16,2176]{2,1,0:T(8,128)(2,1)S(1)}, u32[]{:S(2)}, u32[]{:S(2)}) async-start(bf16[16,16,2176]{2,1,0:T(8,128)(2,1)} %bitcast.6), calls=%async_computation | async-start | bytes 2228224 | tf_op jit(solution)/shard_map/all_to_all | solution.py:536
  50.6 6.3 %tokens.1 = (bf16[18,48,512]{2,1,0:T(8,128)(2,1)S(1)}, bf16[18,48,512]{2,1,0:T(8,128)(2,1)S(1)}, bf16[96,1024]{1,0:T(8,128)(2,1)S(1)}, bf16[128,1024]{1,0:T(8,128)(2,1)S(1)}, bf16[32,1024]{1,0:T(8,128)(2,1)S(1)}) custom-call(bf16[432,512]{1,0:T(8,128)(2,1)} %get-tuple-element.69.x1_h, bf16[432,512]{1,0:T(8,128)(2,1)} %get-tuple-element.70.g1_h, ...), custom_call_target="tpu_custom_call" | custom-call | flops 4000000000 | bytes 8388608 | tf_op jit(solution)/shard_map/tokens/pallas_call | solution.py:469
  56.9 1.6 %collective-permute-start.5 = (bf16[128,1024]{1,0:T(8,128)(2,1)S(1)}, bf16[128,1024]{1,0:T(8,128)(2,1)S(1)}, u32[]{:S(2)}, u32[]{:S(2)}) collective-permute-start(bf16[128,1024]{1,0:T(8,128)(2,1)S(1)} %get-tuple-element.78), channel_id=1, source_target_pairs={{0,1},{1,2},{2,3},{3,4},{4,5},{5,6},{6,7},{7,8},{8,9},{9,10},{10,1... | collective-permute-start | bytes 786440 | tf_op jit(solution)/shard_map/ppermute | solution.py:554
  58.5 1.4 %collective-permute-start.4 = (bf16[96,1024]{1,0:T(8,128)(2,1)S(1)}, bf16[96,1024]{1,0:T(8,128)(2,1)S(1)}, u32[]{:S(2)}, u32[]{:S(2)}) collective-permute-start(bf16[96,1024]{1,0:T(8,128)(2,1)S(1)} %get-tuple-element.77), channel_id=1, source_target_pairs={{0,16},{16,32},{32,48},{48,64},{64,80},{80,96},{96,112},{112,128},... | collective-permute-start | bytes 589832 | tf_op jit(solution)/shard_map/ppermute | solution.py:553
  60.0 12.3 %collective-permute-done.6.h_cor = bf16[32,1024]{1,0:T(8,128)(2,1)S(1)} collective-permute-done((bf16[32,1024]{1,0:T(8,128)(2,1)S(1)}, bf16[32,1024]{1,0:T(8,128)(2,1)S(1)}, u32[]{:S(2)}, u32[]{:S(2)}) %collective-permute-start.6) | collective-permute-done | bytes 65568 | tf_op jit(solution)/shard_map/ppermute | solution.py:555
  72.5 3.1 %collective-permute-done.7.received = bf16[16,2176]{1,0:T(8,128)(2,1)S(1)} collective-permute-done((bf16[16,2176]{1,0:T(8,128)(2,1)S(1)}, bf16[16,2176]{1,0:T(8,128)(2,1)S(1)}, u32[]{:S(2)}, u32[]{:S(2)}) %collective-permute-start.7) | collective-permute-done | bytes 69664 | tf_op jit(solution)/shard_map/ppermute | solution.py:484
  75.8 4.5 %collective-permute-done.8.received = bf16[16,2176]{1,0:T(8,128)(2,1)S(1)} collective-permute-done((bf16[16,2176]{1,0:T(8,128)(2,1)S(1)}, bf16[16,2176]{1,0:T(8,128)(2,1)S(1)}, u32[]{:S(2)}, u32[]{:S(2)}) %collective-permute-start.8) | collective-permute-done | bytes 69664 | tf_op jit(solution)/shard_map/ppermute | solution.py:484
  80.5 5.3 %collective-permute-done.9.received = bf16[16,2176]{1,0:T(8,128)(2,1)S(1)} collective-permute-done((bf16[16,2176]{1,0:T(8,128)(2,1)S(1)}, bf16[16,2176]{1,0:T(8,128)(2,1)S(1)}, u32[]{:S(2)}, u32[]{:S(2)}) %collective-permute-start.9) | collective-permute-done | bytes 69664 | tf_op jit(solution)/shard_map/ppermute | solution.py:484
  86.8 7.7 %all-to-all-start.1 = ((bf16[16,16,2048]{2,1,0:T(8,128)(2,1)}), bf16[16,16,2048]{2,1,0:T(8,128)(2,1)S(1)}, u32[]{:S(2)}, u32[]{:S(2)}) async-start(bf16[16,16,2048]{2,1,0:T(8,128)(2,1)} %get-tuple-element.81), calls=%async_computation.1 | async-start | bytes 2097152 | tf_op jit(solution)/shard_map/all_to_all | solution.py:565
  94.5 1.5 %restore.1 = (bf16[18,48,512]{2,1,0:T(8,128)(2,1)}, bf16[18,48,512]{2,1,0:T(8,128)(2,1)}) custom-call(bf16[18,48,512]{2,1,0:T(8,128)(2,1)S(1)} %get-tuple-element.82.mixed_c, bf16[18,48,512]{2,1,0:T(8,128)(2,1)S(1)} %get-tuple-element.83.tgrad_c, bf16[96,1024]{1,0:T(8,128)(2,1)S(1)} %collective-permute-done.4.h_lon, ...), custom_call_target="tpu_custom_call" | custom-call | flops 1000000 | bytes 8388608 | tf_op jit(solution)/shard_map/restore/pallas_call | solution.py:469
  96.0 12.9 %all-to-all-done.1 = bf16[16,16,2048]{2,1,0:T(8,128)(2,1)S(1)} async-done(((bf16[16,16,2048]{2,1,0:T(8,128)(2,1)}), bf16[16,16,2048]{2,1,0:T(8,128)(2,1)S(1)}, u32[]{:S(2)}, u32[]{:S(2)}) %all-to-all-start.1) | async-done | bytes 1048608 | tf_op jit(solution)/shard_map/all_to_all | solution.py:565
  108.8 4.1 %collective-permute-start.10 = (bf16[256,2048]{1,0:T(8,128)(2,1)S(1)}, bf16[256,2048]{1,0:T(8,128)(2,1)S(1)}, u32[]{:S(2)}, u32[]{:S(2)}) collective-permute-start(bf16[256,2048]{1,0:T(8,128)(2,1)S(1)} %bitcast.12), channel_id=1, source_target_pairs={{0,1},{1,0},{2,3},{3,2},{4,5},{5,4},{6,7},{7,6},{8,9},{9,8},{10,11... | collective-permute-start | bytes 3145736 | tf_op jit(solution)/shard_map/ppermute | solution.py:484
  113.6 1.4 %place.2 = (f32[512,1536]{1,0:T(8,128)}, f32[512,512]{1,0:T(8,128)}) custom-call(s32[1]{0:T(128)} %bitcast.half, bf16[256,2048]{1,0:T(8,128)(2,1)S(1)} %bitcast.13), custom_call_target="tpu_custom_call" | custom-call | flops 1000000 | bytes 3145728 | tf_op jit(solution)/shard_map/place/pallas_call | solution.py:405
  115.3 1.4 %place.3 = (f32[512,1536]{1,0:T(8,128)}, f32[512,512]{1,0:T(8,128)}) custom-call(s32[1]{0:T(128)S(6)} %sub.3.half, bf16[256,2048]{1,0:T(8,128)(2,1)S(1)} %collective-permute-done.10.grads, f32[512,1536]{1,0:T(8,128)} %get-tuple-element.92.refs_0_, f32[512,512]{1,0:T(8,128)} %get-tuple-element.93.refs_1_), custom_call_target="tpu_custom_call", output_to_operand_aliasing={{0}: (2, {}), {1}: (3, {})} | custom-call | flops 1000000 | bytes 3145728 | tf_op jit(solution)/shard_map/place/pallas_call | solution.py:405
  (38 shorter events, 10.1 us)
Async XLA Ops:
  0.6 14.9 %copy-start = (f32[512]{0:T(512)S(1)}, f32[512]{0:T(512)}, u32[]{:S(2)}) copy-start(f32[512]{0:T(512)} %param.14) | copy-start | bytes 6148
  2.5 25.9 %collective-permute-start.1 = (bf16[128,1024]{1,0:T(8,128)(2,1)S(1)}, bf16[128,1024]{1,0:T(8,128)(2,1)S(1)}, u32[]{:S(2)}, u32[]{:S(2)}) collective-permute-start(bf16[128,1024]{1,0:T(8,128)(2,1)S(1)} %get-tuple-element.52), channel_id=1, source_target_pairs={{1,0},{2,1},{3,2},{4,3},{5,4},{6,5},{7,6},{8,7},{9,8},{10,9},{11,1... | collective-permute-start | bytes 786440 | tf_op jit(solution)/shard_map/ppermute | solution.py:500
  5.8 22.6 %collective-permute-start = (bf16[96,1024]{1,0:T(8,128)(2,1)S(1)}, bf16[96,1024]{1,0:T(8,128)(2,1)S(1)}, u32[]{:S(2)}, u32[]{:S(2)}) collective-permute-start(bf16[96,1024]{1,0:T(8,128)(2,1)S(1)} %get-tuple-element.51), channel_id=1, source_target_pairs={{16,0},{32,16},{48,32},{64,48},{80,64},{96,80},{112,96},{128,112},... | collective-permute-start | bytes 589832 | tf_op jit(solution)/shard_map/ppermute | solution.py:499
  10.7 17.8 %collective-permute-start.2 = (bf16[32,1024]{1,0:T(8,128)(2,1)S(1)}, bf16[32,1024]{1,0:T(8,128)(2,1)S(1)}, u32[]{:S(2)}, u32[]{:S(2)}) collective-permute-start(bf16[32,1024]{1,0:T(8,128)(2,1)S(1)} %get-tuple-element.53), channel_id=1, source_target_pairs={{17,0},{18,1},{19,2},{20,3},{21,4},{22,5},{23,6},{24,7},{25,8},{26... | collective-permute-start | bytes 196616 | tf_op jit(solution)/shard_map/ppermute | solution.py:501
  23.5 1.7 %copy-start.1 = (f32[512,1536]{1,0:T(8,128)}, f32[512,1536]{1,0:T(8,128)S(1)}, u32[]{:S(2)}) copy-start(f32[512,1536]{1,0:T(8,128)S(1)} %get-tuple-element.54.gqkv1) | copy-start | bytes 9437188
  25.2 1.0 copy-start.3
  26.2 0.8 copy-start.5
  26.9 0.7 copy-start.7
  27.6 0.7 copy-start.9
  28.4 1.9 %copy-start.2 = (f32[512,1536]{1,0:T(8,128)S(1)}, f32[512,1536]{1,0:T(8,128)}, u32[]{:S(2)}) copy-start(f32[512,1536]{1,0:T(8,128)} %copy-done.1) | copy-start | bytes 9437188
  30.3 1.2 %copy-start.4 = (f32[512,512]{1,0:T(8,128)S(1)}, f32[512,512]{1,0:T(8,128)}, u32[]{:S(2)}) copy-start(f32[512,512]{1,0:T(8,128)} %copy-done.3) | copy-start | bytes 3145732
  31.6 1.0 copy-start.6
  32.6 1.0 copy-start.8
  33.5 1.0 copy-start.10
  42.6 3.1 %collective-permute-start.3 = (bf16[256,2176]{1,0:T(8,128)(2,1)S(1)}, bf16[256,2176]{1,0:T(8,128)(2,1)S(1)}, u32[]{:S(2)}, u32[]{:S(2)}) collective-permute-start(bf16[256,2176]{1,0:T(8,128)(2,1)S(1)} %get-tuple-element.65), channel_id=1, source_target_pairs={{0,1},{1,0},{2,3},{3,2},{4,5},{5,4},{6,7},{7,6},{8,9},{9,8},{10,11... | collective-permute-start | bytes 3342344 | tf_op jit(solution)/shard_map/ppermute | solution.py:484
  46.9 25.4 %all-to-all-start = ((bf16[16,16,2176]{2,1,0:T(8,128)(2,1)}), bf16[16,16,2176]{2,1,0:T(8,128)(2,1)S(1)}, u32[]{:S(2)}, u32[]{:S(2)}) async-start(bf16[16,16,2176]{2,1,0:T(8,128)(2,1)} %bitcast.6), calls=%async_computation | async-start | bytes 2228224 | tf_op jit(solution)/shard_map/all_to_all | solution.py:536
  56.9 15.4 %collective-permute-start.5 = (bf16[128,1024]{1,0:T(8,128)(2,1)S(1)}, bf16[128,1024]{1,0:T(8,128)(2,1)S(1)}, u32[]{:S(2)}, u32[]{:S(2)}) collective-permute-start(bf16[128,1024]{1,0:T(8,128)(2,1)S(1)} %get-tuple-element.78), channel_id=1, source_target_pairs={{0,1},{1,2},{2,3},{3,4},{4,5},{5,6},{6,7},{7,8},{8,9},{9,10},{10,1... | collective-permute-start | bytes 786440 | tf_op jit(solution)/shard_map/ppermute | solution.py:554
  58.5 13.7 %collective-permute-start.4 = (bf16[96,1024]{1,0:T(8,128)(2,1)S(1)}, bf16[96,1024]{1,0:T(8,128)(2,1)S(1)}, u32[]{:S(2)}, u32[]{:S(2)}) collective-permute-start(bf16[96,1024]{1,0:T(8,128)(2,1)S(1)} %get-tuple-element.77), channel_id=1, source_target_pairs={{0,16},{16,32},{32,48},{48,64},{64,80},{80,96},{96,112},{112,128},... | collective-permute-start | bytes 589832 | tf_op jit(solution)/shard_map/ppermute | solution.py:553
  60.0 12.3 %collective-permute-start.6 = (bf16[32,1024]{1,0:T(8,128)(2,1)S(1)}, bf16[32,1024]{1,0:T(8,128)(2,1)S(1)}, u32[]{:S(2)}, u32[]{:S(2)}) collective-permute-start(bf16[32,1024]{1,0:T(8,128)(2,1)S(1)} %get-tuple-element.79), channel_id=1, source_target_pairs={{0,17},{1,18},{2,19},{3,20},{4,21},{5,22},{6,23},{7,24},{8,25},{9,... | collective-permute-start | bytes 196616 | tf_op jit(solution)/shard_map/ppermute | solution.py:555
  72.4 3.2 %collective-permute-start.7 = (bf16[16,2176]{1,0:T(8,128)(2,1)S(1)}, bf16[16,2176]{1,0:T(8,128)(2,1)S(1)}, u32[]{:S(2)}, u32[]{:S(2)}) collective-permute-start(bf16[16,2176]{1,0:T(8,128)(2,1)S(1)} %sum.1.keep), channel_id=1, source_target_pairs={{0,16},{16,0},{32,48},{48,32},{64,80},{80,64},{96,112},{112,96},{1... | collective-permute-start | bytes 208904 | tf_op jit(solution)/shard_map/ppermute | solution.py:484
  75.7 4.6 %collective-permute-start.8 = (bf16[16,2176]{1,0:T(8,128)(2,1)S(1)}, bf16[16,2176]{1,0:T(8,128)(2,1)S(1)}, u32[]{:S(2)}, u32[]{:S(2)}) collective-permute-start(bf16[16,2176]{1,0:T(8,128)(2,1)S(1)} %add.14.keep), channel_id=1, source_target_pairs={{0,32},{16,48},{32,0},{48,16},{64,96},{80,112},{96,64},{112,80},{1... | collective-permute-start | bytes 208904 | tf_op jit(solution)/shard_map/ppermute | solution.py:484
  80.4 5.4 %collective-permute-start.9 = (bf16[16,2176]{1,0:T(8,128)(2,1)S(1)}, bf16[16,2176]{1,0:T(8,128)(2,1)S(1)}, u32[]{:S(2)}, u32[]{:S(2)}) collective-permute-start(bf16[16,2176]{1,0:T(8,128)(2,1)S(1)} %add.15.piece), channel_id=1, source_target_pairs={{0,96},{16,112},{32,64},{48,80},{64,32},{80,48},{96,0},{112,16},{1... | collective-permute-start | bytes 208904 | tf_op jit(solution)/shard_map/ppermute | solution.py:484
  86.8 22.0 %all-to-all-start.1 = ((bf16[16,16,2048]{2,1,0:T(8,128)(2,1)}), bf16[16,16,2048]{2,1,0:T(8,128)(2,1)S(1)}, u32[]{:S(2)}, u32[]{:S(2)}) async-start(bf16[16,16,2048]{2,1,0:T(8,128)(2,1)} %get-tuple-element.81), calls=%async_computation.1 | async-start | bytes 2097152 | tf_op jit(solution)/shard_map/all_to_all | solution.py:565
  108.8 6.4 %collective-permute-start.10 = (bf16[256,2048]{1,0:T(8,128)(2,1)S(1)}, bf16[256,2048]{1,0:T(8,128)(2,1)S(1)}, u32[]{:S(2)}, u32[]{:S(2)}) collective-permute-start(bf16[256,2048]{1,0:T(8,128)(2,1)S(1)} %bitcast.12), channel_id=1, source_target_pairs={{0,1},{1,0},{2,3},{3,2},{4,5},{5,4},{6,7},{7,6},{8,9},{9,8},{10,11... | collective-permute-start | bytes 3145736 | tf_op jit(solution)/shard_map/ppermute | solution.py:484

commit v3 on v2

--- a/solution.py
+++ b/solution.py
@@ -419,7 +419,7 @@
     )(half, grads, *filled)
 
 
-def edges_kernel(x_h, g_h, region_h, h_lon, h_lat, h_cor, strips, slabs, region, sems):
+def edges_kernel(where, x_h, g_h, region_h, h_lon, h_lat, h_cor, strips, slabs, region, sems):
     loads = [(region_h, region)]
     for at, ref in enumerate((x_h, g_h)):
         loads += [(ref.at[:, pl.ds(0, 2 * EDGE), :], strips.at[at]), (ref.at[pl.ds(0, SHIFT_LAT)], slabs.at[at])]
@@ -488,10 +488,11 @@
     x = tokens.transpose(1, 0, 2)
     g = cotangent.transpose(1, 0, 2)
     edges = [((rows, 2 * D), BF16) for rows in (LON_ROWS, LAT_ROWS, COR_ROWS)]
+    where = jnp.stack([lax.axis_index("core"), (lax.axis_index(LAT_AXES) == 15).astype(jnp.int32)]).astype(jnp.int32)
     ids = region.T
     scratch = [pltpu.VMEM((2, COLS_LAT, 2 * EDGE, D), BF16), pltpu.VMEM((2, SHIFT_LAT, ROWS_LON, D), BF16)]
     scratch += [pltpu.VMEM((COLS_LAT, ROWS_LON), jnp.int32), pltpu.SemaphoreType.DMA((5,))]
-    e_lon, e_lat, e_cor = call(edges_kernel, edges, scratch, 10**6, "edges", far=3, vmem=8)(x, g, ids)
+    e_lon, e_lat, e_cor = call(edges_kernel, edges, scratch, 10**6, "edges", 1, far=3, vmem=8)(where, x, g, ids)
     lon_back = [((i + 1) % 16, i) for i in range(16)]
     lat_back = lon_back
     both_back = [(((i + 1) % 16) * 16 + (j + 1) % 16, i * 16 + j) for i in range(16) for j in range(16)]
@@ -519,7 +520,6 @@
         kept=4,
     )(x, g, ids, picks[0], w_qkv, w_proj, *picks[1:], gain_row)
 
-    where = jnp.stack([lax.axis_index("core"), (lax.axis_index(LAT_AXES) == 15).astype(jnp.int32)]).astype(jnp.int32)
     width = 4 * D + 128
     x2, g2, att2, dp2, keep, send = call(
         second_kernel,

time: 117 us -> 107 us (0.915)
  local copies, waits for them, and re-layouts: 10.8 us -> 0.01 us
    unnamed x22 -> x2, local copies, waits for them, and re-layouts: 10.8 us -> 0.01 us
  transfers between devices with their start and end apart: 13 -> 13, of which waited for: 7 -> 7; matrix products, arithmetic and copies ran while one was open for 1% -> 1% of each run, Pallas kernels for 15% -> 16%
where the time goes in v3:
time: 107 us
  waiting for transfers between devices  41.3 us (39%)
  starting transfers between devices  32 us (30%)
  Pallas kernels  31.7 us (30%)
    pallas_call x10, Pallas kernels, run(): pl.pallas_call(kernel, out_shape=[pltpu.HBM(*out) if at < kept else jax.S...  28.9 us
    ppermute x5, waiting for transfers between devices, swapped(): return lax.ppermute(block, axis, [(i, i ^ bit) for i in range(size)])  16.2 us
    all_to_all x1, waiting for transfers between devices, body(): grads = lax.all_to_all(copies, PLANE, 0, 0, tiled=True)  12.8 us
    ppermute x1, waiting for transfers between devices, body(): t_cor = lax.ppermute(s_cor, LON_AXES + LAT_AXES, both_on)  12.3 us
    all_to_all x1, starting transfers between devices, body(): grads = lax.all_to_all(copies, PLANE, 0, 0, tiled=True)  7.46 us
    ppermute x1, starting transfers between devices, body(): h_lon = lax.ppermute(e_lon, LON_AXES, lon_back)  4.85 us
    ppermute x5, starting transfers between devices, swapped(): return lax.ppermute(block, axis, [(i, i ^ bit) for i in range(size)])  4.84 us
    ppermute x1, starting transfers between devices, body(): h_cor = lax.ppermute(e_cor, LON_AXES + LAT_AXES, both_back)  4.82 us
  transfers between devices with their start and end apart: 13, of which 7 were waited for; matrix products, arithmetic and copies ran while one was open for 1% of the time, Pallas kernels for 16%

profile of v3, /device:TPU:1, one launch (start us, length us, event | category | flops | bytes accessed | tf_op | source)
XLA Modules:
  0.0 106.6 jit_solution(5554305931947881347)
XLA Ops:
  0.7 2.4 %edges.1 = (bf16[96,1024]{1,0:T(8,128)(2,1)S(1)}, bf16[128,1024]{1,0:T(8,128)(2,1)S(1)}, bf16[32,1024]{1,0:T(8,128)(2,1)S(1)}) custom-call(s32[2]{0:T(128)S(1)} %pad_add_fusion.where, bf16[18,48,512]{2,1,0:T(8,128)(2,1)} %bitcast.17, bf16[18,48,512]{2,1,0:T(8,128)(2,1)} %bitcast.19, s32[18,48]{1,0:T(8,128)} %bitcast.21), custom_call_target="tpu_custom_call" | custom-call | flops 1000000 | bytes 8388608 | tf_op jit(solution)/shard_map/edges/pallas_call | solution.py:469
  3.1 3.3 %collective-permute-start.1 = (bf16[128,1024]{1,0:T(8,128)(2,1)S(1)}, bf16[128,1024]{1,0:T(8,128)(2,1)S(1)}, u32[]{:S(2)}, u32[]{:S(2)}) collective-permute-start(bf16[128,1024]{1,0:T(8,128)(2,1)S(1)} %get-tuple-element.52), channel_id=1, source_target_pairs={{1,0},{2,1},{3,2},{4,3},{5,4},{6,5},{7,6},{8,7},{9,8},{10,9},{11,1... | collective-permute-start | bytes 786440 | tf_op jit(solution)/shard_map/ppermute | solution.py:501
  6.4 4.9 %collective-permute-start = (bf16[96,1024]{1,0:T(8,128)(2,1)S(1)}, bf16[96,1024]{1,0:T(8,128)(2,1)S(1)}, u32[]{:S(2)}, u32[]{:S(2)}) collective-permute-start(bf16[96,1024]{1,0:T(8,128)(2,1)S(1)} %get-tuple-element.51), channel_id=1, source_target_pairs={{16,0},{32,16},{48,32},{64,48},{80,64},{96,80},{112,96},{128,112},... | collective-permute-start | bytes 589832 | tf_op jit(solution)/shard_map/ppermute | solution.py:500
  11.3 4.8 %collective-permute-start.2 = (bf16[32,1024]{1,0:T(8,128)(2,1)S(1)}, bf16[32,1024]{1,0:T(8,128)(2,1)S(1)}, u32[]{:S(2)}, u32[]{:S(2)}) collective-permute-start(bf16[32,1024]{1,0:T(8,128)(2,1)S(1)} %get-tuple-element.53), channel_id=1, source_target_pairs={{17,0},{18,1},{19,2},{20,3},{21,4},{22,5},{23,6},{24,7},{25,8},{26... | collective-permute-start | bytes 196616 | tf_op jit(solution)/shard_map/ppermute | solution.py:502
  16.1 8.0 %inner.1 = (bf16[432,512]{1,0:T(8,128)(2,1)}, bf16[432,512]{1,0:T(8,128)(2,1)}, bf16[432,512]{1,0:T(8,128)(2,1)}, bf16[432,1536]{1,0:T(8,128)(2,1)}, f32[512,153...) custom-call(bf16[18,48,512]{2,1,0:T(8,128)(2,1)} %bitcast.18, ...), custom_call_target="tpu_custom_call" | custom-call | flops 4000000000 | bytes 8388608 | tf_op jit(solution)/shard_map/inner/pallas_call | solution.py:469
  24.2 8.2 %outer.1 = (bf16[432,512]{1,0:T(8,128)(2,1)}, bf16[432,512]{1,0:T(8,128)(2,1)}, bf16[432,512]{1,0:T(8,128)(2,1)}, bf16[432,1536]{1,0:T(8,128)(2,1)}, bf16[256,21...) custom-call(s32[2]{0:T(128)S(1)} %pad_add_fusion.where, bf16[96,1024]{1,0:T(8,128)(2,1)S(1)} %collective-permute-done.h_lon, ...), custom_call_target="tpu_custom_call" | custom-call | flops 4000000000 | bytes 8388608 | tf_op jit(solution)/shard_map/outer/pallas_call | solution.py:469
  32.7 2.7 %collective-permute-done.3.received = bf16[256,2176]{1,0:T(8,128)(2,1)S(1)} collective-permute-done((bf16[256,2176]{1,0:T(8,128)(2,1)S(1)}, bf16[256,2176]{1,0:T(8,128)(2,1)S(1)}, u32[]{:S(2)}, u32[]{:S(2)}) %collective-permute-start.3) | collective-permute-done | bytes 1114144 | tf_op jit(solution)/shard_map/ppermute | solution.py:484
  35.4 1.3 %add.13 = bf16[256,2176]{1,0:T(8,128)(2,1)} custom-call(bf16[256,2176]{1,0:T(8,128)(2,1)S(1)} %get-tuple-element.64.keep, bf16[256,2176]{1,0:T(8,128)(2,1)S(1)} %collective-permute-done.3.received), custom_call_target="tpu_custom_call" | custom-call | flops 100000 | bytes 8388608 | tf_op jit(solution)/shard_map/add/pallas_call | solution.py:469
  36.7 3.7 %all-to-all-start = ((bf16[16,16,2176]{2,1,0:T(8,128)(2,1)}), bf16[16,16,2176]{2,1,0:T(8,128)(2,1)S(1)}, u32[]{:S(2)}, u32[]{:S(2)}) async-start(bf16[16,16,2176]{2,1,0:T(8,128)(2,1)} %bitcast.6), calls=%async_computation | async-start | bytes 2228224 | tf_op jit(solution)/shard_map/all_to_all | solution.py:536
  40.4 6.3 %tokens.1 = (bf16[18,48,512]{2,1,0:T(8,128)(2,1)S(1)}, bf16[18,48,512]{2,1,0:T(8,128)(2,1)S(1)}, bf16[96,1024]{1,0:T(8,128)(2,1)S(1)}, bf16[128,1024]{1,0:T(8,128)(2,1)S(1)}, bf16[32,1024]{1,0:T(8,128)(2,1)S(1)}) custom-call(bf16[432,512]{1,0:T(8,128)(2,1)} %get-tuple-element.69.x1_h, bf16[432,512]{1,0:T(8,128)(2,1)} %get-tuple-element.70.g1_h, ...), custom_call_target="tpu_custom_call" | custom-call | flops 4000000000 | bytes 8388608 | tf_op jit(solution)/shard_map/tokens/pallas_call | solution.py:469
  46.7 1.6 %collective-permute-start.5 = (bf16[128,1024]{1,0:T(8,128)(2,1)S(1)}, bf16[128,1024]{1,0:T(8,128)(2,1)S(1)}, u32[]{:S(2)}, u32[]{:S(2)}) collective-permute-start(bf16[128,1024]{1,0:T(8,128)(2,1)S(1)} %get-tuple-element.78), channel_id=1, source_target_pairs={{0,1},{1,2},{2,3},{3,4},{4,5},{5,6},{6,7},{7,8},{8,9},{9,10},{10,1... | collective-permute-start | bytes 786440 | tf_op jit(solution)/shard_map/ppermute | solution.py:554
  48.3 1.4 %collective-permute-start.4 = (bf16[96,1024]{1,0:T(8,128)(2,1)S(1)}, bf16[96,1024]{1,0:T(8,128)(2,1)S(1)}, u32[]{:S(2)}, u32[]{:S(2)}) collective-permute-start(bf16[96,1024]{1,0:T(8,128)(2,1)S(1)} %get-tuple-element.77), channel_id=1, source_target_pairs={{0,16},{16,32},{32,48},{48,64},{64,80},{80,96},{96,112},{112,128},... | collective-permute-start | bytes 589832 | tf_op jit(solution)/shard_map/ppermute | solution.py:553
  49.7 12.3 %collective-permute-done.6.h_cor = bf16[32,1024]{1,0:T(8,128)(2,1)S(1)} collective-permute-done((bf16[32,1024]{1,0:T(8,128)(2,1)S(1)}, bf16[32,1024]{1,0:T(8,128)(2,1)S(1)}, u32[]{:S(2)}, u32[]{:S(2)}) %collective-permute-start.6) | collective-permute-done | bytes 65568 | tf_op jit(solution)/shard_map/ppermute | solution.py:555
  62.3 3.1 %collective-permute-done.7.received = bf16[16,2176]{1,0:T(8,128)(2,1)S(1)} collective-permute-done((bf16[16,2176]{1,0:T(8,128)(2,1)S(1)}, bf16[16,2176]{1,0:T(8,128)(2,1)S(1)}, u32[]{:S(2)}, u32[]{:S(2)}) %collective-permute-start.7) | collective-permute-done | bytes 69664 | tf_op jit(solution)/shard_map/ppermute | solution.py:484
  65.6 4.6 %collective-permute-done.8.received = bf16[16,2176]{1,0:T(8,128)(2,1)S(1)} collective-permute-done((bf16[16,2176]{1,0:T(8,128)(2,1)S(1)}, bf16[16,2176]{1,0:T(8,128)(2,1)S(1)}, u32[]{:S(2)}, u32[]{:S(2)}) %collective-permute-start.8) | collective-permute-done | bytes 69664 | tf_op jit(solution)/shard_map/ppermute | solution.py:484
  70.3 5.4 %collective-permute-done.9.received = bf16[16,2176]{1,0:T(8,128)(2,1)S(1)} collective-permute-done((bf16[16,2176]{1,0:T(8,128)(2,1)S(1)}, bf16[16,2176]{1,0:T(8,128)(2,1)S(1)}, u32[]{:S(2)}, u32[]{:S(2)}) %collective-permute-start.9) | collective-permute-done | bytes 69664 | tf_op jit(solution)/shard_map/ppermute | solution.py:484
  75.7 1.1 %spread.1 = (bf16[16,16,2048]{2,1,0:T(8,128)(2,1)}, f32[16,128]{1,0:T(8,128)S(1)}) custom-call(bf16[16,2176]{1,0:T(8,128)(2,1)S(1)} %add.15.piece, bf16[16,2176]{1,0:T(8,128)(2,1)S(1)} %collective-permute-done.9.received), custom_call_target="tpu_custom_call" | custom-call | flops 100000 | bytes 8388608 | tf_op jit(solution)/shard_map/spread/pallas_call | solution.py:469
  76.8 7.5 %all-to-all-start.1 = ((bf16[16,16,2048]{2,1,0:T(8,128)(2,1)}), bf16[16,16,2048]{2,1,0:T(8,128)(2,1)S(1)}, u32[]{:S(2)}, u32[]{:S(2)}) async-start(bf16[16,16,2048]{2,1,0:T(8,128)(2,1)} %get-tuple-element.81), calls=%async_computation.1 | async-start | bytes 2097152 | tf_op jit(solution)/shard_map/all_to_all | solution.py:565
  84.2 1.5 %restore.1 = (bf16[18,48,512]{2,1,0:T(8,128)(2,1)}, bf16[18,48,512]{2,1,0:T(8,128)(2,1)}) custom-call(bf16[18,48,512]{2,1,0:T(8,128)(2,1)S(1)} %get-tuple-element.82.mixed_c, bf16[18,48,512]{2,1,0:T(8,128)(2,1)S(1)} %get-tuple-element.83.tgrad_c, bf16[96,1024]{1,0:T(8,128)(2,1)S(1)} %collective-permute-done.4.h_lon, ...), custom_call_target="tpu_custom_call" | custom-call | flops 1000000 | bytes 8388608 | tf_op jit(solution)/shard_map/restore/pallas_call | solution.py:469
  85.7 12.8 %all-to-all-done.1 = bf16[16,16,2048]{2,1,0:T(8,128)(2,1)S(1)} async-done(((bf16[16,16,2048]{2,1,0:T(8,128)(2,1)}), bf16[16,16,2048]{2,1,0:T(8,128)(2,1)S(1)}, u32[]{:S(2)}, u32[]{:S(2)}) %all-to-all-start.1) | async-done | bytes 1048608 | tf_op jit(solution)/shard_map/all_to_all | solution.py:565
  98.5 4.2 %collective-permute-start.10 = (bf16[256,2048]{1,0:T(8,128)(2,1)S(1)}, bf16[256,2048]{1,0:T(8,128)(2,1)S(1)}, u32[]{:S(2)}, u32[]{:S(2)}) collective-permute-start(bf16[256,2048]{1,0:T(8,128)(2,1)S(1)} %bitcast.12), channel_id=1, source_target_pairs={{0,1},{1,0},{2,3},{3,2},{4,5},{5,4},{6,7},{7,6},{8,9},{9,8},{10,11... | collective-permute-start | bytes 3145736 | tf_op jit(solution)/shard_map/ppermute | solution.py:484
  102.8 0.6 bitcast_divide_fusion
  103.4 1.4 %place.2 = (f32[512,1536]{1,0:T(8,128)}, f32[512,512]{1,0:T(8,128)}) custom-call(s32[1]{0:T(128)} %bitcast.half, bf16[256,2048]{1,0:T(8,128)(2,1)S(1)} %bitcast.13), custom_call_target="tpu_custom_call" | custom-call | flops 1000000 | bytes 3145728 | tf_op jit(solution)/shard_map/place/pallas_call | solution.py:405
  105.1 1.4 %place.3 = (f32[512,1536]{1,0:T(8,128)}, f32[512,512]{1,0:T(8,128)}) custom-call(s32[1]{0:T(128)S(6)} %sub.3.half, bf16[256,2048]{1,0:T(8,128)(2,1)S(1)} %collective-permute-done.10.grads, f32[512,1536]{1,0:T(8,128)} %get-tuple-element.92.refs_0_, f32[512,512]{1,0:T(8,128)} %get-tuple-element.93.refs_1_), custom_call_target="tpu_custom_call", output_to_operand_aliasing={{0}: (2, {}), {1}: (3, {})} | custom-call | flops 1000000 | bytes 3145728 | tf_op jit(solution)/shard_map/place/pallas_call | solution.py:405
  (18 shorter events, 1.2 us)
Async XLA Ops:
  0.6 15.5 %copy-start = (f32[512]{0:T(512)S(1)}, f32[512]{0:T(512)}, u32[]{:S(2)}) copy-start(f32[512]{0:T(512)} %param.14) | copy-start | bytes 6148
  3.1 21.0 %collective-permute-start.1 = (bf16[128,1024]{1,0:T(8,128)(2,1)S(1)}, bf16[128,1024]{1,0:T(8,128)(2,1)S(1)}, u32[]{:S(2)}, u32[]{:S(2)}) collective-permute-start(bf16[128,1024]{1,0:T(8,128)(2,1)S(1)} %get-tuple-element.52), channel_id=1, source_target_pairs={{1,0},{2,1},{3,2},{4,3},{5,4},{6,5},{7,6},{8,7},{9,8},{10,9},{11,1... | collective-permute-start | bytes 786440 | tf_op jit(solution)/shard_map/ppermute | solution.py:501
  6.4 17.7 %collective-permute-start = (bf16[96,1024]{1,0:T(8,128)(2,1)S(1)}, bf16[96,1024]{1,0:T(8,128)(2,1)S(1)}, u32[]{:S(2)}, u32[]{:S(2)}) collective-permute-start(bf16[96,1024]{1,0:T(8,128)(2,1)S(1)} %get-tuple-element.51), channel_id=1, source_target_pairs={{16,0},{32,16},{48,32},{64,48},{80,64},{96,80},{112,96},{128,112},... | collective-permute-start | bytes 589832 | tf_op jit(solution)/shard_map/ppermute | solution.py:500
  11.3 12.8 %collective-permute-start.2 = (bf16[32,1024]{1,0:T(8,128)(2,1)S(1)}, bf16[32,1024]{1,0:T(8,128)(2,1)S(1)}, u32[]{:S(2)}, u32[]{:S(2)}) collective-permute-start(bf16[32,1024]{1,0:T(8,128)(2,1)S(1)} %get-tuple-element.53), channel_id=1, source_target_pairs={{17,0},{18,1},{19,2},{20,3},{21,4},{22,5},{23,6},{24,7},{25,8},{26... | collective-permute-start | bytes 196616 | tf_op jit(solution)/shard_map/ppermute | solution.py:502
  32.3 3.1 %collective-permute-start.3 = (bf16[256,2176]{1,0:T(8,128)(2,1)S(1)}, bf16[256,2176]{1,0:T(8,128)(2,1)S(1)}, u32[]{:S(2)}, u32[]{:S(2)}) collective-permute-start(bf16[256,2176]{1,0:T(8,128)(2,1)S(1)} %get-tuple-element.65), channel_id=1, source_target_pairs={{0,1},{1,0},{2,3},{3,2},{4,5},{5,4},{6,7},{7,6},{8,9},{9,8},{10,11... | collective-permute-start | bytes 3342344 | tf_op jit(solution)/shard_map/ppermute | solution.py:484
  36.7 25.4 %all-to-all-start = ((bf16[16,16,2176]{2,1,0:T(8,128)(2,1)}), bf16[16,16,2176]{2,1,0:T(8,128)(2,1)S(1)}, u32[]{:S(2)}, u32[]{:S(2)}) async-start(bf16[16,16,2176]{2,1,0:T(8,128)(2,1)} %bitcast.6), calls=%async_computation | async-start | bytes 2228224 | tf_op jit(solution)/shard_map/all_to_all | solution.py:536
  46.7 15.4 %collective-permute-start.5 = (bf16[128,1024]{1,0:T(8,128)(2,1)S(1)}, bf16[128,1024]{1,0:T(8,128)(2,1)S(1)}, u32[]{:S(2)}, u32[]{:S(2)}) collective-permute-start(bf16[128,1024]{1,0:T(8,128)(2,1)S(1)} %get-tuple-element.78), channel_id=1, source_target_pairs={{0,1},{1,2},{2,3},{3,4},{4,5},{5,6},{6,7},{7,8},{8,9},{9,10},{10,1... | collective-permute-start | bytes 786440 | tf_op jit(solution)/shard_map/ppermute | solution.py:554
  48.3 13.7 %collective-permute-start.4 = (bf16[96,1024]{1,0:T(8,128)(2,1)S(1)}, bf16[96,1024]{1,0:T(8,128)(2,1)S(1)}, u32[]{:S(2)}, u32[]{:S(2)}) collective-permute-start(bf16[96,1024]{1,0:T(8,128)(2,1)S(1)} %get-tuple-element.77), channel_id=1, source_target_pairs={{0,16},{16,32},{32,48},{48,64},{64,80},{80,96},{96,112},{112,128},... | collective-permute-start | bytes 589832 | tf_op jit(solution)/shard_map/ppermute | solution.py:553
  49.7 12.3 %collective-permute-start.6 = (bf16[32,1024]{1,0:T(8,128)(2,1)S(1)}, bf16[32,1024]{1,0:T(8,128)(2,1)S(1)}, u32[]{:S(2)}, u32[]{:S(2)}) collective-permute-start(bf16[32,1024]{1,0:T(8,128)(2,1)S(1)} %get-tuple-element.79), channel_id=1, source_target_pairs={{0,17},{1,18},{2,19},{3,20},{4,21},{5,22},{6,23},{7,24},{8,25},{9,... | collective-permute-start | bytes 196616 | tf_op jit(solution)/shard_map/ppermute | solution.py:555
  62.2 3.2 %collective-permute-start.7 = (bf16[16,2176]{1,0:T(8,128)(2,1)S(1)}, bf16[16,2176]{1,0:T(8,128)(2,1)S(1)}, u32[]{:S(2)}, u32[]{:S(2)}) collective-permute-start(bf16[16,2176]{1,0:T(8,128)(2,1)S(1)} %sum.1.keep), channel_id=1, source_target_pairs={{0,16},{16,0},{32,48},{48,32},{64,80},{80,64},{96,112},{112,96},{1... | collective-permute-start | bytes 208904 | tf_op jit(solution)/shard_map/ppermute | solution.py:484
  65.5 4.7 %collective-permute-start.8 = (bf16[16,2176]{1,0:T(8,128)(2,1)S(1)}, bf16[16,2176]{1,0:T(8,128)(2,1)S(1)}, u32[]{:S(2)}, u32[]{:S(2)}) collective-permute-start(bf16[16,2176]{1,0:T(8,128)(2,1)S(1)} %add.14.keep), channel_id=1, source_target_pairs={{0,32},{16,48},{32,0},{48,16},{64,96},{80,112},{96,64},{112,80},{1... | collective-permute-start | bytes 208904 | tf_op jit(solution)/shard_map/ppermute | solution.py:484
  70.2 5.5 %collective-permute-start.9 = (bf16[16,2176]{1,0:T(8,128)(2,1)S(1)}, bf16[16,2176]{1,0:T(8,128)(2,1)S(1)}, u32[]{:S(2)}, u32[]{:S(2)}) collective-permute-start(bf16[16,2176]{1,0:T(8,128)(2,1)S(1)} %add.15.piece), channel_id=1, source_target_pairs={{0,96},{16,112},{32,64},{48,80},{64,32},{80,48},{96,0},{112,16},{1... | collective-permute-start | bytes 208904 | tf_op jit(solution)/shard_map/ppermute | solution.py:484
  76.8 21.8 %all-to-all-start.1 = ((bf16[16,16,2048]{2,1,0:T(8,128)(2,1)}), bf16[16,16,2048]{2,1,0:T(8,128)(2,1)S(1)}, u32[]{:S(2)}, u32[]{:S(2)}) async-start(bf16[16,16,2048]{2,1,0:T(8,128)(2,1)} %get-tuple-element.81), calls=%async_computation.1 | async-start | bytes 2097152 | tf_op jit(solution)/shard_map/all_to_all | solution.py:565
  98.5 6.5 %collective-permute-start.10 = (bf16[256,2048]{1,0:T(8,128)(2,1)S(1)}, bf16[256,2048]{1,0:T(8,128)(2,1)S(1)}, u32[]{:S(2)}, u32[]{:S(2)}) collective-permute-start(bf16[256,2048]{1,0:T(8,128)(2,1)S(1)} %bitcast.12), channel_id=1, source_target_pairs={{0,1},{1,0},{2,3},{3,2},{4,5},{5,4},{6,7},{7,6},{8,9},{9,8},{10,11... | collective-permute-start | bytes 3145736 | tf_op jit(solution)/shard_map/ppermute | solution.py:484

commit v4 on v3

--- a/solution.py
+++ b/solution.py
@@ -21,14 +21,15 @@
 SLAB = WIN_LAT * ROWS_LON
 EDGE = 8
 HALF = 6 * WIN
+PIECES = 32
 LON_ROWS, LAT_ROWS, COR_ROWS = 96, 128, 32
 LON_IDS, LAT_IDS, COR_IDS = 90, 126, 18
 F32 = jnp.float32
 BF16 = jnp.bfloat16
 MIB = 1024 * 1024
 
-PLANE = ("y_lo", "y_hi", "x")
-LON_AXES = ("y_lo", "z")
+PLANE = ("y_lo", "z_lo", "y_hi", "x")
+LON_AXES = ("y_lo", "z_hi", "z_lo")
 LAT_AXES = ("y_hi", "x", "core")
 
 
@@ -154,11 +155,9 @@
     ).astype(BF16)
 
 
-def windows_pass(x_w, g_w, lab_w, gain, wqkv, wproj, att_b, dp_b, proj, gatt, onehot, att, dp, loads=()):
+def windows_pass(x_w, g_w, lab_w, gain, wqkv, wproj, att_b, dp_b, proj, gatt, onehot, att, dp):
     normed, _ = normalise(x_w[...].astype(F32))
     hidden = (normed * gain[...]).astype(BF16)
-    for load in loads:
-        load.wait()
     proj[...] = dot(hidden, wqkv[...])
     gatt[...] = dot_nt(g_w[...], wproj[...])
     lane = lax.broadcasted_iota(jnp.int32, (HALF, 128), 1).astype(F32)
@@ -209,19 +208,9 @@
 
 
 def first_kernel(
-    x_h, g_h, region_h, pick_h, wqkv_h, wproj_h, pick0_h, pick1_h, pick2_h, gain,
-    x_o, g_o, att_o, dp_o, gqkv, gproj, wqkv, wproj, pick0, pick1, pick2, strips, tails, region,
-    proj, gatt, onehot, att, dp, x_w, g_w, att_b, dp_b, out_sems, x, g, pick, sems,
+    x, g, wqkv, wproj, pick, region, gain, x_o, g_o, att_o, dp_o, gqkv, gproj,
+    proj, gatt, onehot, att, dp, x_w, g_w, att_b, dp_b, out_sems,
 ):
-    lats = pl.ds(SHIFT_LAT, 2 * WIN_LAT)
-    end = pl.ds(COLS_LAT - SHIFT_LAT, SHIFT_LAT)
-    own = [(region_h, region), (pick_h, pick), (x_h.at[lats], x), (g_h.at[lats], g), (wqkv_h, wqkv), (wproj_h, wproj)]
-    later = [(pick0_h, pick0), (pick1_h, pick1), (pick2_h, pick2)]
-    for at, ref in enumerate((x_h, g_h)):
-        later += [(ref.at[lats, pl.ds(32, 16), :], strips.at[at]), (ref.at[end], tails.at[at])]
-    loads = staged(own + later, sems)
-    for load in loads[:4]:
-        load.wait()
     ids = region[...].astype(F32)
     parts = {"r": []}
     for column in range(2):
@@ -237,16 +226,16 @@
     x_w[...] = parts["x"].astype(BF16)
     g_w[...] = parts["g"].astype(BF16)
     stores = staged([(x_w, x_o), (g_w, g_o)], out_sems.at[0])
-    hidden = windows_pass(x_w, g_w, parts["r"], gain, wqkv, wproj, att_b, dp_b, proj, gatt, onehot, att, dp, loads[4:6])
+    hidden = windows_pass(x_w, g_w, parts["r"], gain, wqkv, wproj, att_b, dp_b, proj, gatt, onehot, att, dp)
     stores += staged([(att_b, att_o), (dp_b, dp_o)], out_sems.at[1])
     gqkv[...] = dot_tn(hidden, dp_b[...])
     gproj[...] = dot_tn(att_b[...], g_w[...])
-    for copy in loads[6:] + stores:
-        copy.wait()
+    for store in stores:
+        store.wait()
 
 
 def second_kernel(
-    where, h_lon, h_lat, h_cor, gain, gqkv1, gproj1, wqkv, wproj, pick0, pick1, pick2, strips, tails, region,
+    where, h_lon, h_lat, h_cor, gain, gqkv1, gproj1, wqkv, wproj, pick0, pick1, pick2, ends, tails, region,
     x_o, g_o, att_o, dp_o, keep, send, proj, gatt, onehot, att, dp, x_w, g_w, att_b, dp_b, out_sems, total,
 ):
     parts = []
@@ -269,7 +258,7 @@
                 marks = region_marks(ids, range(SHIFT_LAT + first, SHIFT_LAT + first + WIN_LAT))
                 own = jnp.concatenate([marks[lat * ROWS_LON + 32 : (lat + 1) * ROWS_LON] for lat in range(WIN_LAT)], 0)
             else:
-                own = strips[array, first : first + WIN_LAT].reshape(WIN_LAT * 16, D)
+                own = ends[array, first : first + WIN_LAT].reshape(WIN_LAT * 16, D)
             got.append(dot(pick[...], jnp.concatenate([own, halo[0]], 0)))
         if array == 2:
             own = region_marks(ids, range(COLS_LAT - SHIFT_LAT, COLS_LAT))
@@ -296,9 +285,11 @@
     tile = jnp.concatenate(line + [jnp.zeros((12, 128), F32)], 0).astype(BF16)
     core = where[0]
     for ref, half in ((keep, core), (send, 1 - core)):
-        ref[:, pl.ds(0, 4 * D)] = total[pl.ds(pl.multiple_of(half * 256, 256), 256), :].astype(BF16)
-        for piece in range(16):
-            ref[pl.ds(piece * 16, 16), pl.ds(4 * D, 128)] = tile
+        rows = pl.ds(pl.multiple_of(half * 256, 256), 256)
+        for side in range(2):
+            ref[pl.ds(side * 256, 256), pl.ds(0, 2 * D)] = total[rows, pl.ds(side * 2 * D, 2 * D)].astype(BF16)
+        for piece in range(PIECES):
+            ref[pl.ds(piece * 16, 16), pl.ds(2 * D, 128)] = tile
     for store in stores:
         store.wait()
 
@@ -373,16 +364,16 @@
 
 def sum_kernel(pieces, out):
     total = pieces[0].astype(F32)
-    for piece in range(1, 16):
+    for piece in range(1, PIECES):
         total = total + pieces[piece].astype(F32)
     out[...] = total.astype(BF16)
 
 
 def spread_kernel(piece, received, copies, gain):
     total = (piece[...].astype(F32) + received[...].astype(F32)).astype(BF16)
-    gain[...] = total[:, 4 * D :].astype(F32)
-    for at in range(16):
-        copies[at] = total[:, : 4 * D]
+    gain[...] = total[:, 2 * D :].astype(F32)
+    for at in range(PIECES):
+        copies[at] = total[:, : 2 * D]
 
 
 def place_kernel(later, half, grads, *refs):
@@ -390,8 +381,10 @@
     copies = []
     for part in range(4):
         rows = pl.ds(part * 64, 64)
-        wide[rows, :] = grads[rows, pl.ds(0, 3 * D)].astype(F32)
-        square[rows, :] = grads[rows, pl.ds(3 * D, D)].astype(F32)
+        right = pl.ds(256 + part * 64, 64)
+        wide[rows, pl.ds(0, 2 * D)] = grads[rows, :].astype(F32)
+        wide[rows, pl.ds(2 * D, D)] = grads[right, pl.ds(0, D)].astype(F32)
+        square[rows, :] = grads[right, pl.ds(D, D)].astype(F32)
         there = pl.ds(pl.multiple_of(half[0] * 256 + part * 64, 64), 64)
         for at, (source, out) in enumerate(((wide, gqkv), (square, gproj))):
             copies.append(pltpu.make_async_copy(source.at[rows], out.at[there], sems.at[part, at]))
@@ -419,28 +412,40 @@
     )(half, grads, *filled)
 
 
-def edges_kernel(where, x_h, g_h, region_h, h_lon, h_lat, h_cor, strips, slabs, region, sems):
+def edges_kernel(
+    where, x_h, g_h, region_h, wqkv_h, wproj_h, pick_h, pick0_h, pick1_h, pick2_h,
+    h_lon, h_lat, h_cor, x, g, wqkv, wproj, pick, pick0, pick1, pick2, ends, tails, region, strips, slabs, sems,
+):
+    lats = pl.ds(SHIFT_LAT, 2 * WIN_LAT)
+    end = pl.ds(COLS_LAT - SHIFT_LAT, SHIFT_LAT)
     loads = [(region_h, region)]
     for at, ref in enumerate((x_h, g_h)):
         loads += [(ref.at[:, pl.ds(0, 2 * EDGE), :], strips.at[at]), (ref.at[pl.ds(0, SHIFT_LAT)], slabs.at[at])]
-    for load in staged(loads, sems):
+    loads += [(pick_h, pick), (x_h.at[lats], x), (g_h.at[lats], g), (wqkv_h, wqkv), (wproj_h, wproj)]
+    loads += [(pick0_h, pick0), (pick1_h, pick1), (pick2_h, pick2)]
+    for at, ref in enumerate((x_h, g_h)):
+        loads += [(ref.at[lats, pl.ds(32, 16), :], ends.at[at]), (ref.at[end], tails.at[at])]
+    loads = staged(loads, sems)
+    for load in loads[:5]:
         load.wait()
     ids = region[...].astype(F32)
     marks = region_marks(ids, range(COLS_LAT))
     strip = jnp.concatenate([marks[lat * ROWS_LON : lat * ROWS_LON + 2 * EDGE] for lat in range(COLS_LAT)], 0)
     width = COLS_LAT * 2 * EDGE
     slab = SHIFT_LAT * ROWS_LON
-    for out, rows, at, pick, source in (
+    for out, rows, at, chosen, source in (
         (h_lon, LON_ROWS, LON_IDS, rows_of((LON_ROWS, width), strip_row(SHIFT_LAT, 2 * EDGE)), strip),
         (h_lat, LAT_ROWS, LAT_IDS, rows_of((LAT_ROWS, slab), slab_row), marks[:slab]),
         (h_cor, COR_ROWS, COR_IDS, rows_of((COR_ROWS, width), strip_row(0, 2 * EDGE)), strip),
     ):
-        line = jnp.sum(jnp.where(diagonal(rows), dot(pick, source), 0.0), axis=0, keepdims=True)
+        line = jnp.sum(jnp.where(diagonal(rows), dot(chosen, source), 0.0), axis=0, keepdims=True)
         line = jnp.concatenate([line] * (D // 128), 1)
         here = lax.broadcasted_iota(jnp.int32, (rows, D), 0) == at
         for array in range(2):
             tokens = slabs[array].reshape(slab, D) if out is h_lat else strips[array].reshape(width, D)
-            out[:, pl.ds(array * D, D)] = jnp.where(here, line, dot(pick, tokens)).astype(BF16)
+            out[:, pl.ds(array * D, D)] = jnp.where(here, line, dot(chosen, tokens)).astype(BF16)
+    for load in loads[5:]:
+        load.wait()
 
 
 def pass_scratch():
@@ -489,51 +494,46 @@
     g = cotangent.transpose(1, 0, 2)
     edges = [((rows, 2 * D), BF16) for rows in (LON_ROWS, LAT_ROWS, COR_ROWS)]
     where = jnp.stack([lax.axis_index("core"), (lax.axis_index(LAT_AXES) == 15).astype(jnp.int32)]).astype(jnp.int32)
-    ids = region.T
+    constant = functools.partial(jnp.asarray, dtype=BF16)
+    picks = [inner_pick(), edge_pick(0), edge_pick(1), last_pick()]
+    weights = [((D, 3 * D), BF16), ((D, D), BF16)]
+    slab = ((2 * WIN_LAT, ROWS_LON, D), BF16)
+    loaded = [slab, slab] + weights + [(pick.shape, BF16) for pick in picks]
+    loaded += [((2, 2 * WIN_LAT, 16, D), BF16), ((2, SHIFT_LAT, ROWS_LON, D), BF16), ((COLS_LAT, ROWS_LON), jnp.int32)]
     scratch = [pltpu.VMEM((2, COLS_LAT, 2 * EDGE, D), BF16), pltpu.VMEM((2, SHIFT_LAT, ROWS_LON, D), BF16)]
-    scratch += [pltpu.VMEM((COLS_LAT, ROWS_LON), jnp.int32), pltpu.SemaphoreType.DMA((5,))]
-    e_lon, e_lat, e_cor = call(edges_kernel, edges, scratch, 10**6, "edges", 1, far=3, vmem=8)(where, x, g, ids)
+    scratch += [pltpu.SemaphoreType.DMA((17,))]
+    e_lon, e_lat, e_cor, x_s, g_s, wqkv_s, wproj_s, pick, pick0, pick1, pick2, ends, tails, ids = call(
+        edges_kernel, edges + loaded, scratch, 10**6, "edges", 1, far=9, vmem=12
+    )(where, x, g, region.T, w_qkv, w_proj, *[constant(pick) for pick in picks])
     lon_back = [((i + 1) % 16, i) for i in range(16)]
     lat_back = lon_back
     both_back = [(((i + 1) % 16) * 16 + (j + 1) % 16, i * 16 + j) for i in range(16) for j in range(16)]
-
     h_lon = lax.ppermute(e_lon, LON_AXES, lon_back)
     h_lat = lax.ppermute(e_lat, LAT_AXES, lat_back)
     h_cor = lax.ppermute(e_cor, LON_AXES + LAT_AXES, both_back)
 
     gain_row = gain.reshape(1, D)
     acts = [((HALF, D), BF16), ((HALF, D), BF16), ((HALF, D), BF16), ((HALF, 3 * D), BF16)]
-    constant = functools.partial(jnp.asarray, dtype=BF16)
-    weights = [((D, 3 * D), BF16), ((D, D), BF16)]
-    picks = [inner_pick(), edge_pick(0), edge_pick(1), last_pick()]
-    passed = [((D, 3 * D), F32), ((D, D), F32)] + weights + [(pick.shape, BF16) for pick in picks[1:]]
-    passed += [((2, 2 * WIN_LAT, 16, D), BF16), ((2, SHIFT_LAT, ROWS_LON, D), BF16), ((COLS_LAT, ROWS_LON), jnp.int32)]
-    slabs = [pltpu.VMEM((2 * WIN_LAT, ROWS_LON, D), BF16)] * 2 + [pltpu.VMEM((3 * WIN, SLAB), BF16)]
-    picks = [constant(pick) for pick in picks]
-    x1, g1, att1, dp1, *passed = call(
-        first_kernel,
-        acts + passed,
-        pass_scratch() + slabs + [pltpu.SemaphoreType.DMA((13,))],
-        4 * 10**9,
-        "inner",
-        far=9,
-        kept=4,
-    )(x, g, ids, picks[0], w_qkv, w_proj, *picks[1:], gain_row)
-
-    width = 4 * D + 128
+    x1, g1, att1, dp1, gqkv1, gproj1 = call(
+        first_kernel, acts + [((D, 3 * D), F32), ((D, D), F32)], pass_scratch(), 4 * 10**9, "inner", kept=4
+    )(x_s, g_s, wqkv_s, wproj_s, pick, ids, gain_row)
+
+    width = 2 * D + 128
     x2, g2, att2, dp2, keep, send = call(
         second_kernel,
-        acts + [((256, width), BF16), ((256, width), BF16)],
+        acts + [((16 * PIECES, width), BF16)] * 2,
         pass_scratch() + [pltpu.VMEM((D, 4 * D), F32)],
         4 * 10**9,
         "outer",
         1,
         kept=4,
-    )(where, h_lon, h_lat, h_cor, gain_row, *passed)
-
-    (mine,) = call(add_kernel, [((256, width), BF16)], [], 10**5, "add", vmem=8)(keep, swapped(send, "core", 2, 1))
+    )(
+        where, h_lon, h_lat, h_cor, gain_row, gqkv1, gproj1, wqkv_s, wproj_s, pick0, pick1, pick2, ends, tails, ids
+    )
+
+    (mine,) = call(add_kernel, [((16 * PIECES, width), BF16)], [], 10**5, "add", vmem=8)(keep, swapped(send, "core", 2, 1))
     mine, x1, x2 = lax.optimization_barrier((mine, x1, x2))
-    pieces = lax.all_to_all(mine.reshape(16, 16, -1), PLANE, 0, 0, tiled=True)
+    pieces = lax.all_to_all(mine.reshape(PIECES, 16, -1), PLANE, 0, 0, tiled=True)
     mixed_c, tgrad_c, s_lon, s_lat, s_cor = call(
         third_kernel,
         [((COLS_LAT, ROWS_LON, D), BF16)] * 2
@@ -556,18 +556,17 @@
 
     pieces, t_lon, t_lat, t_cor = lax.optimization_barrier((pieces, t_lon, t_lat, t_cor))
     (piece,) = call(sum_kernel, [((16, width), BF16)], [], 10**5, "sum", vmem=8)(pieces)
-    for bit in (1, 2):
-        (piece,) = call(add_kernel, [((16, width), BF16)], [], 10**5, "add", vmem=4)(piece, swapped(piece, "z", 8, bit))
-    copies, gain_tile = call(spread_kernel, [((16, 16, 4 * D), BF16), ((16, 128), F32)], [], 10**5, "spread", vmem=8)(
-        piece, swapped(piece, "z", 8, 6)
-    )
+    (piece,) = call(add_kernel, [((16, width), BF16)], [], 10**5, "add", vmem=4)(piece, swapped(piece, "z_hi", 4, 1))
+    copies, gain_tile = call(
+        spread_kernel, [((PIECES, 16, 2 * D), BF16), ((16, 128), F32)], [], 10**5, "spread", vmem=8
+    )(piece, swapped(piece, "z_hi", 4, 3))
     gain_grad = gain_tile[:4].reshape(D) / gain
     grads = lax.all_to_all(copies, PLANE, 0, 0, tiled=True)
     mixed, tokens_grad = call(restore_kernel, [((COLS_LAT, ROWS_LON, D), BF16)] * 2, [], 10**6, "restore", vmem=10)(
         mixed_c, tgrad_c, t_lon, t_lat, t_cor
     )
     grads, mixed, tokens_grad = lax.optimization_barrier((grads, mixed, tokens_grad))
-    grads = grads.reshape(256, 4 * D)
+    grads = grads.reshape(16 * PIECES, 2 * D)
     other = swapped(grads, "core", 2, 1)
     core = where[:1]
     qkv_grad, proj_grad = place(1 - core, other, *place(core, grads))
@@ -576,7 +575,7 @@
 
 
 def solution(mesh):
-    fine = Mesh(mesh.devices.reshape(2, 8, 2, 4, 2), ("y_lo", "z", "y_hi", "x", "core"))
+    fine = Mesh(mesh.devices.reshape(2, 4, 2, 2, 4, 2), ("y_lo", "z_hi", "z_lo", "y_hi", "x", "core"))
     grid = P(LON_AXES, LAT_AXES, None)
     return jax.shard_map(
         body,

time: 107 us -> 101 us (0.944)
  waiting for transfers between devices: 41.3 us -> 38.6 us
  starting transfers between devices: 32 us -> 29.4 us
    ppermute x5 -> x4, waiting for transfers between devices: 16.2 us -> 11.7 us  [swapped(): return lax.ppermute(block, axis, [(i, i ^ bit) for i in range(size)])]
    all_to_all x1, starting transfers between devices: 7.46 us -> 4.01 us  [body(): grads = lax.all_to_all(copies, PLANE, 0, 0, tiled=True)]
    ppermute x1, waiting for transfers between devices: 12.3 us -> 15.4 us  [body(): t_cor = lax.ppermute(s_cor, LON_AXES + LAT_AXES, both_on)]
    all_to_all x1, waiting for transfers between devices: 12.8 us -> 11.4 us  [body(): grads = lax.all_to_all(copies, PLANE, 0, 0, tiled=True)]
    ppermute x5 -> x4, starting transfers between devices: 4.84 us -> 5.59 us  [swapped(): return lax.ppermute(block, axis, [(i, i ^ bit) for i in range(size)])]
    pallas_call x10 -> x9, Pallas kernels: 28.9 us -> 28.7 us  [run(): pl.pallas_call(kernel, out_shape=[pltpu.HBM(*out) if at < kept else jax.S...]
  transfers between devices with their start and end apart: 13 -> 12, of which waited for: 7 -> 7; matrix products, arithmetic and copies ran while one was open for 1% -> 1% of each run, Pallas kernels for 16% -> 16%
where the time goes in v4:
time: 101 us
  waiting for transfers between devices  38.6 us (38%)
  Pallas kernels  31.5 us (31%)
  starting transfers between devices  29.4 us (29%)
    pallas_call x9, Pallas kernels, run(): pl.pallas_call(kernel, out_shape=[pltpu.HBM(*out) if at < kept else jax.S...  28.7 us
    ppermute x1, waiting for transfers between devices, body(): t_cor = lax.ppermute(s_cor, LON_AXES + LAT_AXES, both_on)  15.4 us
    ppermute x4, waiting for transfers between devices, swapped(): return lax.ppermute(block, axis, [(i, i ^ bit) for i in range(size)])  11.7 us
    all_to_all x1, waiting for transfers between devices, body(): grads = lax.all_to_all(copies, PLANE, 0, 0, tiled=True)  11.4 us
    ppermute x4, starting transfers between devices, swapped(): return lax.ppermute(block, axis, [(i, i ^ bit) for i in range(size)])  5.59 us
    ppermute x1, starting transfers between devices, body(): h_lon = lax.ppermute(e_lon, LON_AXES, lon_back)  4.85 us
    ppermute x1, starting transfers between devices, body(): h_cor = lax.ppermute(e_cor, LON_AXES + LAT_AXES, both_back)  4.82 us
    all_to_all x1, starting transfers between devices, body(): grads = lax.all_to_all(copies, PLANE, 0, 0, tiled=True)  4.01 us
  transfers between devices with their start and end apart: 12, of which 7 were waited for; matrix products, arithmetic and copies ran while one was open for 1% of the time, Pallas kernels for 16%

profile of v4, /device:TPU:1, one launch (start us, length us, event | category | flops | bytes accessed | tf_op | source)
XLA Modules:
  0.0 101.1 jit_solution(18294874945288566596)
XLA Ops:
  0.7 3.2 %edges.1 = (bf16[96,1024]{1,0:T(8,128)(2,1)S(1)}, bf16[128,1024]{1,0:T(8,128)(2,1)S(1)}, bf16[32,1024]{1,0:T(8,128)(2,1)S(1)}, bf16[12,48,512]{2,1,0:T(8,128)(2,...) custom-call(s32[2]{0:T(128)S(1)} %pad_add_fusion.where, ...), custom_call_target="tpu_custom_call" | custom-call | flops 1000000 | bytes 8388608 | tf_op jit(solution)/shard_map/edges/pallas_call | solution.py:474
  3.9 3.3 %collective-permute-start.1 = (bf16[128,1024]{1,0:T(8,128)(2,1)S(1)}, bf16[128,1024]{1,0:T(8,128)(2,1)S(1)}, u32[]{:S(2)}, u32[]{:S(2)}) collective-permute-start(bf16[128,1024]{1,0:T(8,128)(2,1)S(1)} %get-tuple-element.55), channel_id=1, source_target_pairs={{1,0},{2,1},{3,2},{4,3},{5,4},{6,5},{7,6},{8,7},{9,8},{10,9},{11,1... | collective-permute-start | bytes 786440 | tf_op jit(solution)/shard_map/ppermute | solution.py:512
  7.3 4.9 %collective-permute-start = (bf16[96,1024]{1,0:T(8,128)(2,1)S(1)}, bf16[96,1024]{1,0:T(8,128)(2,1)S(1)}, u32[]{:S(2)}, u32[]{:S(2)}) collective-permute-start(bf16[96,1024]{1,0:T(8,128)(2,1)S(1)} %get-tuple-element.54), channel_id=1, source_target_pairs={{16,0},{32,16},{48,32},{64,48},{80,64},{96,80},{112,96},{128,112},... | collective-permute-start | bytes 589832 | tf_op jit(solution)/shard_map/ppermute | solution.py:511
  12.1 4.8 %collective-permute-start.2 = (bf16[32,1024]{1,0:T(8,128)(2,1)S(1)}, bf16[32,1024]{1,0:T(8,128)(2,1)S(1)}, u32[]{:S(2)}, u32[]{:S(2)}) collective-permute-start(bf16[32,1024]{1,0:T(8,128)(2,1)S(1)} %get-tuple-element.56), channel_id=1, source_target_pairs={{17,0},{18,1},{19,2},{20,3},{21,4},{22,5},{23,6},{24,7},{25,8},{26... | collective-permute-start | bytes 196616 | tf_op jit(solution)/shard_map/ppermute | solution.py:513
  16.9 7.2 %inner.1 = (bf16[432,512]{1,0:T(8,128)(2,1)}, bf16[432,512]{1,0:T(8,128)(2,1)}, bf16[432,512]{1,0:T(8,128)(2,1)}, bf16[432,1536]{1,0:T(8,128)(2,1)}, f32[512,1536]{1,0:T(8,128)S(1)}, /*index=5*/f32[512,512]{1,0:T(8,128)S(1)}) custom-call(bf16[12,48,512]{2,1,0:T(8,128)(2,1)S(1)} %get-tuple-element.57.x, bf16[12,48,512]{2,1,0:T(8,128)(2,1)S(1)} %get-tuple-element.58.g, ...), custom_call_target="tpu_custom_call" | custom-call | flops 4000000000 | bytes 8388608 | tf_op jit(solution)/shard_map/inner/pallas_call | solution.py:474
  24.2 7.8 %outer.1 = (bf16[432,512]{1,0:T(8,128)(2,1)}, bf16[432,512]{1,0:T(8,128)(2,1)}, bf16[432,512]{1,0:T(8,128)(2,1)}, bf16[432,1536]{1,0:T(8,128)(2,1)}, bf16[512,11...) custom-call(s32[2]{0:T(128)S(1)} %pad_add_fusion.where, bf16[96,1024]{1,0:T(8,128)(2,1)S(1)} %collective-permute-done.h_lon, ...), custom_call_target="tpu_custom_call" | custom-call | flops 4000000000 | bytes 8388608 | tf_op jit(solution)/shard_map/outer/pallas_call | solution.py:474
  32.1 0.3 collective-permute-start.3
  32.4 2.8 %collective-permute-done.3.received = bf16[512,1152]{1,0:T(8,128)(2,1)S(1)} collective-permute-done((bf16[512,1152]{1,0:T(8,128)(2,1)S(1)}, bf16[512,1152]{1,0:T(8,128)(2,1)S(1)}, u32[]{:S(2)}, u32[]{:S(2)}) %collective-permute-start.3) | collective-permute-done | bytes 1179680 | tf_op jit(solution)/shard_map/ppermute | solution.py:489
  35.2 1.3 %add.12 = bf16[512,1152]{1,0:T(8,128)(2,1)} custom-call(bf16[512,1152]{1,0:T(8,128)(2,1)S(1)} %get-tuple-element.70.keep, bf16[512,1152]{1,0:T(8,128)(2,1)S(1)} %collective-permute-done.3.received), custom_call_target="tpu_custom_call" | custom-call | flops 100000 | bytes 8388608 | tf_op jit(solution)/shard_map/add/pallas_call | solution.py:474
  36.5 3.9 %all-to-all-start = ((bf16[32,16,1152]{2,1,0:T(8,128)(2,1)}), bf16[32,16,1152]{2,1,0:T(8,128)(2,1)S(1)}, u32[]{:S(2)}, u32[]{:S(2)}) async-start(bf16[32,16,1152]{2,1,0:T(8,128)(2,1)} %bitcast.6), calls=%async_computation | async-start | bytes 2359296 | tf_op jit(solution)/shard_map/all_to_all | solution.py:536
  40.5 6.3 %tokens.1 = (bf16[18,48,512]{2,1,0:T(8,128)(2,1)S(1)}, bf16[18,48,512]{2,1,0:T(8,128)(2,1)S(1)}, bf16[96,1024]{1,0:T(8,128)(2,1)S(1)}, bf16[128,1024]{1,0:T(8,128)(2,1)S(1)}, bf16[32,1024]{1,0:T(8,128)(2,1)S(1)}) custom-call(bf16[432,512]{1,0:T(8,128)(2,1)} %get-tuple-element.75.x1_h, bf16[432,512]{1,0:T(8,128)(2,1)} %get-tuple-element.76.g1_h, ...), custom_call_target="tpu_custom_call" | custom-call | flops 4000000000 | bytes 8388608 | tf_op jit(solution)/shard_map/tokens/pallas_call | solution.py:474
  46.8 1.6 %collective-permute-start.5 = (bf16[128,1024]{1,0:T(8,128)(2,1)S(1)}, bf16[128,1024]{1,0:T(8,128)(2,1)S(1)}, u32[]{:S(2)}, u32[]{:S(2)}) collective-permute-start(bf16[128,1024]{1,0:T(8,128)(2,1)S(1)} %get-tuple-element.84), channel_id=1, source_target_pairs={{0,1},{1,2},{2,3},{3,4},{4,5},{5,6},{6,7},{7,8},{8,9},{9,10},{10,1... | collective-permute-start | bytes 786440 | tf_op jit(solution)/shard_map/ppermute | solution.py:554
  48.4 1.2 %collective-permute-start.4 = (bf16[96,1024]{1,0:T(8,128)(2,1)S(1)}, bf16[96,1024]{1,0:T(8,128)(2,1)S(1)}, u32[]{:S(2)}, u32[]{:S(2)}) collective-permute-start(bf16[96,1024]{1,0:T(8,128)(2,1)S(1)} %get-tuple-element.83), channel_id=1, source_target_pairs={{0,16},{16,32},{32,48},{48,64},{64,80},{80,96},{96,112},{112,128},... | collective-permute-start | bytes 589832 | tf_op jit(solution)/shard_map/ppermute | solution.py:553
  49.6 15.4 %collective-permute-done.6.h_cor = bf16[32,1024]{1,0:T(8,128)(2,1)S(1)} collective-permute-done((bf16[32,1024]{1,0:T(8,128)(2,1)S(1)}, bf16[32,1024]{1,0:T(8,128)(2,1)S(1)}, u32[]{:S(2)}, u32[]{:S(2)}) %collective-permute-start.6) | collective-permute-done | bytes 65568 | tf_op jit(solution)/shard_map/ppermute | solution.py:555
  65.4 3.7 %collective-permute-done.7.received = bf16[16,1152]{1,0:T(8,128)(2,1)S(1)} collective-permute-done((bf16[16,1152]{1,0:T(8,128)(2,1)S(1)}, bf16[16,1152]{1,0:T(8,128)(2,1)S(1)}, u32[]{:S(2)}, u32[]{:S(2)}) %collective-permute-start.7) | collective-permute-done | bytes 36896 | tf_op jit(solution)/shard_map/ppermute | solution.py:489
  69.2 4.9 %collective-permute-done.8.received = bf16[16,1152]{1,0:T(8,128)(2,1)S(1)} collective-permute-done((bf16[16,1152]{1,0:T(8,128)(2,1)S(1)}, bf16[16,1152]{1,0:T(8,128)(2,1)S(1)}, u32[]{:S(2)}, u32[]{:S(2)}) %collective-permute-start.8) | collective-permute-done | bytes 36896 | tf_op jit(solution)/shard_map/ppermute | solution.py:489
  74.1 1.1 %spread.1 = (bf16[32,16,1024]{2,1,0:T(8,128)(2,1)}, f32[16,128]{1,0:T(8,128)S(1)}) custom-call(bf16[16,1152]{1,0:T(8,128)(2,1)S(1)} %add.13.piece, bf16[16,1152]{1,0:T(8,128)(2,1)S(1)} %collective-permute-done.8.received), custom_call_target="tpu_custom_call" | custom-call | flops 100000 | bytes 8388608 | tf_op jit(solution)/shard_map/spread/pallas_call | solution.py:474
  75.2 4.0 %all-to-all-start.1 = ((bf16[32,16,1024]{2,1,0:T(8,128)(2,1)}), bf16[32,16,1024]{2,1,0:T(8,128)(2,1)S(1)}, u32[]{:S(2)}, u32[]{:S(2)}) async-start(bf16[32,16,1024]{2,1,0:T(8,128)(2,1)} %get-tuple-element.87), calls=%async_computation.1 | async-start | bytes 2097152 | tf_op jit(solution)/shard_map/all_to_all | solution.py:564
  79.2 1.5 %restore.1 = (bf16[18,48,512]{2,1,0:T(8,128)(2,1)}, bf16[18,48,512]{2,1,0:T(8,128)(2,1)}) custom-call(bf16[18,48,512]{2,1,0:T(8,128)(2,1)S(1)} %get-tuple-element.88.mixed_c, bf16[18,48,512]{2,1,0:T(8,128)(2,1)S(1)} %get-tuple-element.89.tgrad_c, bf16[96,1024]{1,0:T(8,128)(2,1)S(1)} %collective-permute-done.4.h_lon, ...), custom_call_target="tpu_custom_call" | custom-call | flops 1000000 | bytes 8388608 | tf_op jit(solution)/shard_map/restore/pallas_call | solution.py:474
  80.8 11.4 %all-to-all-done.1 = bf16[32,16,1024]{2,1,0:T(8,128)(2,1)S(1)} async-done(((bf16[32,16,1024]{2,1,0:T(8,128)(2,1)}), bf16[32,16,1024]{2,1,0:T(8,128)(2,1)S(1)}, u32[]{:S(2)}, u32[]{:S(2)}) %all-to-all-start.1) | async-done | bytes 1048608 | tf_op jit(solution)/shard_map/all_to_all | solution.py:564
  92.1 5.1 %collective-permute-start.9 = (bf16[512,1024]{1,0:T(8,128)(2,1)S(1)}, bf16[512,1024]{1,0:T(8,128)(2,1)S(1)}, u32[]{:S(2)}, u32[]{:S(2)}) collective-permute-start(bf16[512,1024]{1,0:T(8,128)(2,1)S(1)} %bitcast.12), channel_id=1, source_target_pairs={{0,1},{1,0},{2,3},{3,2},{4,5},{5,4},{6,7},{7,6},{8,9},{9,8},{10,11... | collective-permute-start | bytes 3145736 | tf_op jit(solution)/shard_map/ppermute | solution.py:489
  97.2 0.6 bitcast_divide_fusion
  97.8 1.4 %place.2 = (f32[512,1536]{1,0:T(8,128)}, f32[512,512]{1,0:T(8,128)}) custom-call(s32[1]{0:T(128)} %bitcast.half, bf16[512,1024]{1,0:T(8,128)(2,1)S(1)} %bitcast.13), custom_call_target="tpu_custom_call" | custom-call | flops 1000000 | bytes 3145728 | tf_op jit(solution)/shard_map/place/pallas_call | solution.py:398
  99.5 1.4 %place.3 = (f32[512,1536]{1,0:T(8,128)}, f32[512,512]{1,0:T(8,128)}) custom-call(s32[1]{0:T(128)S(6)} %sub.3.half, bf16[512,1024]{1,0:T(8,128)(2,1)S(1)} %collective-permute-done.9.grads, f32[512,1536]{1,0:T(8,128)} %get-tuple-element.98.refs_0_, f32[512,512]{1,0:T(8,128)} %get-tuple-element.99.refs_1_), custom_call_target="tpu_custom_call", output_to_operand_aliasing={{0}: (2, {}), {1}: (3, {})} | custom-call | flops 1000000 | bytes 3145728 | tf_op jit(solution)/shard_map/place/pallas_call | solution.py:398
  (15 shorter events, 0.8 us)
Async XLA Ops:
  0.7 16.2 %copy-start = (f32[512]{0:T(512)S(1)}, f32[512]{0:T(512)}, u32[]{:S(2)}) copy-start(f32[512]{0:T(512)} %param.14) | copy-start | bytes 6148
  3.9 20.2 %collective-permute-start.1 = (bf16[128,1024]{1,0:T(8,128)(2,1)S(1)}, bf16[128,1024]{1,0:T(8,128)(2,1)S(1)}, u32[]{:S(2)}, u32[]{:S(2)}) collective-permute-start(bf16[128,1024]{1,0:T(8,128)(2,1)S(1)} %get-tuple-element.55), channel_id=1, source_target_pairs={{1,0},{2,1},{3,2},{4,3},{5,4},{6,5},{7,6},{8,7},{9,8},{10,9},{11,1... | collective-permute-start | bytes 786440 | tf_op jit(solution)/shard_map/ppermute | solution.py:512
  7.3 16.9 %collective-permute-start = (bf16[96,1024]{1,0:T(8,128)(2,1)S(1)}, bf16[96,1024]{1,0:T(8,128)(2,1)S(1)}, u32[]{:S(2)}, u32[]{:S(2)}) collective-permute-start(bf16[96,1024]{1,0:T(8,128)(2,1)S(1)} %get-tuple-element.54), channel_id=1, source_target_pairs={{16,0},{32,16},{48,32},{64,48},{80,64},{96,80},{112,96},{128,112},... | collective-permute-start | bytes 589832 | tf_op jit(solution)/shard_map/ppermute | solution.py:511
  12.1 12.1 %collective-permute-start.2 = (bf16[32,1024]{1,0:T(8,128)(2,1)S(1)}, bf16[32,1024]{1,0:T(8,128)(2,1)S(1)}, u32[]{:S(2)}, u32[]{:S(2)}) collective-permute-start(bf16[32,1024]{1,0:T(8,128)(2,1)S(1)} %get-tuple-element.56), channel_id=1, source_target_pairs={{17,0},{18,1},{19,2},{20,3},{21,4},{22,5},{23,6},{24,7},{25,8},{26... | collective-permute-start | bytes 196616 | tf_op jit(solution)/shard_map/ppermute | solution.py:513
  32.1 3.2 %collective-permute-start.3 = (bf16[512,1152]{1,0:T(8,128)(2,1)S(1)}, bf16[512,1152]{1,0:T(8,128)(2,1)S(1)}, u32[]{:S(2)}, u32[]{:S(2)}) collective-permute-start(bf16[512,1152]{1,0:T(8,128)(2,1)S(1)} %get-tuple-element.71), channel_id=1, source_target_pairs={{0,1},{1,0},{2,3},{3,2},{4,5},{5,4},{6,7},{7,6},{8,9},{9,8},{10,11... | collective-permute-start | bytes 3538952 | tf_op jit(solution)/shard_map/ppermute | solution.py:489
  36.5 28.6 %all-to-all-start = ((bf16[32,16,1152]{2,1,0:T(8,128)(2,1)}), bf16[32,16,1152]{2,1,0:T(8,128)(2,1)S(1)}, u32[]{:S(2)}, u32[]{:S(2)}) async-start(bf16[32,16,1152]{2,1,0:T(8,128)(2,1)} %bitcast.6), calls=%async_computation | async-start | bytes 2359296 | tf_op jit(solution)/shard_map/all_to_all | solution.py:536
  46.8 18.4 %collective-permute-start.5 = (bf16[128,1024]{1,0:T(8,128)(2,1)S(1)}, bf16[128,1024]{1,0:T(8,128)(2,1)S(1)}, u32[]{:S(2)}, u32[]{:S(2)}) collective-permute-start(bf16[128,1024]{1,0:T(8,128)(2,1)S(1)} %get-tuple-element.84), channel_id=1, source_target_pairs={{0,1},{1,2},{2,3},{3,4},{4,5},{5,6},{6,7},{7,8},{8,9},{9,10},{10,1... | collective-permute-start | bytes 786440 | tf_op jit(solution)/shard_map/ppermute | solution.py:554
  48.4 16.7 %collective-permute-start.4 = (bf16[96,1024]{1,0:T(8,128)(2,1)S(1)}, bf16[96,1024]{1,0:T(8,128)(2,1)S(1)}, u32[]{:S(2)}, u32[]{:S(2)}) collective-permute-start(bf16[96,1024]{1,0:T(8,128)(2,1)S(1)} %get-tuple-element.83), channel_id=1, source_target_pairs={{0,16},{16,32},{32,48},{48,64},{64,80},{80,96},{96,112},{112,128},... | collective-permute-start | bytes 589832 | tf_op jit(solution)/shard_map/ppermute | solution.py:553
  49.6 15.4 %collective-permute-start.6 = (bf16[32,1024]{1,0:T(8,128)(2,1)S(1)}, bf16[32,1024]{1,0:T(8,128)(2,1)S(1)}, u32[]{:S(2)}, u32[]{:S(2)}) collective-permute-start(bf16[32,1024]{1,0:T(8,128)(2,1)S(1)} %get-tuple-element.85), channel_id=1, source_target_pairs={{0,17},{1,18},{2,19},{3,20},{4,21},{5,22},{6,23},{7,24},{8,25},{9,... | collective-permute-start | bytes 196616 | tf_op jit(solution)/shard_map/ppermute | solution.py:555
  65.3 3.8 %collective-permute-start.7 = (bf16[16,1152]{1,0:T(8,128)(2,1)S(1)}, bf16[16,1152]{1,0:T(8,128)(2,1)S(1)}, u32[]{:S(2)}, u32[]{:S(2)}) collective-permute-start(bf16[16,1152]{1,0:T(8,128)(2,1)S(1)} %sum.1.keep), channel_id=1, source_target_pairs={{0,32},{32,0},{64,96},{96,64},{1,33},{33,1},{65,97},{97,65},{2,34}... | collective-permute-start | bytes 110600 | tf_op jit(solution)/shard_map/ppermute | solution.py:489
  69.1 5.0 %collective-permute-start.8 = (bf16[16,1152]{1,0:T(8,128)(2,1)S(1)}, bf16[16,1152]{1,0:T(8,128)(2,1)S(1)}, u32[]{:S(2)}, u32[]{:S(2)}) collective-permute-start(bf16[16,1152]{1,0:T(8,128)(2,1)S(1)} %add.13.piece), channel_id=1, source_target_pairs={{0,96},{32,64},{64,32},{96,0},{1,97},{33,65},{65,33},{97,1},{2,98}... | collective-permute-start | bytes 110600 | tf_op jit(solution)/shard_map/ppermute | solution.py:489
  75.2 16.9 %all-to-all-start.1 = ((bf16[32,16,1024]{2,1,0:T(8,128)(2,1)}), bf16[32,16,1024]{2,1,0:T(8,128)(2,1)S(1)}, u32[]{:S(2)}, u32[]{:S(2)}) async-start(bf16[32,16,1024]{2,1,0:T(8,128)(2,1)} %get-tuple-element.87), calls=%async_computation.1 | async-start | bytes 2097152 | tf_op jit(solution)/shard_map/all_to_all | solution.py:564
  92.1 7.4 %collective-permute-start.9 = (bf16[512,1024]{1,0:T(8,128)(2,1)S(1)}, bf16[512,1024]{1,0:T(8,128)(2,1)S(1)}, u32[]{:S(2)}, u32[]{:S(2)}) collective-permute-start(bf16[512,1024]{1,0:T(8,128)(2,1)S(1)} %bitcast.12), channel_id=1, source_target_pairs={{0,1},{1,0},{2,3},{3,2},{4,5},{5,4},{6,7},{7,6},{8,9},{9,8},{10,11... | collective-permute-start | bytes 3145736 | tf_op jit(solution)/shard_map/ppermute | solution.py:489

commit v5 on v4

--- a/solution.py
+++ b/solution.py
@@ -155,7 +155,9 @@
     ).astype(BF16)
 
 
-def windows_pass(x_w, g_w, lab_w, gain, wqkv, wproj, att_b, dp_b, proj, gatt, onehot, att, dp):
+def windows_pass(
+    x_w, g_w, lab_w, gain, wqkv, wproj, att_o, dp_o, att_b, dp_b, stores, out_sems, proj, gatt, onehot, att, dp
+):
     normed, _ = normalise(x_w[...].astype(F32))
     hidden = (normed * gain[...]).astype(BF16)
     proj[...] = dot(hidden, wqkv[...])
@@ -202,8 +204,12 @@
 
     for window in range(6):
         one_window(window)
-    att_b[...] = att[...].astype(BF16)
-    dp_b[...] = dp[...].astype(BF16)
+        if window % 2:
+            rows = pl.ds((window - 1) * WIN, 2 * WIN)
+            att_b[rows, :] = att[rows, :].astype(BF16)
+            dp_b[rows, :] = dp[rows, :].astype(BF16)
+            pairs = [(att_b.at[rows], att_o.at[rows]), (dp_b.at[rows], dp_o.at[rows])]
+            stores.extend(staged(pairs, out_sems.at[1 + window // 2]))
     return hidden
 
 
@@ -226,8 +232,9 @@
     x_w[...] = parts["x"].astype(BF16)
     g_w[...] = parts["g"].astype(BF16)
     stores = staged([(x_w, x_o), (g_w, g_o)], out_sems.at[0])
-    hidden = windows_pass(x_w, g_w, parts["r"], gain, wqkv, wproj, att_b, dp_b, proj, gatt, onehot, att, dp)
-    stores += staged([(att_b, att_o), (dp_b, dp_o)], out_sems.at[1])
+    hidden = windows_pass(
+        x_w, g_w, parts["r"], gain, wqkv, wproj, att_o, dp_o, att_b, dp_b, stores, out_sems, proj, gatt, onehot, att, dp
+    )
     gqkv[...] = dot_tn(hidden, dp_b[...])
     gproj[...] = dot_tn(att_b[...], g_w[...])
     for store in stores:
@@ -274,8 +281,9 @@
     for window in range(2, 6):
         past = past | ((row >= window * WIN + WIN // 2) & (row < (window + 1) * WIN))
     labels = parts[2] + jnp.where(past, 3.0, 0.0) * where[1].astype(F32)
-    hidden = windows_pass(x_w, g_w, labels, gain, wqkv, wproj, att_b, dp_b, proj, gatt, onehot, att, dp)
-    stores += staged([(att_b, att_o), (dp_b, dp_o)], out_sems.at[1])
+    hidden = windows_pass(
+        x_w, g_w, labels, gain, wqkv, wproj, att_o, dp_o, att_b, dp_b, stores, out_sems, proj, gatt, onehot, att, dp
+    )
     total[:, pl.ds(0, 3 * D)] = gqkv1[...] + dot_tn(hidden, dp_b[...])
     total[:, pl.ds(3 * D, D)] = gproj1[...] + dot_tn(att_b[...], g_w[...])
     scaled = jnp.sum(total[:, pl.ds(0, 3 * D)] * wqkv[...].astype(F32), axis=1, keepdims=True)
@@ -362,6 +370,17 @@
     out[...] = (keep[...].astype(F32) + received[...].astype(F32)).astype(BF16)
 
 
+def add_out_kernel(keep, received, out, total, sems):
+    copies = []
+    for part in range(8):
+        rows = pl.ds(part * 64, 64)
+        total[rows, :] = (keep[rows, :].astype(F32) + received[rows, :].astype(F32)).astype(BF16)
+        copies.append(pltpu.make_async_copy(total.at[rows], out.at[rows], sems.at[part]))
+        copies[-1].start()
+    for copy in copies:
+        copy.wait()
+
+
 def sum_kernel(pieces, out):
     total = pieces[0].astype(F32)
     for piece in range(1, PIECES):
@@ -369,11 +388,13 @@
     out[...] = total.astype(BF16)
 
 
-def spread_kernel(piece, received, copies, gain):
-    total = (piece[...].astype(F32) + received[...].astype(F32)).astype(BF16)
-    gain[...] = total[:, 2 * D :].astype(F32)
-    for at in range(PIECES):
-        copies[at] = total[:, : 2 * D]
+def spread_kernel(piece, received, copies, gain, total, sems):
+    both = piece[...].astype(F32) + received[...].astype(F32)
+    total[...] = both[:, : 2 * D].astype(BF16)
+    sent = staged([(total, copies.at[at]) for at in range(PIECES)], sems)
+    gain[...] = both[:, 2 * D :].astype(BF16).astype(F32)
+    for copy in sent:
+        copy.wait()
 
 
 def place_kernel(later, half, grads, *refs):
@@ -459,7 +480,7 @@
         pltpu.VMEM((HALF, D), BF16),
         pltpu.VMEM((HALF, D), BF16),
         pltpu.VMEM((HALF, 3 * D), BF16),
-        pltpu.SemaphoreType.DMA((2, 2)),
+        pltpu.SemaphoreType.DMA((4, 2)),
     ]
 
 
@@ -531,7 +552,10 @@
         where, h_lon, h_lat, h_cor, gain_row, gqkv1, gproj1, wqkv_s, wproj_s, pick0, pick1, pick2, ends, tails, ids
     )
 
-    (mine,) = call(add_kernel, [((16 * PIECES, width), BF16)], [], 10**5, "add", vmem=8)(keep, swapped(send, "core", 2, 1))
+    scratch = [pltpu.VMEM((16 * PIECES, width), BF16), pltpu.SemaphoreType.DMA((8,))]
+    (mine,) = call(add_out_kernel, [((16 * PIECES, width), BF16)], scratch, 10**5, "add", kept=1, vmem=8)(
+        keep, swapped(send, "core", 2, 1)
+    )
     mine, x1, x2 = lax.optimization_barrier((mine, x1, x2))
     pieces = lax.all_to_all(mine.reshape(PIECES, 16, -1), PLANE, 0, 0, tiled=True)
     mixed_c, tgrad_c, s_lon, s_lat, s_cor = call(
@@ -554,12 +578,19 @@
     t_lat = lax.ppermute(s_lat, LAT_AXES, lon_on)
     t_cor = lax.ppermute(s_cor, LON_AXES + LAT_AXES, both_on)
 
-    pieces, t_lon, t_lat, t_cor = lax.optimization_barrier((pieces, t_lon, t_lat, t_cor))
     (piece,) = call(sum_kernel, [((16, width), BF16)], [], 10**5, "sum", vmem=8)(pieces)
     (piece,) = call(add_kernel, [((16, width), BF16)], [], 10**5, "add", vmem=4)(piece, swapped(piece, "z_hi", 4, 1))
+    received = swapped(piece, "z_hi", 4, 3)
+    received, t_lon, t_lat, t_cor = lax.optimization_barrier((received, t_lon, t_lat, t_cor))
     copies, gain_tile = call(
-        spread_kernel, [((PIECES, 16, 2 * D), BF16), ((16, 128), F32)], [], 10**5, "spread", vmem=8
-    )(piece, swapped(piece, "z_hi", 4, 3))
+        spread_kernel,
+        [((PIECES, 16, 2 * D), BF16), ((16, 128), F32)],
+        [pltpu.VMEM((16, 2 * D), BF16), pltpu.SemaphoreType.DMA((PIECES,))],
+        10**5,
+        "spread",
+        kept=1,
+        vmem=4,
+    )(piece, received)
     gain_grad = gain_tile[:4].reshape(D) / gain
     grads = lax.all_to_all(copies, PLANE, 0, 0, tiled=True)
     mixed, tokens_grad = call(restore_kernel, [((COLS_LAT, ROWS_LON, D), BF16)] * 2, [], 10**6, "restore", vmem=10)(

time: 101 us -> 98.7 us (0.977)
  waiting for transfers between devices: 38.6 us -> 25.5 us
  starting transfers between devices: 29.4 us -> 40.6 us
    ppermute x1, waiting for transfers between devices: 15.4 us -> 1.08 us  [body(): t_cor = lax.ppermute(s_cor, LON_AXES + LAT_AXES, both_on)]
    all_to_all x1, waiting for transfers between devices: 0.01 us -> 7.89 us  [body(): lax.all_to_all(mine.reshape(PIECES, 16, -1), PLANE, 0, 0, tiled=True)]
    ppermute x4, waiting for transfers between devices: 11.7 us -> 4.12 us  [swapped(): return lax.ppermute(block, axis, [(i, i ^ bit) for i in range(size)])]
    ppermute x1, starting transfers between devices: 0.01 us -> 3.92 us  [body(): t_cor = lax.ppermute(s_cor, LON_AXES + LAT_AXES, both_on)]
    all_to_all x1, starting transfers between devices: 4.01 us -> 7.84 us  [body(): grads = lax.all_to_all(copies, PLANE, 0, 0, tiled=True)]
    ppermute x4, starting transfers between devices: 5.59 us -> 9.06 us  [swapped(): return lax.ppermute(block, axis, [(i, i ^ bit) for i in range(size)])]
    all_to_all x1, waiting for transfers between devices: 11.4 us -> 12.4 us  [body(): grads = lax.all_to_all(copies, PLANE, 0, 0, tiled=True)]
  transfers between devices with their start and end apart: 12 -> 12, of which waited for: 7 -> 6; matrix products, arithmetic and copies ran while one was open for 1% -> 1% of each run, Pallas kernels for 16% -> 17%
where the time goes in v5:
time: 98.7 us; the launch traced here: 98.4 us
  starting transfers between devices  40.6 us (41%)
  Pallas kernels  30.7 us (31%)
  waiting for transfers between devices  25.5 us (26%)
    pallas_call x9, Pallas kernels, run(): pl.pallas_call(kernel, out_shape=[pltpu.HBM(*out) if at < kept else jax.S...  27.9 us
    all_to_all x1, waiting for transfers between devices, body(): grads = lax.all_to_all(copies, PLANE, 0, 0, tiled=True)  12.4 us
    ppermute x4, starting transfers between devices, swapped(): return lax.ppermute(block, axis, [(i, i ^ bit) for i in range(size)])  9.06 us
    all_to_all x1, waiting for transfers between devices, body(): lax.all_to_all(mine.reshape(PIECES, 16, -1), PLANE, 0, 0, tiled=True)  7.89 us
    all_to_all x1, starting transfers between devices, body(): grads = lax.all_to_all(copies, PLANE, 0, 0, tiled=True)  7.84 us
    ppermute x1, starting transfers between devices, body(): h_lon = lax.ppermute(e_lon, LON_AXES, lon_back)  4.85 us
    ppermute x1, starting transfers between devices, body(): h_cor = lax.ppermute(e_cor, LON_AXES + LAT_AXES, both_back)  4.82 us
    ppermute x4, waiting for transfers between devices, swapped(): return lax.ppermute(block, axis, [(i, i ^ bit) for i in range(size)])  4.12 us
  transfers between devices with their start and end apart: 12, of which 6 were waited for; matrix products, arithmetic and copies ran while one was open for 1% of the time, Pallas kernels for 17%

profile of v5, /device:TPU:1, one launch (start us, length us, event | category | flops | bytes accessed | tf_op | source)
XLA Modules:
  0.0 98.4 jit_solution(14191620065169543890)
XLA Ops:
  0.7 3.2 %edges.1 = (bf16[96,1024]{1,0:T(8,128)(2,1)S(1)}, bf16[128,1024]{1,0:T(8,128)(2,1)S(1)}, bf16[32,1024]{1,0:T(8,128)(2,1)S(1)}, bf16[12,48,512]{2,1,0:T(8,128)(2,...) custom-call(s32[2]{0:T(128)S(1)} %pad_add_fusion.where, ...), custom_call_target="tpu_custom_call" | custom-call | flops 1000000 | bytes 8388608 | tf_op jit(solution)/shard_map/edges/pallas_call | solution.py:495
  3.9 3.3 %collective-permute-start.1 = (bf16[128,1024]{1,0:T(8,128)(2,1)S(1)}, bf16[128,1024]{1,0:T(8,128)(2,1)S(1)}, u32[]{:S(2)}, u32[]{:S(2)}) collective-permute-start(bf16[128,1024]{1,0:T(8,128)(2,1)S(1)} %get-tuple-element.55), channel_id=1, source_target_pairs={{1,0},{2,1},{3,2},{4,3},{5,4},{6,5},{7,6},{8,7},{9,8},{10,9},{11,1... | collective-permute-start | bytes 786440 | tf_op jit(solution)/shard_map/ppermute | solution.py:533
  7.3 4.9 %collective-permute-start = (bf16[96,1024]{1,0:T(8,128)(2,1)S(1)}, bf16[96,1024]{1,0:T(8,128)(2,1)S(1)}, u32[]{:S(2)}, u32[]{:S(2)}) collective-permute-start(bf16[96,1024]{1,0:T(8,128)(2,1)S(1)} %get-tuple-element.54), channel_id=1, source_target_pairs={{16,0},{32,16},{48,32},{64,48},{80,64},{96,80},{112,96},{128,112},... | collective-permute-start | bytes 589832 | tf_op jit(solution)/shard_map/ppermute | solution.py:532
  12.1 4.8 %collective-permute-start.2 = (bf16[32,1024]{1,0:T(8,128)(2,1)S(1)}, bf16[32,1024]{1,0:T(8,128)(2,1)S(1)}, u32[]{:S(2)}, u32[]{:S(2)}) collective-permute-start(bf16[32,1024]{1,0:T(8,128)(2,1)S(1)} %get-tuple-element.56), channel_id=1, source_target_pairs={{17,0},{18,1},{19,2},{20,3},{21,4},{22,5},{23,6},{24,7},{25,8},{26... | collective-permute-start | bytes 196616 | tf_op jit(solution)/shard_map/ppermute | solution.py:534
  16.9 6.4 %inner.1 = (bf16[432,512]{1,0:T(8,128)(2,1)}, bf16[432,512]{1,0:T(8,128)(2,1)}, bf16[432,512]{1,0:T(8,128)(2,1)}, bf16[432,1536]{1,0:T(8,128)(2,1)}, f32[512,1536]{1,0:T(8,128)S(1)}, /*index=5*/f32[512,512]{1,0:T(8,128)S(1)}) custom-call(bf16[12,48,512]{2,1,0:T(8,128)(2,1)S(1)} %get-tuple-element.57.x, bf16[12,48,512]{2,1,0:T(8,128)(2,1)S(1)} %get-tuple-element.58.g, ...), custom_call_target="tpu_custom_call" | custom-call | flops 4000000000 | bytes 8388608 | tf_op jit(solution)/shard_map/inner/pallas_call | solution.py:495
  23.3 7.2 %outer.1 = (bf16[432,512]{1,0:T(8,128)(2,1)}, bf16[432,512]{1,0:T(8,128)(2,1)}, bf16[432,512]{1,0:T(8,128)(2,1)}, bf16[432,1536]{1,0:T(8,128)(2,1)}, bf16[512,11...) custom-call(s32[2]{0:T(128)S(1)} %pad_add_fusion.where, bf16[96,1024]{1,0:T(8,128)(2,1)S(1)} %collective-permute-done.h_lon, ...), custom_call_target="tpu_custom_call" | custom-call | flops 4000000000 | bytes 8388608 | tf_op jit(solution)/shard_map/outer/pallas_call | solution.py:495
  30.9 2.8 %collective-permute-done.3.received = bf16[512,1152]{1,0:T(8,128)(2,1)S(1)} collective-permute-done((bf16[512,1152]{1,0:T(8,128)(2,1)S(1)}, bf16[512,1152]{1,0:T(8,128)(2,1)S(1)}, u32[]{:S(2)}, u32[]{:S(2)}) %collective-permute-start.3) | collective-permute-done | bytes 1179680 | tf_op jit(solution)/shard_map/ppermute | solution.py:510
  33.7 1.1 %add.12 = bf16[512,1152]{1,0:T(8,128)(2,1)} custom-call(bf16[512,1152]{1,0:T(8,128)(2,1)S(1)} %get-tuple-element.70.keep, bf16[512,1152]{1,0:T(8,128)(2,1)S(1)} %collective-permute-done.3.received), custom_call_target="tpu_custom_call" | custom-call | flops 100000 | bytes 8388608 | tf_op jit(solution)/shard_map/add/pallas_call | solution.py:495
  34.9 4.0 %all-to-all-start = ((bf16[32,16,1152]{2,1,0:T(8,128)(2,1)}), bf16[32,16,1152]{2,1,0:T(8,128)(2,1)S(1)}, u32[]{:S(2)}, u32[]{:S(2)}) async-start(bf16[32,16,1152]{2,1,0:T(8,128)(2,1)} %bitcast.17), calls=%async_computation | async-start | bytes 2359296 | tf_op jit(solution)/shard_map/all_to_all | solution.py:560
  38.8 7.0 %tokens.1 = (bf16[18,48,512]{2,1,0:T(8,128)(2,1)S(1)}, bf16[18,48,512]{2,1,0:T(8,128)(2,1)S(1)}, bf16[96,1024]{1,0:T(8,128)(2,1)}, bf16[128,1024]{1,0:T(8,128)(2,1)}, bf16[32,1024]{1,0:T(8,128)(2,1)S(1)}) custom-call(bf16[432,512]{1,0:T(8,128)(2,1)} %get-tuple-element.75.x1_h, bf16[432,512]{1,0:T(8,128)(2,1)} %get-tuple-element.76.g1_h, ...), custom_call_target="tpu_custom_call" | custom-call | flops 4000000000 | bytes 8388608 | tf_op jit(solution)/shard_map/tokens/pallas_call | solution.py:495
  45.9 1.6 %collective-permute-start.7 = (bf16[128,1024]{1,0:T(8,128)(2,1)}, bf16[128,1024]{1,0:T(8,128)(2,1)S(1)}, u32[]{:S(2)}, u32[]{:S(2)}) collective-permute-start(bf16[128,1024]{1,0:T(8,128)(2,1)} %get-tuple-element.84), channel_id=1, source_target_pairs={{0,1},{1,2},{2,3},{3,4},{4,5},{5,6},{6,7},{7,8},{8,9},{9,10},{10,1... | collective-permute-start | bytes 786440 | tf_op jit(solution)/shard_map/ppermute | solution.py:578
  47.5 1.2 %collective-permute-start.6 = (bf16[96,1024]{1,0:T(8,128)(2,1)}, bf16[96,1024]{1,0:T(8,128)(2,1)S(1)}, u32[]{:S(2)}, u32[]{:S(2)}) collective-permute-start(bf16[96,1024]{1,0:T(8,128)(2,1)} %get-tuple-element.83), channel_id=1, source_target_pairs={{0,16},{16,32},{32,48},{48,64},{64,80},{80,96},{96,112},{112,128},... | collective-permute-start | bytes 589832 | tf_op jit(solution)/shard_map/ppermute | solution.py:577
  48.7 7.9 %all-to-all-done.pieces = bf16[32,16,1152]{2,1,0:T(8,128)(2,1)S(1)} async-done(((bf16[32,16,1152]{2,1,0:T(8,128)(2,1)}), bf16[32,16,1152]{2,1,0:T(8,128)(2,1)S(1)}, u32[]{:S(2)}, u32[]{:S(2)}) %all-to-all-start) | async-done | bytes 1179680 | tf_op jit(solution)/shard_map/all_to_all | solution.py:560
  57.5 3.9 %collective-permute-start.8 = (bf16[32,1024]{1,0:T(8,128)(2,1)S(1)}, bf16[32,1024]{1,0:T(8,128)(2,1)S(1)}, u32[]{:S(2)}, u32[]{:S(2)}) collective-permute-start(bf16[32,1024]{1,0:T(8,128)(2,1)S(1)} %get-tuple-element.85), channel_id=1, source_target_pairs={{0,17},{1,18},{2,19},{3,20},{4,21},{5,22},{6,23},{7,24},{8,25},{9,... | collective-permute-start | bytes 196616 | tf_op jit(solution)/shard_map/ppermute | solution.py:579
  61.5 3.9 %collective-permute-start.5 = (bf16[16,1152]{1,0:T(8,128)(2,1)S(1)}, bf16[16,1152]{1,0:T(8,128)(2,1)S(1)}, u32[]{:S(2)}, u32[]{:S(2)}) collective-permute-start(bf16[16,1152]{1,0:T(8,128)(2,1)S(1)} %add.13.piece), channel_id=1, source_target_pairs={{0,96},{32,64},{64,32},{96,0},{1,97},{33,65},{65,33},{97,1},{2,98}... | collective-permute-start | bytes 110600 | tf_op jit(solution)/shard_map/ppermute | solution.py:510
  65.4 1.1 %collective-permute-done.8.h_cor = bf16[32,1024]{1,0:T(8,128)(2,1)S(1)} collective-permute-done((bf16[32,1024]{1,0:T(8,128)(2,1)S(1)}, bf16[32,1024]{1,0:T(8,128)(2,1)S(1)}, u32[]{:S(2)}, u32[]{:S(2)}) %collective-permute-start.8) | collective-permute-done | bytes 65568 | tf_op jit(solution)/shard_map/ppermute | solution.py:579
  66.5 1.0 %collective-permute-done.5.received = bf16[16,1152]{1,0:T(8,128)(2,1)S(1)} collective-permute-done((bf16[16,1152]{1,0:T(8,128)(2,1)S(1)}, bf16[16,1152]{1,0:T(8,128)(2,1)S(1)}, u32[]{:S(2)}, u32[]{:S(2)}) %collective-permute-start.5) | collective-permute-done | bytes 36896 | tf_op jit(solution)/shard_map/ppermute | solution.py:510
  67.5 1.2 %spread.1 = (bf16[32,16,1024]{2,1,0:T(8,128)(2,1)}, f32[16,128]{1,0:T(8,128)S(1)}) custom-call(bf16[16,1152]{1,0:T(8,128)(2,1)S(1)} %add.13.piece, bf16[16,1152]{1,0:T(8,128)(2,1)S(1)} %collective-permute-done.5.received), custom_call_target="tpu_custom_call" | custom-call | flops 100000 | bytes 8388608 | tf_op jit(solution)/shard_map/spread/pallas_call | solution.py:495
  68.7 7.8 %all-to-all-start.1 = ((bf16[32,16,1024]{2,1,0:T(8,128)(2,1)}), bf16[32,16,1024]{2,1,0:T(8,128)(2,1)S(1)}, u32[]{:S(2)}, u32[]{:S(2)}) async-start(bf16[32,16,1024]{2,1,0:T(8,128)(2,1)} %get-tuple-element.87), calls=%async_computation.1 | async-start | bytes 2097152 | tf_op jit(solution)/shard_map/all_to_all | solution.py:595
  76.6 1.5 %restore.1 = (bf16[18,48,512]{2,1,0:T(8,128)(2,1)}, bf16[18,48,512]{2,1,0:T(8,128)(2,1)}) custom-call(bf16[18,48,512]{2,1,0:T(8,128)(2,1)S(1)} %get-tuple-element.88.mixed_c, bf16[18,48,512]{2,1,0:T(8,128)(2,1)S(1)} %get-tuple-element.89.tgrad_c, bf16[96,1024]{1,0:T(8,128)(2,1)S(1)} %collective-permute-done.6.h_lon, ...), custom_call_target="tpu_custom_call" | custom-call | flops 1000000 | bytes 8388608 | tf_op jit(solution)/shard_map/restore/pallas_call | solution.py:495
  78.1 12.4 %all-to-all-done.1 = bf16[32,16,1024]{2,1,0:T(8,128)(2,1)S(1)} async-done(((bf16[32,16,1024]{2,1,0:T(8,128)(2,1)}), bf16[32,16,1024]{2,1,0:T(8,128)(2,1)S(1)}, u32[]{:S(2)}, u32[]{:S(2)}) %all-to-all-start.1) | async-done | bytes 1048608 | tf_op jit(solution)/shard_map/all_to_all | solution.py:595
  90.5 4.0 %collective-permute-start.9 = (bf16[512,1024]{1,0:T(8,128)(2,1)S(1)}, bf16[512,1024]{1,0:T(8,128)(2,1)S(1)}, u32[]{:S(2)}, u32[]{:S(2)}) collective-permute-start(bf16[512,1024]{1,0:T(8,128)(2,1)S(1)} %bitcast.12), channel_id=1, source_target_pairs={{0,1},{1,0},{2,3},{3,2},{4,5},{5,4},{6,7},{7,6},{8,9},{9,8},{10,11... | collective-permute-start | bytes 3145736 | tf_op jit(solution)/shard_map/ppermute | solution.py:510
  95.1 1.4 %place.2 = (f32[512,1536]{1,0:T(8,128)}, f32[512,512]{1,0:T(8,128)}) custom-call(s32[1]{0:T(128)} %bitcast.half, bf16[512,1024]{1,0:T(8,128)(2,1)S(1)} %bitcast.13), custom_call_target="tpu_custom_call" | custom-call | flops 1000000 | bytes 3145728 | tf_op jit(solution)/shard_map/place/pallas_call | solution.py:419
  96.8 1.4 %place.3 = (f32[512,1536]{1,0:T(8,128)}, f32[512,512]{1,0:T(8,128)}) custom-call(s32[1]{0:T(128)S(6)} %sub.3.half, bf16[512,1024]{1,0:T(8,128)(2,1)S(1)} %collective-permute-done.9.grads, f32[512,1536]{1,0:T(8,128)} %get-tuple-element.98.refs_0_, f32[512,512]{1,0:T(8,128)} %get-tuple-element.99.refs_1_), custom_call_target="tpu_custom_call", output_to_operand_aliasing={{0}: (2, {}), {1}: (3, {})} | custom-call | flops 1000000 | bytes 3145728 | tf_op jit(solution)/shard_map/place/pallas_call | solution.py:419
  (15 shorter events, 2.3 us)
Async XLA Ops:
  0.7 16.2 %copy-start = (f32[512]{0:T(512)S(1)}, f32[512]{0:T(512)}, u32[]{:S(2)}) copy-start(f32[512]{0:T(512)} %param.14) | copy-start | bytes 6148
  3.9 19.4 %collective-permute-start.1 = (bf16[128,1024]{1,0:T(8,128)(2,1)S(1)}, bf16[128,1024]{1,0:T(8,128)(2,1)S(1)}, u32[]{:S(2)}, u32[]{:S(2)}) collective-permute-start(bf16[128,1024]{1,0:T(8,128)(2,1)S(1)} %get-tuple-element.55), channel_id=1, source_target_pairs={{1,0},{2,1},{3,2},{4,3},{5,4},{6,5},{7,6},{8,7},{9,8},{10,9},{11,1... | collective-permute-start | bytes 786440 | tf_op jit(solution)/shard_map/ppermute | solution.py:533
  7.3 16.1 %collective-permute-start = (bf16[96,1024]{1,0:T(8,128)(2,1)S(1)}, bf16[96,1024]{1,0:T(8,128)(2,1)S(1)}, u32[]{:S(2)}, u32[]{:S(2)}) collective-permute-start(bf16[96,1024]{1,0:T(8,128)(2,1)S(1)} %get-tuple-element.54), channel_id=1, source_target_pairs={{16,0},{32,16},{48,32},{64,48},{80,64},{96,80},{112,96},{128,112},... | collective-permute-start | bytes 589832 | tf_op jit(solution)/shard_map/ppermute | solution.py:532
  12.1 11.2 %collective-permute-start.2 = (bf16[32,1024]{1,0:T(8,128)(2,1)S(1)}, bf16[32,1024]{1,0:T(8,128)(2,1)S(1)}, u32[]{:S(2)}, u32[]{:S(2)}) collective-permute-start(bf16[32,1024]{1,0:T(8,128)(2,1)S(1)} %get-tuple-element.56), channel_id=1, source_target_pairs={{17,0},{18,1},{19,2},{20,3},{21,4},{22,5},{23,6},{24,7},{25,8},{26... | collective-permute-start | bytes 196616 | tf_op jit(solution)/shard_map/ppermute | solution.py:534
  30.6 3.2 %collective-permute-start.3 = (bf16[512,1152]{1,0:T(8,128)(2,1)S(1)}, bf16[512,1152]{1,0:T(8,128)(2,1)S(1)}, u32[]{:S(2)}, u32[]{:S(2)}) collective-permute-start(bf16[512,1152]{1,0:T(8,128)(2,1)S(1)} %get-tuple-element.71), channel_id=1, source_target_pairs={{0,1},{1,0},{2,3},{3,2},{4,5},{5,4},{6,7},{7,6},{8,9},{9,8},{10,11... | collective-permute-start | bytes 3538952 | tf_op jit(solution)/shard_map/ppermute | solution.py:510
  34.9 21.7 %all-to-all-start = ((bf16[32,16,1152]{2,1,0:T(8,128)(2,1)}), bf16[32,16,1152]{2,1,0:T(8,128)(2,1)S(1)}, u32[]{:S(2)}, u32[]{:S(2)}) async-start(bf16[32,16,1152]{2,1,0:T(8,128)(2,1)} %bitcast.17), calls=%async_computation | async-start | bytes 2359296 | tf_op jit(solution)/shard_map/all_to_all | solution.py:560
  45.9 20.6 %collective-permute-start.7 = (bf16[128,1024]{1,0:T(8,128)(2,1)}, bf16[128,1024]{1,0:T(8,128)(2,1)S(1)}, u32[]{:S(2)}, u32[]{:S(2)}) collective-permute-start(bf16[128,1024]{1,0:T(8,128)(2,1)} %get-tuple-element.84), channel_id=1, source_target_pairs={{0,1},{1,2},{2,3},{3,4},{4,5},{5,6},{6,7},{7,8},{8,9},{9,10},{10,1... | collective-permute-start | bytes 786440 | tf_op jit(solution)/shard_map/ppermute | solution.py:578
  47.5 19.0 %collective-permute-start.6 = (bf16[96,1024]{1,0:T(8,128)(2,1)}, bf16[96,1024]{1,0:T(8,128)(2,1)S(1)}, u32[]{:S(2)}, u32[]{:S(2)}) collective-permute-start(bf16[96,1024]{1,0:T(8,128)(2,1)} %get-tuple-element.83), channel_id=1, source_target_pairs={{0,16},{16,32},{32,48},{48,64},{64,80},{80,96},{96,112},{112,128},... | collective-permute-start | bytes 589832 | tf_op jit(solution)/shard_map/ppermute | solution.py:577
  56.7 4.7 %collective-permute-start.4 = (bf16[16,1152]{1,0:T(8,128)(2,1)S(1)}, bf16[16,1152]{1,0:T(8,128)(2,1)S(1)}, u32[]{:S(2)}, u32[]{:S(2)}) collective-permute-start(bf16[16,1152]{1,0:T(8,128)(2,1)S(1)} %sum.1.keep), channel_id=1, source_target_pairs={{0,32},{32,0},{64,96},{96,64},{1,33},{33,1},{65,97},{97,65},{2,34}... | collective-permute-start | bytes 110600 | tf_op jit(solution)/shard_map/ppermute | solution.py:510
  57.5 8.9 %collective-permute-start.8 = (bf16[32,1024]{1,0:T(8,128)(2,1)S(1)}, bf16[32,1024]{1,0:T(8,128)(2,1)S(1)}, u32[]{:S(2)}, u32[]{:S(2)}) collective-permute-start(bf16[32,1024]{1,0:T(8,128)(2,1)S(1)} %get-tuple-element.85), channel_id=1, source_target_pairs={{0,17},{1,18},{2,19},{3,20},{4,21},{5,22},{6,23},{7,24},{8,25},{9,... | collective-permute-start | bytes 196616 | tf_op jit(solution)/shard_map/ppermute | solution.py:579
  61.5 6.0 %collective-permute-start.5 = (bf16[16,1152]{1,0:T(8,128)(2,1)S(1)}, bf16[16,1152]{1,0:T(8,128)(2,1)S(1)}, u32[]{:S(2)}, u32[]{:S(2)}) collective-permute-start(bf16[16,1152]{1,0:T(8,128)(2,1)S(1)} %add.13.piece), channel_id=1, source_target_pairs={{0,96},{32,64},{64,32},{96,0},{1,97},{33,65},{65,33},{97,1},{2,98}... | collective-permute-start | bytes 110600 | tf_op jit(solution)/shard_map/ppermute | solution.py:510
  68.7 21.8 %all-to-all-start.1 = ((bf16[32,16,1024]{2,1,0:T(8,128)(2,1)}), bf16[32,16,1024]{2,1,0:T(8,128)(2,1)S(1)}, u32[]{:S(2)}, u32[]{:S(2)}) async-start(bf16[32,16,1024]{2,1,0:T(8,128)(2,1)} %get-tuple-element.87), calls=%async_computation.1 | async-start | bytes 2097152 | tf_op jit(solution)/shard_map/all_to_all | solution.py:595
  90.5 6.3 %collective-permute-start.9 = (bf16[512,1024]{1,0:T(8,128)(2,1)S(1)}, bf16[512,1024]{1,0:T(8,128)(2,1)S(1)}, u32[]{:S(2)}, u32[]{:S(2)}) collective-permute-start(bf16[512,1024]{1,0:T(8,128)(2,1)S(1)} %bitcast.12), channel_id=1, source_target_pairs={{0,1},{1,0},{2,3},{3,2},{4,5},{5,4},{6,7},{7,6},{8,9},{9,8},{10,11... | collective-permute-start | bytes 3145736 | tf_op jit(solution)/shard_map/ppermute | solution.py:510

commit v6 on v5

--- a/solution.py
+++ b/solution.py
@@ -366,10 +366,6 @@
                 out[row, pl.ds(0, 2 * EDGE), :] = whole.astype(BF16)
 
 
-def add_kernel(keep, received, out):
-    out[...] = (keep[...].astype(F32) + received[...].astype(F32)).astype(BF16)
-
-
 def add_out_kernel(keep, received, out, total, sems):
     copies = []
     for part in range(8):
@@ -388,8 +384,9 @@
     out[...] = total.astype(BF16)
 
 
-def spread_kernel(piece, received, copies, gain, total, sems):
-    both = piece[...].astype(F32) + received[...].astype(F32)
+def spread_kernel(piece, second, first, third, copies, gain, total, sems):
+    both = piece[...].astype(F32) + first[...].astype(F32)
+    both = both + (second[...].astype(F32) + third[...].astype(F32))
     total[...] = both[:, : 2 * D].astype(BF16)
     sent = staged([(total, copies.at[at]) for at in range(PIECES)], sems)
     gain[...] = both[:, 2 * D :].astype(BF16).astype(F32)
@@ -579,8 +576,7 @@
     t_cor = lax.ppermute(s_cor, LON_AXES + LAT_AXES, both_on)
 
     (piece,) = call(sum_kernel, [((16, width), BF16)], [], 10**5, "sum", vmem=8)(pieces)
-    (piece,) = call(add_kernel, [((16, width), BF16)], [], 10**5, "add", vmem=4)(piece, swapped(piece, "z_hi", 4, 1))
-    received = swapped(piece, "z_hi", 4, 3)
+    received = [swapped(piece, "z_hi", 4, bit) for bit in (2, 1, 3)]
     received, t_lon, t_lat, t_cor = lax.optimization_barrier((received, t_lon, t_lat, t_cor))
     copies, gain_tile = call(
         spread_kernel,
@@ -590,7 +586,7 @@
         "spread",
         kept=1,
         vmem=4,
-    )(piece, received)
+    )(piece, *received)
     gain_grad = gain_tile[:4].reshape(D) / gain
     grads = lax.all_to_all(copies, PLANE, 0, 0, tiled=True)
     mixed, tokens_grad = call(restore_kernel, [((COLS_LAT, ROWS_LON, D), BF16)] * 2, [], 10**6, "restore", vmem=10)(

time: 98.7 us -> 98.8 us (level)
  waiting for transfers between devices: 25.5 us -> 28.6 us
  starting transfers between devices: 40.6 us -> 37.7 us
    ppermute x4 -> x5, waiting for transfers between devices: 4.12 us -> 8.58 us  [swapped(): return lax.ppermute(block, axis, [(i, i ^ bit) for i in range(size)])]
    ppermute x1, starting transfers between devices: 3.92 us -> 0.45 us  [body(): t_cor = lax.ppermute(s_cor, LON_AXES + LAT_AXES, both_on)]
    ppermute x4 -> x5, starting transfers between devices: 9.06 us -> 11.1 us  [swapped(): return lax.ppermute(block, axis, [(i, i ^ bit) for i in range(size)])]
    all_to_all x1, starting transfers between devices: 7.84 us -> 6.36 us  [body(): grads = lax.all_to_all(copies, PLANE, 0, 0, tiled=True)]
    pallas_call x9 -> x8, Pallas kernels: 27.9 us -> 27.9 us  [run(): pl.pallas_call(kernel, out_shape=[pltpu.HBM(*out) if at < kept else jax.S...]
  transfers between devices with their start and end apart: 12 -> 13, of which waited for: 6 -> 8; matrix products, arithmetic and copies ran while one was open for 1% -> 1% of each run, Pallas kernels for 17% -> 17%
where the time goes in v6:
time: 98.8 us; the launch traced here: 98.5 us
  starting transfers between devices  37.7 us (38%)
  Pallas kernels  30.7 us (31%)
  waiting for transfers between devices  28.6 us (29%)
    pallas_call x8, Pallas kernels, run(): pl.pallas_call(kernel, out_shape=[pltpu.HBM(*out) if at < kept else jax.S...  27.9 us
    all_to_all x1, waiting for transfers between devices, body(): grads = lax.all_to_all(copies, PLANE, 0, 0, tiled=True)  12.3 us
    ppermute x5, starting transfers between devices, swapped(): return lax.ppermute(block, axis, [(i, i ^ bit) for i in range(size)])  11.1 us
    ppermute x5, waiting for transfers between devices, swapped(): return lax.ppermute(block, axis, [(i, i ^ bit) for i in range(size)])  8.58 us
    all_to_all x1, waiting for transfers between devices, body(): lax.all_to_all(mine.reshape(PIECES, 16, -1), PLANE, 0, 0, tiled=True)  7.43 us
    all_to_all x1, starting transfers between devices, body(): grads = lax.all_to_all(copies, PLANE, 0, 0, tiled=True)  6.36 us
    ppermute x1, starting transfers between devices, body(): h_lon = lax.ppermute(e_lon, LON_AXES, lon_back)  4.85 us
    ppermute x1, starting transfers between devices, body(): h_cor = lax.ppermute(e_cor, LON_AXES + LAT_AXES, both_back)  4.82 us
  transfers between devices with their start and end apart: 13, of which 8 were waited for; matrix products, arithmetic and copies ran while one was open for 1% of the time, Pallas kernels for 17%

profile of v6, /device:TPU:1, one launch (start us, length us, event | category | flops | bytes accessed | tf_op | source)
XLA Modules:
  0.0 98.5 jit_solution(3153870633293794097)
XLA Ops:
  0.7 3.2 %edges.1 = (bf16[96,1024]{1,0:T(8,128)(2,1)S(1)}, bf16[128,1024]{1,0:T(8,128)(2,1)S(1)}, bf16[32,1024]{1,0:T(8,128)(2,1)S(1)}, bf16[12,48,512]{2,1,0:T(8,128)(2,...) custom-call(s32[2]{0:T(128)S(1)} %pad_add_fusion.where, ...), custom_call_target="tpu_custom_call" | custom-call | flops 1000000 | bytes 8388608 | tf_op jit(solution)/shard_map/edges/pallas_call | solution.py:492
  3.9 3.3 %collective-permute-start.1 = (bf16[128,1024]{1,0:T(8,128)(2,1)S(1)}, bf16[128,1024]{1,0:T(8,128)(2,1)S(1)}, u32[]{:S(2)}, u32[]{:S(2)}) collective-permute-start(bf16[128,1024]{1,0:T(8,128)(2,1)S(1)} %get-tuple-element.57), channel_id=1, source_target_pairs={{1,0},{2,1},{3,2},{4,3},{5,4},{6,5},{7,6},{8,7},{9,8},{10,9},{11,1... | collective-permute-start | bytes 786440 | tf_op jit(solution)/shard_map/ppermute | solution.py:530
  7.3 4.9 %collective-permute-start = (bf16[96,1024]{1,0:T(8,128)(2,1)S(1)}, bf16[96,1024]{1,0:T(8,128)(2,1)S(1)}, u32[]{:S(2)}, u32[]{:S(2)}) collective-permute-start(bf16[96,1024]{1,0:T(8,128)(2,1)S(1)} %get-tuple-element.56), channel_id=1, source_target_pairs={{16,0},{32,16},{48,32},{64,48},{80,64},{96,80},{112,96},{128,112},... | collective-permute-start | bytes 589832 | tf_op jit(solution)/shard_map/ppermute | solution.py:529
  12.1 4.8 %collective-permute-start.2 = (bf16[32,1024]{1,0:T(8,128)(2,1)S(1)}, bf16[32,1024]{1,0:T(8,128)(2,1)S(1)}, u32[]{:S(2)}, u32[]{:S(2)}) collective-permute-start(bf16[32,1024]{1,0:T(8,128)(2,1)S(1)} %get-tuple-element.58), channel_id=1, source_target_pairs={{17,0},{18,1},{19,2},{20,3},{21,4},{22,5},{23,6},{24,7},{25,8},{26... | collective-permute-start | bytes 196616 | tf_op jit(solution)/shard_map/ppermute | solution.py:531
  16.9 6.4 %inner.1 = (bf16[432,512]{1,0:T(8,128)(2,1)}, bf16[432,512]{1,0:T(8,128)(2,1)}, bf16[432,512]{1,0:T(8,128)(2,1)}, bf16[432,1536]{1,0:T(8,128)(2,1)}, f32[512,1536]{1,0:T(8,128)S(1)}, /*index=5*/f32[512,512]{1,0:T(8,128)S(1)}) custom-call(bf16[12,48,512]{2,1,0:T(8,128)(2,1)S(1)} %get-tuple-element.59.x, bf16[12,48,512]{2,1,0:T(8,128)(2,1)S(1)} %get-tuple-element.60.g, ...), custom_call_target="tpu_custom_call" | custom-call | flops 4000000000 | bytes 8388608 | tf_op jit(solution)/shard_map/inner/pallas_call | solution.py:492
  23.3 7.2 %outer.1 = (bf16[432,512]{1,0:T(8,128)(2,1)}, bf16[432,512]{1,0:T(8,128)(2,1)}, bf16[432,512]{1,0:T(8,128)(2,1)}, bf16[432,1536]{1,0:T(8,128)(2,1)}, bf16[512,11...) custom-call(s32[2]{0:T(128)S(1)} %pad_add_fusion.where, bf16[96,1024]{1,0:T(8,128)(2,1)S(1)} %collective-permute-done.h_lon, ...), custom_call_target="tpu_custom_call" | custom-call | flops 4000000000 | bytes 8388608 | tf_op jit(solution)/shard_map/outer/pallas_call | solution.py:492
  30.9 2.8 %collective-permute-done.3.received = bf16[512,1152]{1,0:T(8,128)(2,1)S(1)} collective-permute-done((bf16[512,1152]{1,0:T(8,128)(2,1)S(1)}, bf16[512,1152]{1,0:T(8,128)(2,1)S(1)}, u32[]{:S(2)}, u32[]{:S(2)}) %collective-permute-start.3) | collective-permute-done | bytes 1179680 | tf_op jit(solution)/shard_map/ppermute | solution.py:507
  33.7 1.1 %add.11 = bf16[512,1152]{1,0:T(8,128)(2,1)} custom-call(bf16[512,1152]{1,0:T(8,128)(2,1)S(1)} %get-tuple-element.72.keep, bf16[512,1152]{1,0:T(8,128)(2,1)S(1)} %collective-permute-done.3.received), custom_call_target="tpu_custom_call" | custom-call | flops 100000 | bytes 8388608 | tf_op jit(solution)/shard_map/add/pallas_call | solution.py:492
  34.9 4.0 %all-to-all-start = ((bf16[32,16,1152]{2,1,0:T(8,128)(2,1)}), bf16[32,16,1152]{2,1,0:T(8,128)(2,1)S(1)}, u32[]{:S(2)}, u32[]{:S(2)}) async-start(bf16[32,16,1152]{2,1,0:T(8,128)(2,1)} %bitcast.17), calls=%async_computation | async-start | bytes 2359296 | tf_op jit(solution)/shard_map/all_to_all | solution.py:557
  38.9 7.0 %tokens.1 = (bf16[18,48,512]{2,1,0:T(8,128)(2,1)S(1)}, bf16[18,48,512]{2,1,0:T(8,128)(2,1)S(1)}, bf16[96,1024]{1,0:T(8,128)(2,1)}, bf16[128,1024]{1,0:T(8,128)(2,1)}, bf16[32,1024]{1,0:T(8,128)(2,1)S(1)}) custom-call(bf16[432,512]{1,0:T(8,128)(2,1)} %get-tuple-element.77.x1_h, bf16[432,512]{1,0:T(8,128)(2,1)} %get-tuple-element.78.g1_h, ...), custom_call_target="tpu_custom_call" | custom-call | flops 4000000000 | bytes 8388608 | tf_op jit(solution)/shard_map/tokens/pallas_call | solution.py:492
  45.9 1.6 %collective-permute-start.8 = (bf16[128,1024]{1,0:T(8,128)(2,1)}, bf16[128,1024]{1,0:T(8,128)(2,1)S(1)}, u32[]{:S(2)}, u32[]{:S(2)}) collective-permute-start(bf16[128,1024]{1,0:T(8,128)(2,1)} %get-tuple-element.86), channel_id=1, source_target_pairs={{0,1},{1,2},{2,3},{3,4},{4,5},{5,6},{6,7},{7,8},{8,9},{9,10},{10,1... | collective-permute-start | bytes 786440 | tf_op jit(solution)/shard_map/ppermute | solution.py:575
  47.5 1.2 %collective-permute-start.7 = (bf16[96,1024]{1,0:T(8,128)(2,1)}, bf16[96,1024]{1,0:T(8,128)(2,1)S(1)}, u32[]{:S(2)}, u32[]{:S(2)}) collective-permute-start(bf16[96,1024]{1,0:T(8,128)(2,1)} %get-tuple-element.85), channel_id=1, source_target_pairs={{0,16},{16,32},{32,48},{48,64},{64,80},{80,96},{96,112},{112,128},... | collective-permute-start | bytes 589832 | tf_op jit(solution)/shard_map/ppermute | solution.py:574
  49.2 7.4 %all-to-all-done.pieces = bf16[32,16,1152]{2,1,0:T(8,128)(2,1)S(1)} async-done(((bf16[32,16,1152]{2,1,0:T(8,128)(2,1)}), bf16[32,16,1152]{2,1,0:T(8,128)(2,1)S(1)}, u32[]{:S(2)}, u32[]{:S(2)}) %all-to-all-start) | async-done | bytes 1179680 | tf_op jit(solution)/shard_map/all_to_all | solution.py:557
  56.8 3.1 %collective-permute-start.4 = (bf16[16,1152]{1,0:T(8,128)(2,1)S(1)}, bf16[16,1152]{1,0:T(8,128)(2,1)S(1)}, u32[]{:S(2)}, u32[]{:S(2)}) collective-permute-start(bf16[16,1152]{1,0:T(8,128)(2,1)S(1)} %sum.1.piece), channel_id=1, source_target_pairs={{0,64},{32,96},{64,0},{96,32},{1,65},{33,97},{65,1},{97,33},{2,66}... | collective-permute-start | bytes 110600 | tf_op jit(solution)/shard_map/ppermute | solution.py:507
  59.8 3.6 %collective-permute-start.5 = (bf16[16,1152]{1,0:T(8,128)(2,1)S(1)}, bf16[16,1152]{1,0:T(8,128)(2,1)S(1)}, u32[]{:S(2)}, u32[]{:S(2)}) collective-permute-start(bf16[16,1152]{1,0:T(8,128)(2,1)S(1)} %sum.1.piece), channel_id=1, source_target_pairs={{0,32},{32,0},{64,96},{96,64},{1,33},{33,1},{65,97},{97,65},{2,34}... | collective-permute-start | bytes 110600 | tf_op jit(solution)/shard_map/ppermute | solution.py:507
  63.7 1.1 %collective-permute-done.5.first = bf16[16,1152]{1,0:T(8,128)(2,1)S(1)} collective-permute-done((bf16[16,1152]{1,0:T(8,128)(2,1)S(1)}, bf16[16,1152]{1,0:T(8,128)(2,1)S(1)}, u32[]{:S(2)}, u32[]{:S(2)}) %collective-permute-start.5) | collective-permute-done | bytes 36896 | tf_op jit(solution)/shard_map/ppermute | solution.py:507
  64.8 4.3 %collective-permute-done.6.third = bf16[16,1152]{1,0:T(8,128)(2,1)S(1)} collective-permute-done((bf16[16,1152]{1,0:T(8,128)(2,1)S(1)}, bf16[16,1152]{1,0:T(8,128)(2,1)S(1)}, u32[]{:S(2)}, u32[]{:S(2)}) %collective-permute-start.6) | collective-permute-done | bytes 36896 | tf_op jit(solution)/shard_map/ppermute | solution.py:507
  69.1 1.2 %spread.1 = (bf16[32,16,1024]{2,1,0:T(8,128)(2,1)}, f32[16,128]{1,0:T(8,128)S(1)}) custom-call(bf16[16,1152]{1,0:T(8,128)(2,1)S(1)} %sum.1.piece, bf16[16,1152]{1,0:T(8,128)(2,1)S(1)} %collective-permute-done.4.second, bf16[16,1152]{1,0:T(8,128)(2,1)S(1)} %collective-permute-done.5.first, bf16[16,1152]{1,0:T(8,128)(2,1)S(1)} %collective-permute-done.6.third), custom_call_target="tpu_custom_call" | custom-call | flops 100000 | bytes 8388608 | tf_op jit(solution)/shard_map/spread/pallas_call | solution.py:492
  70.3 6.4 %all-to-all-start.1 = ((bf16[32,16,1024]{2,1,0:T(8,128)(2,1)}), bf16[32,16,1024]{2,1,0:T(8,128)(2,1)S(1)}, u32[]{:S(2)}, u32[]{:S(2)}) async-start(bf16[32,16,1024]{2,1,0:T(8,128)(2,1)} %get-tuple-element.91), calls=%async_computation.1 | async-start | bytes 2097152 | tf_op jit(solution)/shard_map/all_to_all | solution.py:591
  76.7 1.5 %restore.1 = (bf16[18,48,512]{2,1,0:T(8,128)(2,1)}, bf16[18,48,512]{2,1,0:T(8,128)(2,1)}) custom-call(bf16[18,48,512]{2,1,0:T(8,128)(2,1)S(1)} %get-tuple-element.92.mixed_c, bf16[18,48,512]{2,1,0:T(8,128)(2,1)S(1)} %get-tuple-element.93.tgrad_c, bf16[96,1024]{1,0:T(8,128)(2,1)S(1)} %collective-permute-done.7.h_lon, ...), custom_call_target="tpu_custom_call" | custom-call | flops 1000000 | bytes 8388608 | tf_op jit(solution)/shard_map/restore/pallas_call | solution.py:492
  78.2 12.3 %all-to-all-done.1 = bf16[32,16,1024]{2,1,0:T(8,128)(2,1)S(1)} async-done(((bf16[32,16,1024]{2,1,0:T(8,128)(2,1)}), bf16[32,16,1024]{2,1,0:T(8,128)(2,1)S(1)}, u32[]{:S(2)}, u32[]{:S(2)}) %all-to-all-start.1) | async-done | bytes 1048608 | tf_op jit(solution)/shard_map/all_to_all | solution.py:591
  90.6 4.1 %collective-permute-start.10 = (bf16[512,1024]{1,0:T(8,128)(2,1)S(1)}, bf16[512,1024]{1,0:T(8,128)(2,1)S(1)}, u32[]{:S(2)}, u32[]{:S(2)}) collective-permute-start(bf16[512,1024]{1,0:T(8,128)(2,1)S(1)} %bitcast.12), channel_id=1, source_target_pairs={{0,1},{1,0},{2,3},{3,2},{4,5},{5,4},{6,7},{7,6},{8,9},{9,8},{10,11... | collective-permute-start | bytes 3145736 | tf_op jit(solution)/shard_map/ppermute | solution.py:507
  95.3 1.4 %place.2 = (f32[512,1536]{1,0:T(8,128)}, f32[512,512]{1,0:T(8,128)}) custom-call(s32[1]{0:T(128)} %bitcast.half, bf16[512,1024]{1,0:T(8,128)(2,1)S(1)} %bitcast.13), custom_call_target="tpu_custom_call" | custom-call | flops 1000000 | bytes 3145728 | tf_op jit(solution)/shard_map/place/pallas_call | solution.py:416
  97.0 1.4 %place.3 = (f32[512,1536]{1,0:T(8,128)}, f32[512,512]{1,0:T(8,128)}) custom-call(s32[1]{0:T(128)S(6)} %sub.3.half, bf16[512,1024]{1,0:T(8,128)(2,1)S(1)} %collective-permute-done.10.grads, f32[512,1536]{1,0:T(8,128)} %get-tuple-element.102.refs_0_, f32[512,512]{1,0:T(8,128)} %get-tuple-element.103.refs_1_), custom_call_target="tpu_custom_call", output_to_operand_aliasing={{0}: (2, {}), {1}: (3, {})} | custom-call | flops 1000000 | bytes 3145728 | tf_op jit(solution)/shard_map/place/pallas_call | solution.py:416
  (16 shorter events, 2.1 us)
Async XLA Ops:
  0.7 16.2 %copy-start = (f32[512]{0:T(512)S(1)}, f32[512]{0:T(512)}, u32[]{:S(2)}) copy-start(f32[512]{0:T(512)} %param.14) | copy-start | bytes 6148
  3.9 19.4 %collective-permute-start.1 = (bf16[128,1024]{1,0:T(8,128)(2,1)S(1)}, bf16[128,1024]{1,0:T(8,128)(2,1)S(1)}, u32[]{:S(2)}, u32[]{:S(2)}) collective-permute-start(bf16[128,1024]{1,0:T(8,128)(2,1)S(1)} %get-tuple-element.57), channel_id=1, source_target_pairs={{1,0},{2,1},{3,2},{4,3},{5,4},{6,5},{7,6},{8,7},{9,8},{10,9},{11,1... | collective-permute-start | bytes 786440 | tf_op jit(solution)/shard_map/ppermute | solution.py:530
  7.3 16.1 %collective-permute-start = (bf16[96,1024]{1,0:T(8,128)(2,1)S(1)}, bf16[96,1024]{1,0:T(8,128)(2,1)S(1)}, u32[]{:S(2)}, u32[]{:S(2)}) collective-permute-start(bf16[96,1024]{1,0:T(8,128)(2,1)S(1)} %get-tuple-element.56), channel_id=1, source_target_pairs={{16,0},{32,16},{48,32},{64,48},{80,64},{96,80},{112,96},{128,112},... | collective-permute-start | bytes 589832 | tf_op jit(solution)/shard_map/ppermute | solution.py:529
  12.1 11.2 %collective-permute-start.2 = (bf16[32,1024]{1,0:T(8,128)(2,1)S(1)}, bf16[32,1024]{1,0:T(8,128)(2,1)S(1)}, u32[]{:S(2)}, u32[]{:S(2)}) collective-permute-start(bf16[32,1024]{1,0:T(8,128)(2,1)S(1)} %get-tuple-element.58), channel_id=1, source_target_pairs={{17,0},{18,1},{19,2},{20,3},{21,4},{22,5},{23,6},{24,7},{25,8},{26... | collective-permute-start | bytes 196616 | tf_op jit(solution)/shard_map/ppermute | solution.py:531
  30.6 3.2 %collective-permute-start.3 = (bf16[512,1152]{1,0:T(8,128)(2,1)S(1)}, bf16[512,1152]{1,0:T(8,128)(2,1)S(1)}, u32[]{:S(2)}, u32[]{:S(2)}) collective-permute-start(bf16[512,1152]{1,0:T(8,128)(2,1)S(1)} %get-tuple-element.73), channel_id=1, source_target_pairs={{0,1},{1,0},{2,3},{3,2},{4,5},{5,4},{6,7},{7,6},{8,9},{9,8},{10,11... | collective-permute-start | bytes 3538952 | tf_op jit(solution)/shard_map/ppermute | solution.py:507
  34.9 21.7 %all-to-all-start = ((bf16[32,16,1152]{2,1,0:T(8,128)(2,1)}), bf16[32,16,1152]{2,1,0:T(8,128)(2,1)S(1)}, u32[]{:S(2)}, u32[]{:S(2)}) async-start(bf16[32,16,1152]{2,1,0:T(8,128)(2,1)} %bitcast.17), calls=%async_computation | async-start | bytes 2359296 | tf_op jit(solution)/shard_map/all_to_all | solution.py:557
  45.9 17.8 %collective-permute-start.8 = (bf16[128,1024]{1,0:T(8,128)(2,1)}, bf16[128,1024]{1,0:T(8,128)(2,1)S(1)}, u32[]{:S(2)}, u32[]{:S(2)}) collective-permute-start(bf16[128,1024]{1,0:T(8,128)(2,1)} %get-tuple-element.86), channel_id=1, source_target_pairs={{0,1},{1,2},{2,3},{3,4},{4,5},{5,6},{6,7},{7,8},{8,9},{9,10},{10,1... | collective-permute-start | bytes 786440 | tf_op jit(solution)/shard_map/ppermute | solution.py:575
  47.5 16.1 %collective-permute-start.7 = (bf16[96,1024]{1,0:T(8,128)(2,1)}, bf16[96,1024]{1,0:T(8,128)(2,1)S(1)}, u32[]{:S(2)}, u32[]{:S(2)}) collective-permute-start(bf16[96,1024]{1,0:T(8,128)(2,1)} %get-tuple-element.85), channel_id=1, source_target_pairs={{0,16},{16,32},{32,48},{48,64},{64,80},{80,96},{96,112},{112,128},... | collective-permute-start | bytes 589832 | tf_op jit(solution)/shard_map/ppermute | solution.py:574
  48.7 14.9 %collective-permute-start.9 = (bf16[32,1024]{1,0:T(8,128)(2,1)S(1)}, bf16[32,1024]{1,0:T(8,128)(2,1)S(1)}, u32[]{:S(2)}, u32[]{:S(2)}) collective-permute-start(bf16[32,1024]{1,0:T(8,128)(2,1)S(1)} %get-tuple-element.87), channel_id=1, source_target_pairs={{0,17},{1,18},{2,19},{3,20},{4,21},{5,22},{6,23},{7,24},{8,25},{9,... | collective-permute-start | bytes 196616 | tf_op jit(solution)/shard_map/ppermute | solution.py:576
  56.8 6.9 %collective-permute-start.4 = (bf16[16,1152]{1,0:T(8,128)(2,1)S(1)}, bf16[16,1152]{1,0:T(8,128)(2,1)S(1)}, u32[]{:S(2)}, u32[]{:S(2)}) collective-permute-start(bf16[16,1152]{1,0:T(8,128)(2,1)S(1)} %sum.1.piece), channel_id=1, source_target_pairs={{0,64},{32,96},{64,0},{96,32},{1,65},{33,97},{65,1},{97,33},{2,66}... | collective-permute-start | bytes 110600 | tf_op jit(solution)/shard_map/ppermute | solution.py:507
  59.8 5.0 %collective-permute-start.5 = (bf16[16,1152]{1,0:T(8,128)(2,1)S(1)}, bf16[16,1152]{1,0:T(8,128)(2,1)S(1)}, u32[]{:S(2)}, u32[]{:S(2)}) collective-permute-start(bf16[16,1152]{1,0:T(8,128)(2,1)S(1)} %sum.1.piece), channel_id=1, source_target_pairs={{0,32},{32,0},{64,96},{96,64},{1,33},{33,1},{65,97},{97,65},{2,34}... | collective-permute-start | bytes 110600 | tf_op jit(solution)/shard_map/ppermute | solution.py:507
  63.6 5.5 %collective-permute-start.6 = (bf16[16,1152]{1,0:T(8,128)(2,1)S(1)}, bf16[16,1152]{1,0:T(8,128)(2,1)S(1)}, u32[]{:S(2)}, u32[]{:S(2)}) collective-permute-start(bf16[16,1152]{1,0:T(8,128)(2,1)S(1)} %sum.1.piece), channel_id=1, source_target_pairs={{0,96},{32,64},{64,32},{96,0},{1,97},{33,65},{65,33},{97,1},{2,98}... | collective-permute-start | bytes 110600 | tf_op jit(solution)/shard_map/ppermute | solution.py:507
  70.3 20.2 %all-to-all-start.1 = ((bf16[32,16,1024]{2,1,0:T(8,128)(2,1)}), bf16[32,16,1024]{2,1,0:T(8,128)(2,1)S(1)}, u32[]{:S(2)}, u32[]{:S(2)}) async-start(bf16[32,16,1024]{2,1,0:T(8,128)(2,1)} %get-tuple-element.91), calls=%async_computation.1 | async-start | bytes 2097152 | tf_op jit(solution)/shard_map/all_to_all | solution.py:591
  90.6 6.4 %collective-permute-start.10 = (bf16[512,1024]{1,0:T(8,128)(2,1)S(1)}, bf16[512,1024]{1,0:T(8,128)(2,1)S(1)}, u32[]{:S(2)}, u32[]{:S(2)}) collective-permute-start(bf16[512,1024]{1,0:T(8,128)(2,1)S(1)} %bitcast.12), channel_id=1, source_target_pairs={{0,1},{1,0},{2,3},{3,2},{4,5},{5,4},{6,7},{7,6},{8,9},{9,8},{10,11... | collective-permute-start | bytes 3145736 | tf_op jit(solution)/shard_map/ppermute | solution.py:507
